TPU v7x, 32 devices: a whole 2x2x4 slice. The times are simulated.
32 devices in a mesh: fsdp: 4 (over y, core), ctx: 8 (over z, x).
Axes of the slice: x: 2, y: 2, z: 4, core: 2. Of those that a mesh axis runs over, the one named last changes fastest.
Arguments:
- tokens: bfloat16 [4, 4096, 576], P('fsdp', 'ctx'), may hold values from -6 to 6
- segment_ids: int32 [4, 4096], P('fsdp'), may hold values from 0 to 20, as said below
- positions: int32 [4, 4096], P('fsdp'), may hold values from 0 to 1999, as said below
- cotangent: bfloat16 [4, 4096, 576], P('fsdp', 'ctx'), may hold values from -6 to 6
- norm_first: bfloat16 [576], P('fsdp'), may hold values from 0.099609375 to 1.8984375
- query_weight: bfloat16 [576, 576], P('fsdp'), may hold values from -0.25 to 0.25
- key_weight: bfloat16 [576, 192], P('fsdp'), may hold values from -0.25 to 0.25
- value_weight: bfloat16 [576, 192], P('fsdp'), may hold values from -0.25 to 0.25
- output_weight: bfloat16 [576, 576], P('fsdp'), may hold values from -1 to 1
- norm_second: bfloat16 [576], P('fsdp'), may hold values from 0.099609375 to 1.8984375
- gate_weight: bfloat16 [576, 1536], P('fsdp'), may hold values from -0.25 to 0.25
- up_weight: bfloat16 [576, 1536], P('fsdp'), may hold values from -0.25 to 0.25
- down_weight: bfloat16 [1536, 576], P('fsdp'), may hold values from -0.15625 to 0.15625
Outputs:
- result: bfloat16 [4, 4096, 576], P('fsdp', 'ctx')
- tokens_grad: bfloat16 [4, 4096, 576], P('fsdp', 'ctx')
- first_grad: float32 [576], P('fsdp')
- query_grad: float32 [576, 576], P('fsdp')
- key_grad: float32 [576, 192], P('fsdp')
- value_grad: float32 [576, 192], P('fsdp')
- output_grad: float32 [576, 576], P('fsdp')
- second_grad: float32 [576], P('fsdp')
- gate_grad: float32 [576, 1536], P('fsdp')
- up_grad: float32 [576, 1536], P('fsdp')
- down_grad: float32 [1536, 576], P('fsdp')
Inputs may be any that keep to these rules, and one draw needn't show every extreme that they name: `segment_ids`: within a sequence, listed in order of place, documents follow one another and each is 200 to 2000 tokens long (the last one may be cut by the sequence's end); ids count documents from 0 in order of place; in every draw some sequence holds only documents of 200 tokens. Row r of a sequence holds place b * 256 + r % 256 with c = r // 512 and b = c if r % (512) < 256, else 2 * 8 - 1 - c. `positions`: A token's position is its place minus the place where its document begins; some document in every draw has exactly 2000 tokens.
All inputs are finite; a program needn't handle non-finite values.
Results may differ from a plain program's by a relative error of at most 0.02.
Values may be sent and summed in bfloat16 or wider, within the bound.
No kernel may reach another device: no remote copies, remote signals or barrier semaphores. Data moves between devices by JAX's collectives and lax.ppermute only.
A program may use at most 192 MiB of HBM per device.

v0:
```python
import functools
import math

import jax
import jax.numpy as jnp
from jax import lax
from jax.experimental import pallas as pl
from jax.experimental.pallas import tpu as pltpu
from jax.sharding import Mesh
from jax.sharding import PartitionSpec as P

HEADS = 9
KV_HEADS = 3
GROUP = HEADS // KV_HEADS
HEAD_DIM = 64
EPSILON = 1e-05
MASKED = -1e30
DOC_MOST = 2000
AXES = ("y", "core", "h", "x")
CTX = ("h", "x")
F32 = jnp.float32
BF16 = jnp.bfloat16


def moves(fsdp, ctx, step):
    pairs = []
    for f in range(fsdp):
        for c in range(ctx):
            to = step(f // 2, f % 2, c // 2, c % 2)
            if to is not None:
                y, core, h, x = to
                pairs.append((f * ctx + c, (2 * y + core) * ctx + 2 * h + x))
    return pairs


def make_send(fsdp, ctx):
    ys, hs, blocks = fsdp // 2, ctx // 2, 2 * ctx

    def along(pairs):
        return lambda a: lax.ppermute(a, AXES, pairs)

    def by(step):
        return along(moves(fsdp, ctx, step))

    def home(slot):
        def step(y, core, h, x):
            low = 2 * h + x
            block = low if h % 2 == slot else blocks - 1 - low
            return (y, int(block % 4 in (1, 2)), block // 4, core)

        return moves(fsdp, ctx, step)

    def back(pairs):
        return along([(b, a) for a, b in pairs])

    return dict(
        home=[along(home(0)), along(home(1))],
        back=[back(home(0)), back(home(1))],
        core=by(lambda y, k, h, x: (y, 1 - k, h, x)),
        across=by(lambda y, k, h, x: (y, k, h, 1 - x)),
        up=by(lambda y, k, h, x: (y, k, h + 1, x) if h + 1 < hs else None),
        down=by(lambda y, k, h, x: (y, k, h - 1, x) if h > 0 else None),
        shift=[by(lambda y, k, h, x, s=s: ((y + s) % ys, k, h, x)) for s in range(ys)],
    )


def pick_home(a, h):
    r = a.shape[1] // 2
    low, high = a[:, :r], a[:, r:]
    even = lax.rem(h, 2) == 0
    return jnp.where(even, low, high), jnp.where(even, high, low)


def send_home(send, pair):
    return send["home"][0](pair[0]), send["home"][1](pair[1])


def send_back(send, a, b):
    return send["back"][0](a), send["back"][1](b)


def low_high(a, b, h):
    even = lax.rem(h, 2) == 0
    return jnp.concatenate([jnp.where(even, a, b), jnp.where(even, b, a)], axis=1)


def tie(*values):
    return lax.optimization_barrier(values)


def bias_of(begin, place, block_id, keys, rows):
    key_place = block_id * keys + lax.broadcasted_iota(jnp.int32, (keys, rows), 0)
    seen = (key_place >= begin) & (key_place <= place)
    return jnp.where(seen, 0.0, MASKED)


def dot(left, right, left_dim, right_dim):
    return lax.dot_general(
        left, right, (((left_dim,), (right_dim,)), ((), ())), preferred_element_type=F32
    )


def load_blocks(pieces, held):
    held[:2] = pieces[0][...]
    held[2:] = pieces[1][...]


def each_pair(sc, stage, work):
    base, core = sc[4] - 4 * stage, sc[5]

    def step(i, _):
        q = lax.div(i, 4)
        k = lax.rem(i, 4)
        within = jnp.where(k < 2, core, 1 - core)
        block_id = base + jnp.where(lax.rem(k, 2) == 0, within, 3 - within)

        @pl.when((block_id >= sc[2 + q]) & (block_id <= sc[q]))
        def _():
            work(q, k, block_id)

        return 0

    lax.fori_loop(0, 8, step, 0)


def forward_kernel(stage, last, *refs):
    first = stage == 0
    refs = list(refs)
    sc, pos, qz = refs[:3]
    kv = refs[3:5]
    refs = refs[5:]
    if not first:
        peak_in, total_in, mix_in = refs[:3]
        refs = refs[3:]
    if last:
        out, lse = refs[:2]
        held, bias, peak, total, mix = refs[2:]
    else:
        peak, total, mix = refs[:3]
        held, bias = refs[3:]
    rows = pos.shape[-1]
    if first:
        peak[...] = jnp.full(peak.shape, MASKED, F32)
        total[...] = jnp.zeros(total.shape, F32)
        mix[...] = jnp.zeros(mix.shape, F32)
    else:
        peak[...] = peak_in[...]
        total[...] = total_in[...]
        mix[...] = mix_in[...]
    load_blocks(kv, held)

    def work(q, k, block_id):
        place = sc[q] * rows + lax.broadcasted_iota(jnp.int32, (1, rows), 1)
        bias[...] = bias_of(place - pos[q], place, block_id, rows, rows)
        for c in range(KV_HEADS):
            seen = dot(held[k, c], qz[q, c], 1, 0) + jnp.concatenate([bias[...]] * GROUP, axis=1)
            old = peak[q, c]
            new = jnp.maximum(old, jnp.max(seen, axis=0, keepdims=True))
            expo = jnp.exp(seen - new)
            fade = jnp.exp(old - new)
            peak[q, c] = new
            total[q, c] = total[q, c] * fade + jnp.sum(expo, axis=0, keepdims=True)
            values = held[k, c].T[HEAD_DIM:]
            mix[q, c] = mix[q, c] * fade + dot(values, expo.astype(BF16), 1, 0)

    each_pair(sc, stage, work)
    if last:
        lse[...] = peak[...] + jnp.log(total[...])
        for q in range(2):
            for c in range(KV_HEADS):
                out[q, c] = (mix[q, c] / total[q, c]).astype(BF16)


def backward_kernel(stage, first, own_type, *refs):
    refs = list(refs)
    sc, pos, qz, gz, lse, delta = refs[:6]
    kv = refs[6:8]
    refs = refs[8:]
    if not first:
        dq_in = refs[0]
        refs = refs[1:]
    dq, own, other_a, other_b, held, bias, dkv = refs
    rows = pos.shape[-1]
    if first:
        dq[...] = jnp.zeros(dq.shape, F32)
    else:
        dq[...] = dq_in[...]
    load_blocks(kv, held)
    dkv[...] = jnp.zeros(dkv.shape, F32)

    def work(q, k, block_id):
        place = sc[q] * rows + lax.broadcasted_iota(jnp.int32, (1, rows), 1)
        bias[...] = bias_of(place - pos[q], place, block_id, rows, rows)
        scores = [dot(held[k, c], qz[q, c], 1, 0) for c in range(KV_HEADS)]
        for c in range(KV_HEADS):
            seen = scores[c] + jnp.concatenate([bias[...]] * GROUP, axis=1)
            probs = jnp.exp(seen - lse[q, c])
            d_scores = (probs * (dot(held[k, c], gz[q, c], 1, 0) - delta[q, c])).astype(BF16)
            dkv[k, c] += dot(d_scores, qz[q, c], 1, 1) + dot(probs.astype(BF16), gz[q, c], 1, 1)
            dq[q, c] += dot(held[k, c].T[:HEAD_DIM], d_scores, 1, 0)

    each_pair(sc, stage, work)
    own[...] = dkv[:2].astype(own_type)
    other_a[...] = dkv[2].astype(BF16)
    other_b[...] = dkv[3].astype(BF16)


SM = pl.BlockSpec(memory_space=pltpu.SMEM)
HB = pl.BlockSpec(memory_space=pl.ANY)


def whole(a):
    return pl.BlockSpec(
        a.shape, lambda i: (0,) * len(a.shape), pipeline_mode=pl.Buffered(buffer_count=1)
    )


def wholes(*arrays):
    return [whole(a) for a in arrays]


FREE = pl.CostEstimate(flops=0, bytes_accessed=0, transcendentals=0)
LIMIT = pltpu.CompilerParams(vmem_limit_bytes=60 << 20)


def attend_forward(stage, sc, pos, qz, pieces, carried, last):
    rows = pos.shape[-1]
    blocks = 4
    first = carried is None
    stat = jax.ShapeDtypeStruct((2, KV_HEADS, 1, GROUP * rows), F32)
    mix = jax.ShapeDtypeStruct((2, KV_HEADS, HEAD_DIM, GROUP * rows), F32)
    scratch = [
        pltpu.VMEM((blocks, KV_HEADS, rows, 2 * HEAD_DIM), BF16),
        pltpu.VMEM((rows, rows), F32),
    ]
    if last:
        out_shape = (jax.ShapeDtypeStruct(mix.shape, BF16), stat)
        scratch += [pltpu.VMEM(s.shape, F32) for s in (stat, stat, mix)]
        aliases = {}
    else:
        out_shape = (stat, stat, mix)
        aliases = {} if first else {3 + len(pieces) + i: i for i in range(3)}
    given = (sc, pos, qz, *pieces) + (() if first else tuple(carried))
    pairs = blocks * HEADS * rows * rows
    return pl.pallas_call(
        functools.partial(forward_kernel, stage, last),
        out_shape=out_shape,
        grid=(1,),
        in_specs=[SM] + wholes(*given[1:]),
        out_specs=wholes(*out_shape),
        scratch_shapes=scratch,
        input_output_aliases=aliases,
        compiler_params=LIMIT,
        cost_estimate=FREE,
    )(*given)


def attend_backward(stage, sc, pos, qz, gz, lse, delta, pieces, dq, own_type):
    rows = pos.shape[-1]
    blocks = 4
    first = dq is None
    wide = (KV_HEADS, rows, 2 * HEAD_DIM)
    given = (sc, pos, qz, gz, lse, delta, *pieces) + (() if first else (dq,))
    pairs = blocks * HEADS * rows * rows
    out_shape = (
        jax.ShapeDtypeStruct((2, KV_HEADS, HEAD_DIM, GROUP * rows), F32),
        jax.ShapeDtypeStruct((blocks // 2,) + wide, own_type),
        jax.ShapeDtypeStruct(wide, BF16),
        jax.ShapeDtypeStruct(wide, BF16),
    )
    return pl.pallas_call(
        functools.partial(backward_kernel, stage, first, own_type),
        out_shape=out_shape,
        grid=(1,),
        in_specs=[SM] + wholes(*given[1:]),
        out_specs=wholes(*out_shape),
        scratch_shapes=[
            pltpu.VMEM((blocks,) + wide, BF16),
            pltpu.VMEM((rows, rows), F32),
            pltpu.VMEM((blocks,) + wide, F32),
        ],
        input_output_aliases={} if first else {len(given) - 1: 0},
        compiler_params=LIMIT,
        cost_estimate=FREE,
    )(*given)


def load_parts(sc, at, pieces, full, sems, dim):
    size = pieces[0].shape[dim]
    copies = []
    for i, piece in enumerate(pieces):
        if len(pieces) == 1:
            to = full
        elif dim == 0:
            to = full.at[pl.ds(pl.multiple_of(sc[at + i] * size, 16), size)]
        else:
            to = full.at[:, pl.ds(pl.multiple_of(sc[at + i] * size, 128), size)]
        copies.append(pltpu.make_async_copy(piece, to, sems.at[i]))
    for copy in copies:
        copy.start()
    return copies


def norm_scale(v):
    return lax.rsqrt(jnp.mean(v * v, axis=0, keepdims=True) + EPSILON)


def project_kernel(pieces, *refs):
    sc, xa, xb, cos, sin = refs[:5]
    parts = refs[5 : 5 + pieces]
    qz, kv, normed_t, gains, pos, ids, full, sems = refs[5 + pieces :]
    copies = load_parts(sc, 3, parts, full, sems, 0)
    rows = xa.shape[-1]
    width = full.shape[0]
    for q, x in enumerate((xa, xb)):
        p = x[width : width + 16].astype(F32)
        p = p[0:1] * 64.0 + p[1:2]
        pos[q] = p.astype(jnp.int32)
        block = sc[2] + (sc[0] if q == 0 else 3 - sc[0])
        lane = lax.broadcasted_iota(jnp.int32, (1, rows), 1).astype(F32)
        begin = block * rows + jnp.min(lane - p).astype(jnp.int32)
        ids[q] = block
        ids[2 + q] = lax.div(begin, rows)
    ids[4] = sc[2]
    ids[5] = sc[0]
    flat = [x[:width].astype(F32) for x in (xa, xb)]
    scaled = [v * norm_scale(v) for v in flat]
    for copy in copies:
        copy.wait()
    gains[...] = full[:, width + 320 : width + 448]
    gain = full[:, width + 384 : width + 385].astype(F32)
    half = HEAD_DIM // 2
    for q in range(2):
        normed = (scaled[q] * gain).astype(BF16)
        at = slice(q * rows, (q + 1) * rows)
        normed_t[:, at] = normed
        made = jnp.dot(normed.T, full[:, : width + 384], preferred_element_type=F32).T
        c, s = cos[:, at], sin[:, at]
        for h in range(HEADS):
            a = made[64 * h : 64 * h + half]
            b = made[64 * h + half : 64 * h + 64]
            ra = (a * c - b * s).astype(BF16) * jnp.asarray(HEAD_DIM**-0.5, BF16)
            rb = (b * c + a * s).astype(BF16) * jnp.asarray(HEAD_DIM**-0.5, BF16)
            group, lanes = h // GROUP, slice(h % GROUP * rows, (h % GROUP + 1) * rows)
            qz[q, group, :half, lanes] = ra
            qz[q, group, half : 2 * half, lanes] = rb
            qz[q, group, 2 * half :, lanes] = jnp.zeros((2 * half, rows), BF16)
        for k in range(KV_HEADS):
            row = width + 64 * k
            a = made[row : row + half]
            b = made[row + half : row + 64]
            ra = (a * c - b * s).astype(BF16)
            rb = (b * c + a * s).astype(BF16)
            v = made[row + 192 : row + 256].astype(BF16)
            kv[q, k] = jnp.concatenate([ra, rb, v], axis=0).T


def project(sc, xs, cos, sin, parts):
    rows = xs[0].shape[1]
    count = 2 * rows
    width = HEADS * HEAD_DIM
    out_shape = (
        jax.ShapeDtypeStruct((2, KV_HEADS, 2 * HEAD_DIM, GROUP * rows), BF16),
        jax.ShapeDtypeStruct((2, KV_HEADS, rows, 2 * HEAD_DIM), BF16),
        jax.ShapeDtypeStruct((width, count), BF16),
        jax.ShapeDtypeStruct((width, 128), BF16),
        jax.ShapeDtypeStruct((2, 1, rows), jnp.int32),
        jax.ShapeDtypeStruct((8,), jnp.int32),
    )
    return pl.pallas_call(
        functools.partial(project_kernel, len(parts)),
        out_shape=out_shape,
        grid=(1,),
        in_specs=[SM] + wholes(*xs, cos, sin) + [HB] * len(parts),
        out_specs=wholes(*out_shape[:-1]) + [SM],
        scratch_shapes=[
            pltpu.VMEM((width, parts[0].shape[1]), BF16),
            pltpu.SemaphoreType.DMA((len(parts),)),
        ],
        compiler_params=LIMIT,
        cost_estimate=FREE,
    )(sc, *xs, cos, sin, *parts)


def wide(value):
    over = -value.shape[1] % 128
    if not over:
        return value
    return jnp.concatenate([value, jnp.zeros((value.shape[0], over), value.dtype)], axis=1)


def slot_of(sc, fsdp, f):
    ys = fsdp // 2
    return lax.rem(f + sc[0], 2), lax.rem(lax.div(f, 2) - sc[1] + ys, ys)


def put_slabs(packed, sc, fsdp, at, value):
    value = wide(value).astype(BF16)
    r = value.shape[0] // fsdp
    for f in range(fsdp):
        k, y = slot_of(sc, fsdp, f)
        for s in range(value.shape[1] // 128):
            packed[k, y, pl.ds(at + s * r, r)] = value[
                f * r : (f + 1) * r, s * 128 : (s + 1) * 128
            ]


def norm_back(v, gain, grad):
    r = norm_scale(v)
    scaled = grad * gain
    d_v = r * scaled - v * (r * r * r * jnp.mean(scaled * v, axis=0, keepdims=True))
    return d_v, jnp.sum(grad * (v * r), axis=1, keepdims=True)


def feed_kernel(fsdp, pieces, chunk, *refs):
    sc, xa, xb, ca, cb, mix, gains = refs[:7]
    parts = refs[7 : 7 + pieces]
    downs = refs[7 + pieces : 7 + 2 * pieces]
    refs = refs[7 + 2 * pieces :]
    res_a, res_b, d_middle, gz, delta, mine, give, second = refs[:8]
    full, out_w, down, packed, att_t, mid, n2, n2_t, res, d_second, cot_t, cot = refs[8:20]
    sems, out_sems, down_sems, grad_sems = refs[20:]
    ff = down.shape[1]
    out_copies = load_parts(sc, 3, [p.at[:, 2 * ff :] for p in parts], out_w, out_sems, 0)
    copies = load_parts(sc, 3, [p.at[:, : 2 * ff] for p in parts], full, sems, 0)
    down_copies = load_parts(sc, 3, downs, down, down_sems, 1)
    rows = xa.shape[-1]
    width, ff = down.shape
    shard = width // fsdp
    down_shard = ff // fsdp
    for q, c in enumerate((ca, cb)):
        cot_t[:, q * rows : (q + 1) * rows] = c[...]
        for h in range(HEADS):
            att_t[64 * h : 64 * h + 64, q * rows : (q + 1) * rows] = mix[
                q, h // GROUP, :, h % GROUP * rows : (h % GROUP + 1) * rows
            ]
    cot[...] = cot_t[...].T
    gain = gains[:, 65:66].astype(F32)
    for copy in out_copies:
        copy.wait()
    branch_t = jnp.dot(out_w[...].T, att_t[...], preferred_element_type=F32)
    for q, x in enumerate((xa, xb)):
        at = slice(q * rows, (q + 1) * rows)
        mid[:, at] = x[:width].astype(F32) + branch_t[:, at]
    n2_t[...] = (mid[...] * norm_scale(mid[...]) * gain).astype(BF16)
    n2[...] = n2_t[...].T
    res[...] = mid[...]
    d_second[...] = jnp.zeros(d_second.shape, F32)
    for copy in copies + down_copies:
        copy.wait()
    up_at = ff // 128 * shard
    out_at = 2 * up_at
    down_at = out_at + -(-width // 128) * shard
    used = down_at + -(-down_shard // 128) * width
    rows_all = packed.shape[2]
    if rows_all > used:
        packed[:, :, used:] = jnp.zeros((2, fsdp // 2, rows_all - used, 128), BF16)

    def step(j, _):
        cols = pl.ds(pl.multiple_of(j * chunk, 128), chunk)
        up_cols = pl.ds(pl.multiple_of(ff + j * chunk, 128), chunk)
        gate_w, up_w, down_w = full[:, cols], full[:, up_cols], down[:, cols]
        gate = jnp.dot(n2[...], gate_w, preferred_element_type=F32)
        up = jnp.dot(n2[...], up_w, preferred_element_type=F32)
        sig = 1.0 / (1.0 + jnp.exp(-gate))
        silu = gate * sig
        hidden = (silu * up).astype(BF16)
        res[...] += dot(down_w, hidden, 1, 1)
        d_hidden = jnp.dot(cot[...], down_w, preferred_element_type=F32)
        d_gate = (d_hidden * up * (sig * (1.0 + gate * (1.0 - sig)))).astype(BF16)
        d_up = (d_hidden * silu).astype(BF16)
        d_second[...] += dot(gate_w, d_gate, 1, 1) + dot(up_w, d_up, 1, 1)
        slab = pl.multiple_of(j * (chunk // 128) * shard, 8)
        put_slabs(packed, sc, fsdp, slab, jnp.dot(n2_t[...], d_gate, preferred_element_type=F32))
        put_slabs(
            packed, sc, fsdp, up_at + slab, jnp.dot(n2_t[...], d_up, preferred_element_type=F32)
        )
        down_g = jnp.dot(cot_t[...], hidden, preferred_element_type=F32).astype(BF16)
        if down_shard % 128:
            for n in range(chunk // down_shard):
                slot_k, slot_y = slot_of(sc, fsdp, j * (chunk // down_shard) + n)
                part = wide(down_g[:, n * down_shard : (n + 1) * down_shard])
                for s in range(part.shape[1] // 128):
                    packed[slot_k, slot_y, down_at + s * width : down_at + (s + 1) * width] = part[
                        :, s * 128 : (s + 1) * 128
                    ]
        else:
            for n in range(chunk // 128):
                slab = j * (chunk // 128) + n
                slot_k, slot_y = slot_of(sc, fsdp, lax.div(slab, down_shard // 128))
                at = pl.multiple_of(down_at + lax.rem(slab, down_shard // 128) * width, 16)
                packed[slot_k, slot_y, pl.ds(at, width)] = down_g[:, n * 128 : (n + 1) * 128]
        return 0

    lax.fori_loop(0, ff // chunk, step, 0)
    spans = [(0, out_at), (down_at, rows_all - down_at), (out_at, down_at - out_at)]
    sends = [
        [
            pltpu.make_async_copy(
                packed.at[k, :, pl.ds(at, n)], to.at[:, pl.ds(at, n)], grad_sems.at[k, i]
            )
            for k, to in enumerate((mine, give))
        ]
        for i, (at, n) in enumerate(spans)
    ]
    for copy in sends[0] + sends[1]:
        copy.start()
    res_a[...] = res[:, :rows].astype(BF16)
    res_b[...] = res[:, rows:].astype(BF16)
    d_v, gain_grad = norm_back(mid[...], gain, d_second[...])
    second[...] = jnp.broadcast_to(gain_grad, second.shape)
    d_mid = cot_t[...].astype(F32) + d_v
    d_middle[...] = d_mid
    branch = d_mid.astype(BF16)
    put_slabs(packed, sc, fsdp, out_at, dot(att_t[...], branch, 1, 1))
    for copy in sends[2]:
        copy.start()
    d_mix = jnp.dot(out_w[...], branch, preferred_element_type=F32).astype(BF16)
    for q in range(2):
        for h in range(HEADS):
            at = slice(q * rows, (q + 1) * rows)
            part = d_mix[64 * h : 64 * h + 64, at]
            group, lanes = h // GROUP, slice(h % GROUP * rows, (h % GROUP + 1) * rows)
            gz[q, group, :64, lanes] = jnp.zeros((64, rows), BF16)
            gz[q, group, 64:, lanes] = part
            delta[q, group, :, lanes] = jnp.sum(
                part.astype(F32) * att_t[64 * h : 64 * h + 64, at].astype(F32),
                axis=0,
                keepdims=True,
            )
    for copy in sends[0] + sends[1] + sends[2]:
        copy.wait()


def feed_rows(fsdp, ctx, width, ff):
    used = (2 * (ff // 128) + -(-width // 128)) * (width // fsdp) + -(-(ff // fsdp) // 128) * width
    return -(-used // (16 * ctx)) * 16 * ctx


def feed(fsdp, ctx, sc, xs, cots, mix, gains, parts, downs):
    rows = cots[0].shape[1]
    width = cots[0].shape[0]
    count = 2 * rows
    ff = downs[0].shape[1] * len(downs)
    packed = (fsdp // 2, feed_rows(fsdp, ctx, width, ff), 128)
    out_shape = (
        jax.ShapeDtypeStruct((width, rows), BF16),
        jax.ShapeDtypeStruct((width, rows), BF16),
        jax.ShapeDtypeStruct((width, count), F32),
        jax.ShapeDtypeStruct((2, KV_HEADS, 2 * HEAD_DIM, GROUP * rows), BF16),
        jax.ShapeDtypeStruct((2, KV_HEADS, 1, GROUP * rows), F32),
        jax.ShapeDtypeStruct(packed, BF16),
        jax.ShapeDtypeStruct(packed, BF16),
        jax.ShapeDtypeStruct((width, 128), F32),
    )
    return pl.pallas_call(
        functools.partial(feed_kernel, fsdp, len(parts), ff // 4 if ff // fsdp % 128 else ff // 3),
        out_shape=out_shape,
        grid=(1,),
        in_specs=[SM] + wholes(*xs, *cots, mix, gains) + [HB] * (2 * len(parts)),
        out_specs=wholes(*out_shape[:5]) + [HB, HB] + wholes(out_shape[7]),
        scratch_shapes=[
            pltpu.VMEM((width, 2 * ff), BF16),
            pltpu.VMEM((width, width), BF16),
            pltpu.VMEM((width, ff), BF16),
            pltpu.VMEM((2,) + packed, BF16),
            pltpu.VMEM((width, count), BF16),
            pltpu.VMEM((width, count), F32),
            pltpu.VMEM((count, width), BF16),
            pltpu.VMEM((width, count), BF16),
            pltpu.VMEM((width, count), F32),
            pltpu.VMEM((width, count), F32),
            pltpu.VMEM((width, count), BF16),
            pltpu.VMEM((count, width), BF16),
            pltpu.SemaphoreType.DMA((len(parts),)),
            pltpu.SemaphoreType.DMA((len(parts),)),
            pltpu.SemaphoreType.DMA((len(parts),)),
            pltpu.SemaphoreType.DMA((2, 3)),
        ],
        compiler_params=LIMIT,
        cost_estimate=FREE,
    )(sc, *xs, *cots, mix, gains, *parts, *downs)


def last_kernel(fsdp, pieces, chain, *refs):
    sc, xa, xb, cos, sin, normed_t, gains, second, d_middle, dq, own, *twin = refs[:13]
    refs = refs[13:]
    if chain:
        came = refs[0]
        refs = refs[1:]
    parts = refs[:pieces]
    grad_a, grad_b, mine, give, full, packed, made, sems = refs[pieces:]
    copies = load_parts(sc, 3, parts, full, sems, 0)
    rows = xa.shape[-1]
    width = full.shape[0]
    half = HEAD_DIM // 2
    for q in range(2):
        at = slice(q * rows, (q + 1) * rows)
        c, s = cos[:, at], sin[:, at]
        for h in range(HEADS):
            group, lanes = h // GROUP, slice(h % GROUP * rows, (h % GROUP + 1) * rows)
            a = dq[q, group, :half, lanes] * HEAD_DIM**-0.5
            b = dq[q, group, half:, lanes] * HEAD_DIM**-0.5
            made[64 * h : 64 * h + half, at] = (a * c + b * s).astype(BF16)
            made[64 * h + half : 64 * h + 64, at] = (b * c - a * s).astype(BF16)
        for k in range(KV_HEADS):
            both = own[q, k] + twin[q][k].astype(F32)
            if chain:
                both = both + came[q, k].astype(F32)
            both = both.T
            a, b = both[:half], both[half : 2 * half]
            row = width + 64 * k
            made[row : row + half, at] = (a * c + b * s).astype(BF16)
            made[row + half : row + 64, at] = (b * c - a * s).astype(BF16)
            made[row + 192 : row + 256, at] = both[2 * half :].astype(BF16)
    for copy in copies:
        copy.wait()
    gain = gains[:, 64:65].astype(F32)
    d_first = jnp.dot(full[:, : width + 384], made[...], preferred_element_type=F32)
    v = jnp.concatenate([xa[:width], xb[:width]], axis=1).astype(F32)
    d_v, first = norm_back(v, gain, d_first)
    d_x = (d_middle[...] + d_v).astype(BF16)
    grad_a[...] = d_x[:, :rows]
    grad_b[...] = d_x[:, rows:]
    front = dot(normed_t[...], made[...], 1, 1)
    lane = lax.broadcasted_iota(jnp.int32, (width, 64), 1)
    ends = jnp.where(lane == 0, first, second[:, :64])
    put_slabs(packed, sc, fsdp, 0, jnp.concatenate([front, ends], axis=1))
    used = (width + 448) // 128 * (width // fsdp)
    total = packed.shape[2]
    if total > used:
        packed[:, :, used:] = jnp.zeros((2, fsdp // 2, total - used, 128), BF16)
    mine[...] = packed[0]
    give[...] = packed[1]


def last(fsdp, ctx, sc, xs, cos, sin, normed_t, gains, second, d_middle, dq, dkv, parts):
    width, count = normed_t.shape
    rows = count // 2
    used = (width + 448) // 128 * (width // fsdp)
    packed = (fsdp // 2, -(-used // (16 * ctx)) * 16 * ctx, 128)
    given = (*xs, cos, sin, normed_t, gains, second, d_middle, dq, *dkv)
    out_shape = (
        jax.ShapeDtypeStruct((width, rows), BF16),
        jax.ShapeDtypeStruct((width, rows), BF16),
        jax.ShapeDtypeStruct(packed, BF16),
        jax.ShapeDtypeStruct(packed, BF16),
    )
    return pl.pallas_call(
        functools.partial(last_kernel, fsdp, len(parts), len(dkv) == 4),
        out_shape=out_shape,
        grid=(1,),
        in_specs=[SM] + wholes(*given) + [HB] * len(parts),
        out_specs=wholes(*out_shape),
        scratch_shapes=[
            pltpu.VMEM((width, parts[0].shape[1]), BF16),
            pltpu.VMEM((2,) + packed, BF16),
            pltpu.VMEM((width + 384, count), BF16),
            pltpu.SemaphoreType.DMA((len(parts),)),
        ],
        compiler_params=LIMIT,
        cost_estimate=FREE,
    )(sc, *given, *parts)


def unpack_kernel(places, flat, *outs):
    for out, (at, rows, skip) in zip(outs, places, strict=True):
        columns = out.shape[1]
        done = 0
        while done < columns:
            slab, lane = divmod(skip + done, 128)
            n = min(128 - lane, columns - done)
            out[:, done : done + n] = flat[
                at + slab * rows : at + (slab + 1) * rows, lane : lane + n
            ].astype(F32)
            done += n


def join_unpack_kernel(places, sc, near, far, *refs):
    *outs, flat = refs
    part = near.shape[0] // 2
    for half in range(2):
        for x in range(2):
            piece = near if x == 0 else far
            at = pl.multiple_of(part * (2 * half + lax.rem(sc[0] + x, 2)), 16)
            flat[pl.ds(at, part)] = piece[half * part : (half + 1) * part]
    unpack_kernel(places, flat, *outs)


def unpack(flat, places):
    out_shape = tuple(jax.ShapeDtypeStruct((p[1], p[3]), F32) for p in places)
    return pl.pallas_call(
        functools.partial(unpack_kernel, [p[:3] for p in places]),
        out_shape=out_shape,
        grid=(1,),
        in_specs=wholes(flat),
        out_specs=wholes(*out_shape),
        compiler_params=LIMIT,
        cost_estimate=FREE,
    )(flat)


def join_unpack(x, near, far, places):
    out_shape = tuple(jax.ShapeDtypeStruct((p[1], p[3]), F32) for p in places)
    return pl.pallas_call(
        functools.partial(join_unpack_kernel, [p[:3] for p in places]),
        out_shape=out_shape,
        grid=(1,),
        in_specs=[SM] + wholes(near, far),
        out_specs=wholes(*out_shape),
        scratch_shapes=[pltpu.VMEM((2 * near.shape[0], 128), BF16)],
        compiler_params=LIMIT,
        cost_estimate=FREE,
    )(x, near, far)


def chip_sum(mine, got, i):
    return mine[i].astype(F32) + got[i].astype(F32)


def sum_y(mine, got, send):
    total = chip_sum(mine, got, 0)
    for s in range(1, mine.shape[0]):
        total = total + send["shift"][s](chip_sum(mine, got, s).astype(BF16)).astype(F32)
    return total.astype(BF16)


def spread_kernel(got, out):
    total = got[0].astype(F32)
    for i in range(1, got.shape[0]):
        total = total + got[i].astype(F32)
    total = total.astype(BF16)
    for i in range(got.shape[0]):
        out[i] = total


def simple_call(kernel, out_shape, *given):
    return pl.pallas_call(
        kernel,
        out_shape=out_shape,
        grid=(1,),
        in_specs=wholes(*given),
        out_specs=whole(out_shape),
        compiler_params=LIMIT,
        cost_estimate=FREE,
    )(*given)


def sum_over(total, axes, size):
    parts = total.reshape(size, total.shape[0] // size, 128)
    got = lax.all_to_all(parts, axes, 0, 0, tiled=True)
    spread = simple_call(spread_kernel, jax.ShapeDtypeStruct(got.shape, BF16), got)
    return lax.all_to_all(spread, axes, 0, 0, tiled=True).reshape(-1, 128)


def came_kernel(own, twin_a, twin_b, *refs):
    *came, out = refs
    for i, twin in enumerate((twin_a, twin_b)):
        total = own[i].astype(F32) + twin[...].astype(F32)
        for c in came:
            total = total + c[i].astype(F32)
        out[i] = total.astype(BF16)


def halves_kernel(one, one_came, two, two_came, out):
    n = one.shape[0]
    out[:n] = (one[...].astype(F32) + one_came[...].astype(F32)).astype(BF16)
    out[n:] = (two[...].astype(F32) + two_came[...].astype(F32)).astype(BF16)


def first_kernel(x, mine, got, to_y, to_x):
    i = pl.program_id(0)
    total = (mine[...].astype(F32) + got[...].astype(F32)).astype(BF16)

    @pl.when(i < 2)
    def _():
        to_y[...] = total

    @pl.when(i >= 2)
    def _():
        to_x[...] = total


def first_sums(x, mine, got):
    n = mine.shape[1] // 4
    block = (1, n, 128)

    def at(i, x):
        return jnp.where(i == 2, 0, 1), jnp.where(i < 2, i, 3 - x[0]), 0

    shapes = (jax.ShapeDtypeStruct((2, n, 128), BF16),) * 2
    return pl.pallas_call(
        first_kernel,
        out_shape=shapes,
        grid_spec=pltpu.PrefetchScalarGridSpec(
            num_scalar_prefetch=1,
            grid=(4,),
            in_specs=[pl.BlockSpec(block, at)] * 2,
            out_specs=[
                pl.BlockSpec(block, lambda i, x: (jnp.minimum(i, 1), 0, 0)),
                pl.BlockSpec(block, lambda i, x: (jnp.maximum(i - 2, 0), 0, 0)),
            ],
        ),
        compiler_params=LIMIT,
        cost_estimate=FREE,
    )(x, mine, got)


def second_kernel(x, mine, got, came_y, came_x, *outs):
    i = pl.program_id(0)
    total = mine[...].astype(F32) + got[...].astype(F32)
    came = jnp.where(i < 2, came_y[...].astype(F32), came_x[...].astype(F32))
    total = (total + came).astype(BF16)[0]
    for n, out in enumerate(outs):

        @pl.when(i == n)
        def _(out=out):
            out[...] = total


def second_sums(x, mine, got, came_y, came_x):
    n = mine.shape[1] // 4
    block = (1, n, 128)

    def own(i, x):
        return (i == 2) * 1, jnp.where(i == 0, 1 - x[0], jnp.where(i == 1, x[0], 2 + x[0])), 0

    def from_y(i, x):
        return jnp.where(i == 0, 1 - x[0], x[0]), 0, 0

    def from_x(i, x):
        return jnp.where(i == 3, 0, 1), 0, 0

    return pl.pallas_call(
        second_kernel,
        out_shape=(jax.ShapeDtypeStruct((n, 128), BF16),) * 4,
        grid_spec=pltpu.PrefetchScalarGridSpec(
            num_scalar_prefetch=1,
            grid=(4,),
            in_specs=[
                pl.BlockSpec(block, own),
                pl.BlockSpec(block, own),
                pl.BlockSpec(block, from_y),
                pl.BlockSpec(block, from_x),
            ],
            out_specs=[pl.BlockSpec((n, 128), lambda i, x: (0, 0))] * 4,
        ),
        compiler_params=LIMIT,
        cost_estimate=FREE,
    )(x, mine, got, came_y, came_x)


def gather_y(own, send, fsdp):
    return [own] + [send["shift"][s](own) for s in range(1, fsdp // 2)]


def gather_pieces(got, send, fsdp, core, y, join, dim):
    pieces = got + [send["core"](g) for g in got]
    own = got[0]
    if not join:
        return pieces
    buffer = jnp.zeros((fsdp,) + own.shape, own.dtype)
    for piece, f in zip(pieces, piece_order(fsdp, core, y), strict=True):
        buffer = lax.dynamic_update_index_in_dim(buffer, piece, f, 0)
    if dim:
        buffer = buffer.swapaxes(0, 1)
        return [buffer.reshape(own.shape[0], fsdp * own.shape[1])]
    return [buffer.reshape(fsdp * own.shape[0], own.shape[1])]


def piece_order(fsdp, core, y):
    ys = fsdp // 2
    source = [lax.rem(y - s + ys, ys) * 2 for s in range(ys)]
    return [f + core for f in source] + [f + 1 - core for f in source]


def body(
    fsdp,
    ctx,
    tokens,
    segment_ids,
    positions,
    cotangent,
    norm_first,
    query_weight,
    key_weight,
    value_weight,
    output_weight,
    norm_second,
    gate_weight,
    up_weight,
    down_weight,
):
    send = make_send(fsdp, ctx)
    ys, hs = fsdp // 2, ctx // 2
    _, count, width = tokens.shape
    rows = count // 2
    kv_width = KV_HEADS * HEAD_DIM
    y, core = lax.axis_index("y"), lax.axis_index("core")
    h, x = lax.axis_index("h"), lax.axis_index("x")
    ci = 2 * h + x
    reach = min(hs - 1, -(-(-(-(DOC_MOST - 1) // rows)) // 4))
    order = jnp.stack([core, y, 4 * h] + piece_order(fsdp, core, y)).astype(jnp.int32)
    shard = gate_weight.shape[0]
    join = shard % 16 != 0
    own_pos = lax.dynamic_slice_in_dim(positions, ci * count, count, 1)
    pos_rows = jnp.concatenate(
        [lax.div(own_pos, 64), lax.rem(own_pos, 64), jnp.zeros((14, count), jnp.int32)], axis=0
    )
    carried = jnp.concatenate([tokens.reshape(count, width).T, pos_rows.astype(BF16)], axis=0)
    *pair, query_weight = tie(*pick_home(carried, h), query_weight)
    xs = send_home(send, pair)
    packed = jnp.concatenate(
        [
            query_weight,
            key_weight,
            value_weight,
            norm_first[:, None],
            norm_second[:, None],
            jnp.zeros((shard, 62), BF16),
        ],
        axis=1,
    )
    first_parts = gather_y(packed, send, fsdp)
    first_parts = gather_pieces(first_parts, send, fsdp, core, y, join, 0)
    pos_f = jnp.concatenate([a[width : width + 2] for a in xs], axis=1).astype(F32)
    pos_f = pos_f[0:1] * 64.0 + pos_f[1:2]
    frequency = jnp.exp(
        jnp.arange(HEAD_DIM // 2, dtype=F32) * (-math.log(10000.0) * 2.0 / HEAD_DIM)
    )
    angle = frequency[:, None] * pos_f
    cos, sin = jnp.cos(angle), jnp.sin(angle)
    qz, kv, normed_t, gains, pos, ids = project(order, xs, cos, sin, first_parts)

    feed_own = jnp.concatenate([gate_weight, up_weight, output_weight], axis=1)
    feed_own, down_own, _ = tie(feed_own, down_weight.T, first_parts[-1])
    feed_got = gather_y(feed_own, send, fsdp)
    down_got = gather_y(down_own, send, fsdp)
    cot_t, _ = tie(cotangent.reshape(count, width).T, kv)
    stages = []
    carried = None
    for s in range(reach + 1):
        stages.append((kv, send["core"](kv)))
        if s < reach:
            kv = send["up"](kv)
        carried = attend_forward(s, ids, pos, qz, stages[s], carried, s == reach)
        if s < reach:
            kv, *carried = tie(kv, *carried)
    mixed, lse = carried
    cots = send_home(send, pick_home(cot_t, h))
    feed_parts = gather_pieces(feed_got, send, fsdp, core, y, join, 0)
    down_parts = gather_pieces(down_got, send, fsdp, core, y, join, 1)
    res_a, res_b, d_middle, gz, delta, mine, give, second = feed(
        fsdp, ctx, order, xs, cots, mixed, gains, feed_parts, down_parts
    )

    got = send["core"](give)
    crossed = ys == 2
    x_ref = x.astype(jnp.int32).reshape(1)
    if crossed:
        first_y, first_x = first_sums(x_ref, mine, got)
    dq = None
    came = None
    for s in range(reach, -1, -1):
        sc = ids
        if s == reach - 1 and crossed:
            sc, first_y, first_x = tie(sc, first_y, first_x)
            came_y, came_x = send["shift"][1](first_y), send["across"](first_x)
        if s == 0 and crossed:
            give_one, keep_one, give_two, keep_two = second_sums(x_ref, mine, got, came_y, came_x)
            sc, give_one, give_two = tie(sc, give_one, give_two)
            came_one, came_two = send["across"](give_one), send["shift"][1](give_two)
        if came is not None:
            sc, came = tie(sc, came)
            came = send["down"](came)
        dq, own, *other = attend_backward(
            s, sc, pos, qz, gz, lse, delta, stages[s], dq, F32 if s == 0 else BF16
        )
        twin = tuple(send["core"](o) for o in other)
        if s > 0:
            if s < reach:
                *twin, came, dq = tie(*twin, came, dq)
            given = (own, *twin) if came is None else (own, *twin, came)
            came = simple_call(came_kernel, jax.ShapeDtypeStruct(own.shape, BF16), *given)
    dkv = (own, *twin) if came is None else (own, *twin, came)
    result = send_back(send, res_a, res_b)
    if crossed:
        *result, came_one, came_two, dq = tie(*result, came_one, came_two, dq)
    else:
        *result, dq = tie(*result, dq)
    tok_a, tok_b, mine_front, give_front = last(
        fsdp, ctx, order, xs, cos, sin, normed_t, gains, second, d_middle, dq, dkv, first_parts
    )
    got_front = send["core"](give_front)
    front = sum_y(mine_front, got_front, send)
    if crossed:
        late = simple_call(
            halves_kernel,
            jax.ShapeDtypeStruct((mine.shape[1] // 2, 128), BF16),
            keep_one,
            came_one,
            keep_two,
            came_two,
        )
        late = sum_over(late, ("h",), hs)
        late_far = send["across"](late)
    else:
        late = sum_over(sum_y(mine, got, send), CTX, ctx)
    front = sum_over(front, CTX, ctx)
    tokens_grad = send_back(send, tok_a, tok_b)

    ff = gate_weight.shape[1]
    down_shard = down_weight.shape[0]
    gate_rows, out_rows = ff // 128 * shard, -(-width // 128) * shard
    places = [
        (0, shard, 0, ff),
        (gate_rows, shard, 0, ff),
        (2 * gate_rows, shard, 0, width),
        (2 * gate_rows + out_rows, width, 0, down_shard),
    ]
    if crossed:
        late_grads = join_unpack(x_ref, late, late_far, places)
    else:
        late_grads = unpack(late, places)
    gate_grad, up_grad, output_grad, down_grad = late_grads
    query_grad, key_grad, value_grad, ends = unpack(
        front,
        [
            (0, shard, 0, width),
            (0, shard, width, kv_width),
            (0, shard, width + kv_width, kv_width),
            (0, shard, width + 2 * kv_width, 64),
        ],
    )
    return (
        low_high(*result, h).T[None],
        low_high(*tokens_grad, h).T[None],
        ends[:, 0],
        query_grad,
        key_grad,
        value_grad,
        output_grad,
        ends[:, 1],
        gate_grad,
        up_grad,
        down_grad.T,
    )


def solution(mesh):
    fsdp, ctx = mesh.shape["fsdp"], mesh.shape["ctx"]
    places = Mesh(mesh.devices.reshape(fsdp // 2, 2, ctx // 2, 2), AXES)
    owner = ("y", "core")
    flat, split = P(owner), P(owner, None)
    whole = P(owner, CTX, None)
    return jax.shard_map(
        functools.partial(body, fsdp, ctx),
        mesh=places,
        in_specs=(whole, split, split, whole, flat, split, split, split, split, flat, split, split, split),
        out_specs=(whole, whole, flat, split, split, split, split, flat, split, split, split),
        check_vma=False,
    )
```

profile of v0, /device:TPU:0, one launch (start us, length us, event | category | flops | bytes accessed | tf_op | source)
XLA Modules:
  0.0 291.4 jit_solution(6975256146641065653)
XLA Ops:
  3.0 1.3 maximum_maximum_fusion
  4.3 0.9 broadcast_select_fusion
  5.4 3.0 %collective-permute-start.2 = (bf16[144,1024]{1,0:T(8,128)(2,1)S(1)}, bf16[144,1024]{1,0:T(8,128)(2,1)S(1)}, u32[]{:S(2)}, u32[]{:S(2)}) collective-permute-start(bf16[144,1024]{1,0:T(8,128)(2,1)S(1)} %concatenate.23.refs_5_.refs_14_), channel_id=1, source_target_pairs={{0,16},{1,17},{2,18},{3,19},{4,20},{5,21},{6,22},{7,23},{8,24},{9,... | collective-permute-start | bytes 884744 | tf_op jit(solution)/shard_map/ppermute | solution.py:40
  8.4 1.6 collective-permute-start
  10.0 6.4 %collective-permute-start.1 = (bf16[592,256]{1,0:T(8,128)(2,1)}, bf16[592,256]{1,0:T(8,128)(2,1)S(1)}, u32[]{:S(2)}, u32[]{:S(2)}) collective-permute-start(bf16[592,256]{1,0:T(8,128)(2,1)} %get-tuple-element.97), channel_id=1, source_target_pairs={{0,6},{1,14},{2,8},{3,0},{4,4},{5,12},{6,10},{7,2},{8,7},{9,15},{1... | collective-permute-start | bytes 909320 | tf_op jit(solution)/shard_map/ppermute | solution.py:40
  16.4 1.0 collective-permute-start.4
  17.4 1.1 pad_maximum_fusion.refs_7_
  19.7 5.2 %collective-permute-done.1.refs_2_ = bf16[592,256]{1,0:T(8,128)(2,1)S(1)} collective-permute-done((bf16[592,256]{1,0:T(8,128)(2,1)}, bf16[592,256]{1,0:T(8,128)(2,1)S(1)}, u32[]{:S(2)}, u32[]{:S(2)}) %collective-permute-start.1) | collective-permute-done | bytes 303136 | tf_op jit(solution)/shard_map/ppermute | solution.py:40
  25.0 1.0 multiply_sine_fusion
  26.7 5.1 %shard_map.203 = (bf16[2,3,128,768]{3,2,1,0:T(8,128)(2,1)}, bf16[2,3,256,128]{3,2,1,0:T(8,128)(2,1)}, bf16[576,512]{1,0:T(8,128)(2,1)}, bf16[576,128]{1,0:T(8,12...) custom-call(s32[7]{0:T(128)} %stack.31.refs_0_, bf16[592,256]{1,0:T(8,128)(2,1)} %copy-done.4, bf16[592,256]{1,0:T(8,128)(2,1)} %copy-done.5, ...), custom_call_target="tpu_custom_call" | custom-call | tf_op jit(solution)/shard_map/pallas_call | solution.py:370
  31.9 7.1 %collective-permute-start.7 = (bf16[2,3,256,128]{3,2,1,0:T(8,128)(2,1)}, bf16[2,3,256,128]{3,2,1,0:T(8,128)(2,1)S(1)}, u32[]{:S(2)}, u32[]{:S(2)}) collective-permute-start(bf16[2,3,256,128]{3,2,1,0:T(8,128)(2,1)} %get-tuple-element.99.refs_3_.refs_6_), channel_id=1, source_target_pairs={{0,2},{1,3},{2,4},{3,5},{4,6},{5,7},{8,10},{9,11},{10,12},{11,13},... | collective-permute-start | bytes 1179656 | tf_op jit(solution)/shard_map/ppermute | solution.py:40
  39.7 10.4 %shard_map.204 = (f32[2,3,1,768]{3,2,1,0:T(1,128)}, f32[2,3,1,768]{3,2,1,0:T(1,128)}, f32[2,3,64,768]{3,2,1,0:T(8,128)}) custom-call(s32[8]{0:T(128)} %get-tuple-element.152.refs_0_, s32[2,1,256]{2,1,0:T(1,128)} %get-tuple-element.102.refs_1_, bf16[2,3,128,768]{3,2,1,0:T(8,128)(2,1)} %get-tuple-element.103.refs_2_, ...), custom_call_target="tpu_custom_call" | custom-call | tf_op jit(solution)/shard_map/pallas_call | solution.py:245
  50.3 2.2 collective-permute-start.9
  54.5 3.3 %collective-permute-start.6 = (bf16[576,256]{1,0:T(8,128)(2,1)}, bf16[576,256]{1,0:T(8,128)(2,1)}, u32[]{:S(2)}, u32[]{:S(2)}) collective-permute-start(bf16[576,256]{1,0:T(8,128)(2,1)} %get-tuple-element.189), channel_id=1, source_target_pairs={{0,6},{1,14},{2,8},{3,0},{4,4},{5,12},{6,10},{7,2},{8,7},{9,15},{1... | collective-permute-start | bytes 884744 | tf_op jit(solution)/shard_map/ppermute | solution.py:40
  57.8 3.3 %shard_map.205 = (f32[2,3,1,768]{3,2,1,0:T(1,128)}, f32[2,3,1,768]{3,2,1,0:T(1,128)}, f32[2,3,64,768]{3,2,1,0:T(8,128)}) custom-call(s32[8]{0:T(128)} %get-tuple-element.152.refs_0_, s32[2,1,256]{2,1,0:T(1,128)} %get-tuple-element.102.refs_1_, ...), custom_call_target="tpu_custom_call", output_to_operand_aliasing={{0}: (5, {}), {1}: (6, {}), {2}: (7, {})} | custom-call | tf_op jit(solution)/shard_map/pallas_call | solution.py:245
  61.9 6.0 %collective-permute-done.6.refs_4_ = bf16[576,256]{1,0:T(8,128)(2,1)} collective-permute-done((bf16[576,256]{1,0:T(8,128)(2,1)}, bf16[576,256]{1,0:T(8,128)(2,1)}, u32[]{:S(2)}, u32[]{:S(2)}) %collective-permute-start.6) | collective-permute-done | bytes 294944 | tf_op jit(solution)/shard_map/ppermute | solution.py:40
  68.4 3.8 %collective-permute-start.5 = (bf16[576,256]{1,0:T(8,128)(2,1)}, bf16[576,256]{1,0:T(8,128)(2,1)}, u32[]{:S(2)}, u32[]{:S(2)}) collective-permute-start(bf16[576,256]{1,0:T(8,128)(2,1)} %get-tuple-element.190), channel_id=1, source_target_pairs={{0,0},{1,8},{2,14},{3,6},{4,2},{5,10},{6,12},{7,4},{8,1},{9,9},{10... | collective-permute-start | bytes 884744 | tf_op jit(solution)/shard_map/ppermute | solution.py:40
  72.2 3.1 %shard_map.206 = (bf16[2,3,64,768]{3,2,1,0:T(8,128)(2,1)}, f32[2,3,1,768]{3,2,1,0:T(1,128)}) custom-call(s32[8]{0:T(128)} %get-tuple-element.152.refs_0_, s32[2,1,256]{2,1,0:T(1,128)} %get-tuple-element.102.refs_1_, bf16[2,3,128,768]{3,2,1,0:T(8,128)(2,1)} %get-tuple-element.103.refs_2_, bf16[2,3,256,128]{3,2,1,0:T(8,128)(2,1)} %copy-done.10, ...), custom_call_target="tpu_custom_call" | custom-call | tf_op jit(solution)/shard_map/pallas_call | solution.py:245
  76.4 20.5 %shard_map.207 = (bf16[576,256]{1,0:T(8,128)(2,1)}, bf16[576,256]{1,0:T(8,128)(2,1)}, f32[576,512]{1,0:T(8,128)}, bf16[2,3,128,768]{3,2,1,0:T(8,128)(2,1)}, f32[...) custom-call(s32[7]{0:T(128)} %stack.31.refs_0_, ...), custom_call_target="tpu_custom_call" | custom-call | tf_op jit(solution)/shard_map/pallas_call | solution.py:556
  96.9 1.6 collective-permute-start.20
  98.5 5.4 %collective-permute-done.20.got = bf16[2,6016,128]{2,1,0:T(8,128)(2,1)S(1)} collective-permute-done((bf16[2,6016,128]{2,1,0:T(8,128)(2,1)}, bf16[2,6016,128]{2,1,0:T(8,128)(2,1)S(1)}, u32[]{:S(2)}, u32[]{:S(2)}) %collective-permute-start.20) | collective-permute-done | bytes 3080224 | tf_op jit(solution)/shard_map/ppermute | solution.py:40
  103.9 1.6 copy-done
  105.6 4.3 %shard_map.208 = (bf16[2,1504,128]{2,1,0:T(8,128)(2,1)}, bf16[2,1504,128]{2,1,0:T(8,128)(2,1)}) custom-call(s32[1]{0:T(128)} %bitcast.13.x.sc, bf16[2,6016,128]{2,1,0:T(8,128)(2,1)} %get-tuple-element.124.mine, bf16[2,6016,128]{2,1,0:T(8,128)(2,1)} %copy-done), custom_call_target="tpu_custom_call" | custom-call | tf_op jit(solution)/shard_map/pallas_call | solution.py:792
  110.4 0.9 collective-permute-start.22
  111.3 3.5 %shard_map.210 = (f32[2,3,64,768]{3,2,1,0:T(8,128)}, bf16[2,3,256,128]{3,2,1,0:T(8,128)(2,1)}, bf16[3,256,128]{2,1,0:T(8,128)(2,1)}, bf16[3,256,128]{2,1,0:T(8,128)(2,1)}) custom-call(s32[8]{0:T(128)} %get-tuple-element.152.refs_0_, s32[2,1,256]{2,1,0:T(1,128)} %get-tuple-element.102.refs_1_, bf16[2,3,128,768]{3,2,1,0:T(8,128)(2,1)} %get-tuple-element.103.refs_2_, ...), custom_call_target="tpu_custom_call" | custom-call | tf_op jit(solution)/shard_map/pallas_call | solution.py:271
  115.3 1.1 collective-permute-done.25.twin_a
  117.4 2.0 shard_map.211
  119.4 1.5 collective-permute-start.29
  120.9 4.0 %shard_map.212 = (f32[2,3,64,768]{3,2,1,0:T(8,128)}, bf16[2,3,256,128]{3,2,1,0:T(8,128)(2,1)}, bf16[3,256,128]{2,1,0:T(8,128)(2,1)}, bf16[3,256,128]{2,1,0:T(8,128)(2,1)}) custom-call(s32[8]{0:T(128)} %get-tuple-element.152.refs_0_, s32[2,1,256]{2,1,0:T(1,128)} %get-tuple-element.102.refs_1_, ...), custom_call_target="tpu_custom_call", output_to_operand_aliasing={{0}: (8, {})} | custom-call | tf_op jit(solution)/shard_map/pallas_call | solution.py:271
  125.4 1.1 collective-permute-done.27.twin_a
  127.3 20.9 %collective-permute-start.19 = (bf16[576,256]{1,0:T(8,128)(2,1)S(1)}, bf16[576,256]{1,0:T(8,128)(2,1)S(1)}, u32[]{:S(2)}, u32[]{:S(2)}) collective-permute-start(bf16[576,256]{1,0:T(8,128)(2,1)S(1)} %copy-done.41), channel_id=1, source_target_pairs={{6,0},{14,1},{8,2},{0,3},{4,4},{12,5},{10,6},{2,7},{7,8},{15,9},{9... | collective-permute-start | bytes 884744 | tf_op jit(solution)/shard_map/ppermute | solution.py:40
  149.0 2.2 shard_map.213
  151.2 0.9 copy-done.18
  152.0 0.9 copy-done.19
  152.9 4.9 %shard_map.209 = (bf16[1504,128]{1,0:T(8,128)(2,1)}, bf16[1504,128]{1,0:T(8,128)(2,1)}, bf16[1504,128]{1,0:T(8,128)(2,1)}, bf16[1504,128]{1,0:T(8,128)(2,1)}) custom-call(s32[1]{0:T(128)} %bitcast.13.x.sc, bf16[2,6016,128]{2,1,0:T(8,128)(2,1)} %get-tuple-element.124.mine, bf16[2,6016,128]{2,1,0:T(8,128)(2,1)} %copy-done, bf16[2,1504,128]{2,1,0:T(8,128)(2,1)} %copy-done.18, ...), custom_call_target="tpu_custom_call" | custom-call | tf_op jit(solution)/shard_map/pallas_call | solution.py:834
  157.8 1.3 collective-permute-start.32
  159.1 2.7 collective-permute-start.23
  161.7 12.0 %shard_map.214 = (f32[2,3,64,768]{3,2,1,0:T(8,128)}, f32[2,3,256,128]{3,2,1,0:T(8,128)}, bf16[3,256,128]{2,1,0:T(8,128)(2,1)}, bf16[3,256,128]{2,1,0:T(8,128)(2,1)}) custom-call(s32[8]{0:T(128)} %get-tuple-element.152.refs_0_, s32[2,1,256]{2,1,0:T(1,128)} %get-tuple-element.102.refs_1_, ...), custom_call_target="tpu_custom_call", output_to_operand_aliasing={{0}: (8, {})} | custom-call | tf_op jit(solution)/shard_map/pallas_call | solution.py:271
  173.7 3.7 %collective-permute-start.30 = (bf16[3,256,128]{2,1,0:T(8,128)(2,1)}, bf16[3,256,128]{2,1,0:T(8,128)(2,1)S(1)}, u32[]{:S(2)}, u32[]{:S(2)}) collective-permute-start(bf16[3,256,128]{2,1,0:T(8,128)(2,1)} %get-tuple-element.162), channel_id=1, source_target_pairs={{0,8},{1,9},{2,10},{3,11},{4,12},{5,13},{6,14},{7,15},{8,0},{9,1},... | collective-permute-start | bytes 589832 | tf_op jit(solution)/shard_map/ppermute | solution.py:40
  177.6 1.2 collective-permute-done.30.refs_11_
  179.9 6.9 %shard_map.215 = (bf16[576,256]{1,0:T(8,128)(2,1)}, bf16[576,256]{1,0:T(8,128)(2,1)}, bf16[2,1152,128]{2,1,0:T(8,128)(2,1)}, bf16[2,1152,128]{2,1,0:T(8,128)(2,1)}) custom-call(s32[7]{0:T(128)} %stack.31.refs_0_, bf16[592,256]{1,0:T(8,128)(2,1)} %copy-done.4, bf16[592,256]{1,0:T(8,128)(2,1)} %copy-done.5, f32[32,512]{1,0:T(8,128)} %get-tuple-element.194.refs_3_, ...), custom_call_target="tpu_custom_call" | custom-call | tf_op jit(solution)/shard_map/pallas_call | solution.py:649
  187.2 2.4 shard_map.218
  189.5 6.0 %all-to-all-start.2 = ((bf16[4,752,128]{2,1,0:T(8,128)(2,1)}), bf16[4,752,128]{2,1,0:T(8,128)(2,1)S(1)}, u32[]{:S(2)}, u32[]{:S(2)}) async-start(bf16[4,752,128]{2,1,0:T(8,128)(2,1)} %bitcast.35), calls=%async_computation.2 | async-start | bytes 1540096 | tf_op jit(solution)/shard_map/all_to_all | solution.py:751
  195.6 2.4 collective-permute-start.36
  198.0 7.2 %collective-permute-done.36 = bf16[1152,128]{1,0:T(8,128)(2,1)S(1)} collective-permute-done((bf16[1152,128]{1,0:T(8,128)(2,1)S(1)}, bf16[1152,128]{1,0:T(8,128)(2,1)S(1)}, u32[]{:S(2)}, u32[]{:S(2)}) %collective-permute-start.36) | collective-permute-done | bytes 294944 | tf_op jit(solution)/shard_map/ppermute | solution.py:40
  206.0 9.7 %all-to-all-done.2.got = bf16[4,752,128]{2,1,0:T(8,128)(2,1)S(1)} async-done(((bf16[4,752,128]{2,1,0:T(8,128)(2,1)}), bf16[4,752,128]{2,1,0:T(8,128)(2,1)S(1)}, u32[]{:S(2)}, u32[]{:S(2)}) %all-to-all-start.2) | async-done | bytes 770080 | tf_op jit(solution)/shard_map/all_to_all | solution.py:751
  215.7 3.4 %all-to-all-start = ((bf16[8,144,128]{2,1,0:T(8,128)(2,1)}), bf16[8,144,128]{2,1,0:T(8,128)(2,1)S(1)}, u32[]{:S(2)}, u32[]{:S(2)}) async-start(bf16[8,144,128]{2,1,0:T(8,128)(2,1)} %bitcast.20), calls=%async_computation | async-start | bytes 589824 | tf_op jit(solution)/shard_map/all_to_all | solution.py:751
  219.1 2.1 shard_map.219
  221.3 6.9 %all-to-all-done.got = bf16[8,144,128]{2,1,0:T(8,128)(2,1)S(1)} async-done(((bf16[8,144,128]{2,1,0:T(8,128)(2,1)}), bf16[8,144,128]{2,1,0:T(8,128)(2,1)S(1)}, u32[]{:S(2)}, u32[]{:S(2)}) %all-to-all-start) | async-done | bytes 294944 | tf_op jit(solution)/shard_map/all_to_all | solution.py:751
  228.2 3.5 %all-to-all-start.3 = ((bf16[4,752,128]{2,1,0:T(8,128)(2,1)}), bf16[4,752,128]{2,1,0:T(8,128)(2,1)S(1)}, u32[]{:S(2)}, u32[]{:S(2)}) async-start(bf16[4,752,128]{2,1,0:T(8,128)(2,1)} %shard_map.219), calls=%async_computation.3 | async-start | bytes 1540096 | tf_op jit(solution)/shard_map/all_to_all | solution.py:753
  231.7 1.6 collective-permute-start.33
  233.3 5.1 %collective-permute-start.34 = (bf16[576,256]{1,0:T(8,128)(2,1)S(1)}, bf16[576,256]{1,0:T(8,128)(2,1)S(1)}, u32[]{:S(2)}, u32[]{:S(2)}) collective-permute-start(bf16[576,256]{1,0:T(8,128)(2,1)S(1)} %copy-done.43), channel_id=1, source_target_pairs={{6,0},{14,1},{8,2},{0,3},{4,4},{12,5},{10,6},{2,7},{7,8},{15,9},{9... | collective-permute-start | bytes 884744 | tf_op jit(solution)/shard_map/ppermute | solution.py:40
  238.5 1.7 shard_map.216
  240.2 22.3 %all-to-all-done.3 = bf16[4,752,128]{2,1,0:T(8,128)(2,1)S(1)} async-done(((bf16[4,752,128]{2,1,0:T(8,128)(2,1)}), bf16[4,752,128]{2,1,0:T(8,128)(2,1)S(1)}, u32[]{:S(2)}, u32[]{:S(2)}) %all-to-all-start.3) | async-done | bytes 770080 | tf_op jit(solution)/shard_map/all_to_all | solution.py:753
  262.4 3.4 %all-to-all-start.1 = ((bf16[8,144,128]{2,1,0:T(8,128)(2,1)}), bf16[8,144,128]{2,1,0:T(8,128)(2,1)S(1)}, u32[]{:S(2)}, u32[]{:S(2)}) async-start(bf16[8,144,128]{2,1,0:T(8,128)(2,1)} %shard_map.216), calls=%async_computation.1 | async-start | bytes 589824 | tf_op jit(solution)/shard_map/all_to_all | solution.py:753
  265.9 1.9 collective-permute-start.37
  267.8 0.9 maximum_bitcast_fusion
  268.8 0.9 maximum_bitcast_fusion.1
  269.6 5.2 %all-to-all-done.1 = bf16[8,144,128]{2,1,0:T(8,128)(2,1)S(1)} async-done(((bf16[8,144,128]{2,1,0:T(8,128)(2,1)}), bf16[8,144,128]{2,1,0:T(8,128)(2,1)S(1)}, u32[]{:S(2)}, u32[]{:S(2)}) %all-to-all-start.1) | async-done | bytes 294944 | tf_op jit(solution)/shard_map/all_to_all | solution.py:753
  275.6 1.8 shard_map.217
  277.4 1.7 slice_reduce_fusion
  279.2 8.2 %collective-permute-done.37.far = bf16[3008,128]{1,0:T(8,128)(2,1)S(1)} collective-permute-done((bf16[3008,128]{1,0:T(8,128)(2,1)S(1)}, bf16[3008,128]{1,0:T(8,128)(2,1)S(1)}, u32[]{:S(2)}, u32[]{:S(2)}) %collective-permute-start.37) | collective-permute-done | bytes 770080 | tf_op jit(solution)/shard_map/ppermute | solution.py:40
  287.4 0.9 copy-done.20
  288.3 3.2 %shard_map.220 = (f32[144,1536]{1,0:T(8,128)}, f32[144,1536]{1,0:T(8,128)}, f32[144,576]{1,0:T(8,128)}, f32[576,384]{1,0:T(8,128)}) custom-call(s32[1]{0:T(128)} %bitcast.13.x.sc, bf16[3008,128]{1,0:T(8,128)(2,1)} %bitcast.37, bf16[3008,128]{1,0:T(8,128)(2,1)} %copy-done.20), custom_call_target="tpu_custom_call" | custom-call | tf_op jit(solution)/shard_map/pallas_call | solution.py:705
  (151 shorter events, 17.1 us)
Async XLA Ops:
  4.3 13.1 %copy-start.23 = (bf16[144,1536]{1,0:T(8,128)(2,1)S(1)}, bf16[144,1536]{1,0:T(8,128)(2,1)}, u32[]{:S(2)}) copy-start(bf16[144,1536]{1,0:T(8,128)(2,1)} %param.23) | copy-start | bytes 1327108
  4.3 13.1 %copy-start.38 = (bf16[144,576]{1,0:T(8,128)(2,1)S(1)}, bf16[144,576]{1,0:T(8,128)(2,1)}, u32[]{:S(2)}) copy-start(bf16[144,576]{1,0:T(8,128)(2,1)} %param.20) | copy-start | bytes 497668
  5.3 20.6 %copy-start.6 = (bf16[144,1024]{1,0:T(8,128)(2,1)}, bf16[144,1024]{1,0:T(8,128)(2,1)S(1)}, u32[]{:S(2)}) copy-start(bf16[144,1024]{1,0:T(8,128)(2,1)S(1)} %concatenate.23.refs_5_.refs_14_) | copy-start | bytes 884740
  5.4 11.0 %collective-permute-start.2 = (bf16[144,1024]{1,0:T(8,128)(2,1)S(1)}, bf16[144,1024]{1,0:T(8,128)(2,1)S(1)}, u32[]{:S(2)}, u32[]{:S(2)}) collective-permute-start(bf16[144,1024]{1,0:T(8,128)(2,1)S(1)} %concatenate.23.refs_5_.refs_14_), channel_id=1, source_target_pairs={{0,16},{1,17},{2,18},{3,19},{4,20},{5,21},{6,22},{7,23},{8,24},{9,... | collective-permute-start | bytes 884744 | tf_op jit(solution)/shard_map/ppermute | solution.py:40
  8.4 17.6 %collective-permute-start.3 = (bf16[144,1024]{1,0:T(8,128)(2,1)S(1)}, bf16[144,1024]{1,0:T(8,128)(2,1)S(1)}, u32[]{:S(2)}, u32[]{:S(2)}) collective-permute-start(bf16[144,1024]{1,0:T(8,128)(2,1)S(1)} %concatenate.23.refs_5_.refs_14_), channel_id=1, source_target_pairs={{0,8},{1,9},{2,10},{3,11},{4,12},{5,13},{6,14},{7,15},{8,0},{9,1},... | collective-permute-start | bytes 884744 | tf_op jit(solution)/shard_map/ppermute | solution.py:40
  8.4 11.3 %collective-permute-start = (bf16[592,256]{1,0:T(8,128)(2,1)}, bf16[592,256]{1,0:T(8,128)(2,1)S(1)}, u32[]{:S(2)}, u32[]{:S(2)}) collective-permute-start(bf16[592,256]{1,0:T(8,128)(2,1)} %get-tuple-element.96), channel_id=1, source_target_pairs={{0,0},{1,8},{2,14},{3,6},{4,2},{5,10},{6,12},{7,4},{8,1},{9,9},{10... | collective-permute-start | bytes 909320 | tf_op jit(solution)/shard_map/ppermute | solution.py:40
  10.0 15.0 %collective-permute-start.1 = (bf16[592,256]{1,0:T(8,128)(2,1)}, bf16[592,256]{1,0:T(8,128)(2,1)S(1)}, u32[]{:S(2)}, u32[]{:S(2)}) collective-permute-start(bf16[592,256]{1,0:T(8,128)(2,1)} %get-tuple-element.97), channel_id=1, source_target_pairs={{0,6},{1,14},{2,8},{3,0},{4,4},{5,12},{6,10},{7,2},{8,7},{9,15},{1... | collective-permute-start | bytes 909320 | tf_op jit(solution)/shard_map/ppermute | solution.py:40
  16.4 9.6 %copy-start.12 = (bf16[144,1024]{1,0:T(8,128)(2,1)}, bf16[144,1024]{1,0:T(8,128)(2,1)S(1)}, u32[]{:S(2)}) copy-start(bf16[144,1024]{1,0:T(8,128)(2,1)S(1)} %collective-permute-done.2.refs_6_.refs_15_) | copy-start | bytes 884740
  16.4 2.2 collective-permute-start.4
  18.5 34.0 %copy-start.1 = (bf16[144,3648]{1,0:T(8,128)(2,1)}, bf16[144,3648]{1,0:T(8,128)(2,1)S(1)}, u32[]{:S(2)}) copy-start(bf16[144,3648]{1,0:T(8,128)(2,1)S(1)} %pad_maximum_fusion.refs_7_) | copy-start | bytes 3151876
  18.6 7.4 %copy-start.14 = (bf16[144,1024]{1,0:T(8,128)(2,1)}, bf16[144,1024]{1,0:T(8,128)(2,1)S(1)}, u32[]{:S(2)}) copy-start(bf16[144,1024]{1,0:T(8,128)(2,1)S(1)} %collective-permute-done.4.refs_8_.refs_17_) | copy-start | bytes 884740
  18.6 34.2 %collective-permute-start.12 = (bf16[144,3648]{1,0:T(8,128)(2,1)S(1)}, bf16[144,3648]{1,0:T(8,128)(2,1)}, u32[]{:S(2)}, u32[]{:S(2)}) collective-permute-start(bf16[144,3648]{1,0:T(8,128)(2,1)S(1)} %pad_maximum_fusion.refs_7_), channel_id=1, source_target_pairs={{0,16},{1,17},{2,18},{3,19},{4,20},{5,21},{6,22},{7,23},{8,24},{9,... | collective-permute-start | bytes 3151880 | tf_op jit(solution)/shard_map/ppermute | solution.py:40
  19.7 6.3 %copy-start.4 = (bf16[592,256]{1,0:T(8,128)(2,1)}, bf16[592,256]{1,0:T(8,128)(2,1)S(1)}, u32[]{:S(2)}) copy-start(bf16[592,256]{1,0:T(8,128)(2,1)S(1)} %collective-permute-done.refs_1_) | copy-start | bytes 909316
  31.8 21.8 %copy-start.21 = (bf16[1,512,576]{1,2,0:T(8,128)(2,1)S(1)}, bf16[1,512,576]{1,2,0:T(8,128)(2,1)}, u32[]{:S(2)}) copy-start(bf16[1,512,576]{1,2,0:T(8,128)(2,1)} %param.15) | copy-start | bytes 1769476
  31.8 7.2 %collective-permute-start.8 = (bf16[2,3,256,128]{3,2,1,0:T(8,128)(2,1)}, bf16[2,3,256,128]{3,2,1,0:T(8,128)(2,1)S(1)}, u32[]{:S(2)}, u32[]{:S(2)}) collective-permute-start(bf16[2,3,256,128]{3,2,1,0:T(8,128)(2,1)} %get-tuple-element.99.refs_3_.refs_6_), channel_id=1, source_target_pairs={{0,8},{1,9},{2,10},{3,11},{4,12},{5,13},{6,14},{7,15},{8,0},{9,1},... | collective-permute-start | bytes 1179656 | tf_op jit(solution)/shard_map/ppermute | solution.py:40
  31.9 18.3 %collective-permute-start.7 = (bf16[2,3,256,128]{3,2,1,0:T(8,128)(2,1)}, bf16[2,3,256,128]{3,2,1,0:T(8,128)(2,1)S(1)}, u32[]{:S(2)}, u32[]{:S(2)}) collective-permute-start(bf16[2,3,256,128]{3,2,1,0:T(8,128)(2,1)} %get-tuple-element.99.refs_3_.refs_6_), channel_id=1, source_target_pairs={{0,2},{1,3},{2,4},{3,5},{4,6},{5,7},{8,10},{9,11},{10,12},{11,13},... | collective-permute-start | bytes 1179656 | tf_op jit(solution)/shard_map/ppermute | solution.py:40
  50.2 7.7 %copy-start.8 = (bf16[2,3,256,128]{3,2,1,0:T(8,128)(2,1)}, bf16[2,3,256,128]{3,2,1,0:T(8,128)(2,1)S(1)}, u32[]{:S(2)}) copy-start(bf16[2,3,256,128]{3,2,1,0:T(8,128)(2,1)S(1)} %collective-permute-done.7.refs_3_.refs_6_) | copy-start | bytes 1179652
  50.2 4.3 %collective-permute-start.10 = (bf16[2,3,256,128]{3,2,1,0:T(8,128)(2,1)S(1)}, bf16[2,3,256,128]{3,2,1,0:T(8,128)(2,1)S(1)}, u32[]{:S(2)}, u32[]{:S(2)}) collective-permute-start(bf16[2,3,256,128]{3,2,1,0:T(8,128)(2,1)S(1)} %collective-permute-done.7.refs_3_.refs_6_), channel_id=1, source_target_pairs={{0,8},{1,9},{2,10},{3,11},{4,12},{5,13},{6,14},{7,15},{8,0},{9,1},... | collective-permute-start | bytes 1179656 | tf_op jit(solution)/shard_map/ppermute | solution.py:40
  50.3 11.6 %collective-permute-start.9 = (bf16[2,3,256,128]{3,2,1,0:T(8,128)(2,1)S(1)}, bf16[2,3,256,128]{3,2,1,0:T(8,128)(2,1)S(1)}, u32[]{:S(2)}, u32[]{:S(2)}) collective-permute-start(bf16[2,3,256,128]{3,2,1,0:T(8,128)(2,1)S(1)} %collective-permute-done.7.refs_3_.refs_6_), channel_id=1, source_target_pairs={{0,2},{1,3},{2,4},{3,5},{4,6},{5,7},{8,10},{9,11},{10,12},{11,13},... | collective-permute-start | bytes 1179656 | tf_op jit(solution)/shard_map/ppermute | solution.py:40
  52.5 22.8 %collective-permute-start.13 = (bf16[144,3648]{1,0:T(8,128)(2,1)S(1)}, bf16[144,3648]{1,0:T(8,128)(2,1)S(1)}, u32[]{:S(2)}, u32[]{:S(2)}) collective-permute-start(bf16[144,3648]{1,0:T(8,128)(2,1)S(1)} %pad_maximum_fusion.refs_7_), channel_id=1, source_target_pairs={{0,8},{1,9},{2,10},{3,11},{4,12},{5,13},{6,14},{7,15},{8,0},{9,1},... | collective-permute-start | bytes 3151880 | tf_op jit(solution)/shard_map/ppermute | solution.py:40
  52.7 22.6 %collective-permute-start.14 = (bf16[144,3648]{1,0:T(8,128)(2,1)}, bf16[144,3648]{1,0:T(8,128)(2,1)}, u32[]{:S(2)}, u32[]{:S(2)}) collective-permute-start(bf16[144,3648]{1,0:T(8,128)(2,1)} %collective-permute-done.12.refs_8_), channel_id=1, source_target_pairs={{0,8},{1,9},{2,10},{3,11},{4,12},{5,13},{6,14},{7,15},{8,0},{9,1},... | collective-permute-start | bytes 3151880 | tf_op jit(solution)/shard_map/ppermute | solution.py:40
  53.1 14.8 %collective-permute-start.15 = (bf16[576,384]{1,0:T(8,128)(2,1)}, bf16[576,384]{1,0:T(8,128)(2,1)}, u32[]{:S(2)}, u32[]{:S(2)}) collective-permute-start(bf16[576,384]{1,0:T(8,128)(2,1)} %bitcast.41), channel_id=1, source_target_pairs={{0,16},{1,17},{2,18},{3,19},{4,20},{5,21},{6,22},{7,23},{8,24},{9,... | collective-permute-start | bytes 1327112 | tf_op jit(solution)/shard_map/ppermute | solution.py:40
  54.5 13.5 %copy-start.24 = (bf16[384,576]{0,1:T(8,128)(2,1)S(1)}, bf16[384,576]{0,1:T(8,128)(2,1)}, u32[]{:S(2)}) copy-start(bf16[384,576]{0,1:T(8,128)(2,1)} %param.24) | copy-start | bytes 1327108
  54.5 13.4 %collective-permute-start.6 = (bf16[576,256]{1,0:T(8,128)(2,1)}, bf16[576,256]{1,0:T(8,128)(2,1)}, u32[]{:S(2)}, u32[]{:S(2)}) collective-permute-start(bf16[576,256]{1,0:T(8,128)(2,1)} %get-tuple-element.189), channel_id=1, source_target_pairs={{0,6},{1,14},{2,8},{3,0},{4,4},{5,12},{6,10},{7,2},{8,7},{9,15},{1... | collective-permute-start | bytes 884744 | tf_op jit(solution)/shard_map/ppermute | solution.py:40
  61.9 10.3 %copy-start.10 = (bf16[2,3,256,128]{3,2,1,0:T(8,128)(2,1)}, bf16[2,3,256,128]{3,2,1,0:T(8,128)(2,1)S(1)}, u32[]{:S(2)}) copy-start(bf16[2,3,256,128]{3,2,1,0:T(8,128)(2,1)S(1)} %collective-permute-done.9.refs_3_.refs_6_) | copy-start | bytes 1179652
  61.9 6.5 %collective-permute-start.11 = (bf16[2,3,256,128]{3,2,1,0:T(8,128)(2,1)S(1)}, bf16[2,3,256,128]{3,2,1,0:T(8,128)(2,1)S(1)}, u32[]{:S(2)}, u32[]{:S(2)}) collective-permute-start(bf16[2,3,256,128]{3,2,1,0:T(8,128)(2,1)S(1)} %collective-permute-done.9.refs_3_.refs_6_), channel_id=1, source_target_pairs={{0,8},{1,9},{2,10},{3,11},{4,12},{5,13},{6,14},{7,15},{8,0},{9,1},... | collective-permute-start | bytes 1179656 | tf_op jit(solution)/shard_map/ppermute | solution.py:40
  67.9 7.4 %collective-permute-start.16 = (bf16[576,384]{1,0:T(8,128)(2,1)S(1)}, bf16[576,384]{1,0:T(8,128)(2,1)S(1)}, u32[]{:S(2)}, u32[]{:S(2)}) collective-permute-start(bf16[576,384]{1,0:T(8,128)(2,1)S(1)} %bitcast.43), channel_id=1, source_target_pairs={{0,8},{1,9},{2,10},{3,11},{4,12},{5,13},{6,14},{7,15},{8,0},{9,1},... | collective-permute-start | bytes 1327112 | tf_op jit(solution)/shard_map/ppermute | solution.py:40
  67.9 7.4 %collective-permute-start.17 = (bf16[576,384]{1,0:T(8,128)(2,1)}, bf16[576,384]{1,0:T(8,128)(2,1)}, u32[]{:S(2)}, u32[]{:S(2)}) collective-permute-start(bf16[576,384]{1,0:T(8,128)(2,1)} %collective-permute-done.15.refs_12_), channel_id=1, source_target_pairs={{0,8},{1,9},{2,10},{3,11},{4,12},{5,13},{6,14},{7,15},{8,0},{9,1},... | collective-permute-start | bytes 1327112 | tf_op jit(solution)/shard_map/ppermute | solution.py:40
  68.4 6.8 %collective-permute-start.5 = (bf16[576,256]{1,0:T(8,128)(2,1)}, bf16[576,256]{1,0:T(8,128)(2,1)}, u32[]{:S(2)}, u32[]{:S(2)}) collective-permute-start(bf16[576,256]{1,0:T(8,128)(2,1)} %get-tuple-element.190), channel_id=1, source_target_pairs={{0,0},{1,8},{2,14},{3,6},{4,2},{5,10},{6,12},{7,4},{8,1},{9,9},{10... | collective-permute-start | bytes 884744 | tf_op jit(solution)/shard_map/ppermute | solution.py:40
  96.9 7.1 %collective-permute-start.20 = (bf16[2,6016,128]{2,1,0:T(8,128)(2,1)}, bf16[2,6016,128]{2,1,0:T(8,128)(2,1)S(1)}, u32[]{:S(2)}, u32[]{:S(2)}) collective-permute-start(bf16[2,6016,128]{2,1,0:T(8,128)(2,1)} %get-tuple-element.125), channel_id=1, source_target_pairs={{0,8},{1,9},{2,10},{3,11},{4,12},{5,13},{6,14},{7,15},{8,0},{9,1},... | collective-permute-start | bytes 9240584 | tf_op jit(solution)/shard_map/ppermute | solution.py:40
  109.8 41.3 %collective-permute-start.21 = (bf16[2,1504,128]{2,1,0:T(8,128)(2,1)}, bf16[2,1504,128]{2,1,0:T(8,128)(2,1)S(1)}, u32[]{:S(2)}, u32[]{:S(2)}) collective-permute-start(bf16[2,1504,128]{2,1,0:T(8,128)(2,1)} %get-tuple-element.128), channel_id=1, source_target_pairs={{0,16},{1,17},{2,18},{3,19},{4,20},{5,21},{6,22},{7,23},{8,24},{9,... | collective-permute-start | bytes 2310152 | tf_op jit(solution)/shard_map/ppermute | solution.py:40
  110.4 40.8 %collective-permute-start.22 = (bf16[2,1504,128]{2,1,0:T(8,128)(2,1)}, bf16[2,1504,128]{2,1,0:T(8,128)(2,1)S(1)}, u32[]{:S(2)}, u32[]{:S(2)}) collective-permute-start(bf16[2,1504,128]{2,1,0:T(8,128)(2,1)} %get-tuple-element.129), channel_id=1, source_target_pairs={{0,1},{1,0},{2,3},{3,2},{4,5},{5,4},{6,7},{7,6},{8,9},{9,8},{10,11... | collective-permute-start | bytes 2310152 | tf_op jit(solution)/shard_map/ppermute | solution.py:40
  114.8 1.7 collective-permute-start.25
  114.8 1.9 collective-permute-start.26
  119.4 28.8 %collective-permute-start.29 = (bf16[2,3,256,128]{3,2,1,0:T(8,128)(2,1)}, bf16[2,3,256,128]{3,2,1,0:T(8,128)(2,1)S(1)}, u32[]{:S(2)}, u32[]{:S(2)}) collective-permute-start(bf16[2,3,256,128]{3,2,1,0:T(8,128)(2,1)} %shard_map.211), channel_id=1, source_target_pairs={{2,0},{3,1},{4,2},{5,3},{6,4},{7,5},{10,8},{11,9},{12,10},{13,11},... | collective-permute-start | bytes 1179656 | tf_op jit(solution)/shard_map/ppermute | solution.py:40
  120.9 5.6 %copy-start.42 = (bf16[576,256]{1,0:T(8,128)(2,1)S(1)}, bf16[576,256]{1,0:T(8,128)(2,1)}, u32[]{:S(2)}) copy-start(bf16[576,256]{1,0:T(8,128)(2,1)} %get-tuple-element.122) | copy-start | bytes 884740
  120.9 6.3 %copy-start.41 = (bf16[576,256]{1,0:T(8,128)(2,1)S(1)}, bf16[576,256]{1,0:T(8,128)(2,1)}, u32[]{:S(2)}) copy-start(bf16[576,256]{1,0:T(8,128)(2,1)} %get-tuple-element.123) | copy-start | bytes 884740
  124.9 1.7 collective-permute-start.27
  125.1 2.1 collective-permute-start.28
  126.5 21.6 %copy-start.33 = (bf16[3,256,128]{2,1,0:T(8,128)(2,1)}, bf16[3,256,128]{2,1,0:T(8,128)(2,1)S(1)}, u32[]{:S(2)}) copy-start(bf16[3,256,128]{2,1,0:T(8,128)(2,1)S(1)} %collective-permute-done.27.twin_a) | copy-start | bytes 589828
  126.5 47.2 %collective-permute-start.18 = (bf16[576,256]{1,0:T(8,128)(2,1)S(1)}, bf16[576,256]{1,0:T(8,128)(2,1)S(1)}, u32[]{:S(2)}, u32[]{:S(2)}) collective-permute-start(bf16[576,256]{1,0:T(8,128)(2,1)S(1)} %copy-done.42), channel_id=1, source_target_pairs={{0,0},{8,1},{14,2},{6,3},{2,4},{10,5},{12,6},{4,7},{1,8},{9,9},{15... | collective-permute-start | bytes 884744 | tf_op jit(solution)/shard_map/ppermute | solution.py:40
  127.2 21.0 %copy-start.34 = (bf16[3,256,128]{2,1,0:T(8,128)(2,1)}, bf16[3,256,128]{2,1,0:T(8,128)(2,1)S(1)}, u32[]{:S(2)}) copy-start(bf16[3,256,128]{2,1,0:T(8,128)(2,1)S(1)} %collective-permute-done.28.twin_b) | copy-start | bytes 589828
  127.3 50.2 %collective-permute-start.19 = (bf16[576,256]{1,0:T(8,128)(2,1)S(1)}, bf16[576,256]{1,0:T(8,128)(2,1)S(1)}, u32[]{:S(2)}, u32[]{:S(2)}) collective-permute-start(bf16[576,256]{1,0:T(8,128)(2,1)S(1)} %copy-done.41), channel_id=1, source_target_pairs={{6,0},{14,1},{8,2},{0,3},{4,4},{12,5},{10,6},{2,7},{7,8},{15,9},{9... | collective-permute-start | bytes 884744 | tf_op jit(solution)/shard_map/ppermute | solution.py:40
  151.2 6.6 %copy-start.26 = (bf16[2,3,256,128]{3,2,1,0:T(8,128)(2,1)S(1)}, bf16[2,3,256,128]{3,2,1,0:T(8,128)(2,1)}, u32[]{:S(2)}) copy-start(bf16[2,3,256,128]{3,2,1,0:T(8,128)(2,1)} %shard_map.213) | copy-start | bytes 1179652
  157.8 21.3 %collective-permute-start.32 = (bf16[2,3,256,128]{3,2,1,0:T(8,128)(2,1)S(1)}, bf16[2,3,256,128]{3,2,1,0:T(8,128)(2,1)S(1)}, u32[]{:S(2)}, u32[]{:S(2)}) collective-permute-start(bf16[2,3,256,128]{3,2,1,0:T(8,128)(2,1)S(1)} %copy-done.26), channel_id=1, source_target_pairs={{2,0},{3,1},{4,2},{5,3},{6,4},{7,5},{10,8},{11,9},{12,10},{13,11},... | collective-permute-start | bytes 1179656 | tf_op jit(solution)/shard_map/ppermute | solution.py:40
  159.1 18.5 %collective-permute-start.23 = (bf16[1504,128]{1,0:T(8,128)(2,1)}, bf16[1504,128]{1,0:T(8,128)(2,1)S(1)}, u32[]{:S(2)}, u32[]{:S(2)}) collective-permute-start(bf16[1504,128]{1,0:T(8,128)(2,1)} %get-tuple-element.132), channel_id=1, source_target_pairs={{0,1},{1,0},{2,3},{3,2},{4,5},{5,4},{6,7},{7,6},{8,9},{9,8},{10,11... | collective-permute-start | bytes 1155080 | tf_op jit(solution)/shard_map/ppermute | solution.py:40
  161.7 15.8 %collective-permute-start.24 = (bf16[1504,128]{1,0:T(8,128)(2,1)}, bf16[1504,128]{1,0:T(8,128)(2,1)S(1)}, u32[]{:S(2)}, u32[]{:S(2)}) collective-permute-start(bf16[1504,128]{1,0:T(8,128)(2,1)} %get-tuple-element.133), channel_id=1, source_target_pairs={{0,16},{1,17},{2,18},{3,19},{4,20},{5,21},{6,22},{7,23},{8,24},{9,... | collective-permute-start | bytes 1155080 | tf_op jit(solution)/shard_map/ppermute | solution.py:40
  173.7 5.0 %collective-permute-start.30 = (bf16[3,256,128]{2,1,0:T(8,128)(2,1)}, bf16[3,256,128]{2,1,0:T(8,128)(2,1)S(1)}, u32[]{:S(2)}, u32[]{:S(2)}) collective-permute-start(bf16[3,256,128]{2,1,0:T(8,128)(2,1)} %get-tuple-element.162), channel_id=1, source_target_pairs={{0,8},{1,9},{2,10},{3,11},{4,12},{5,13},{6,14},{7,15},{8,0},{9,1},... | collective-permute-start | bytes 589832 | tf_op jit(solution)/shard_map/ppermute | solution.py:40
  177.5 1.7 collective-permute-start.31
  177.6 9.6 %copy-start.29 = (bf16[1504,128]{1,0:T(8,128)(2,1)}, bf16[1504,128]{1,0:T(8,128)(2,1)S(1)}, u32[]{:S(2)}) copy-start(bf16[1504,128]{1,0:T(8,128)(2,1)S(1)} %collective-permute-done.23.one_came) | copy-start | bytes 1155076
  177.6 9.6 %copy-start.30 = (bf16[1504,128]{1,0:T(8,128)(2,1)}, bf16[1504,128]{1,0:T(8,128)(2,1)S(1)}, u32[]{:S(2)}) copy-start(bf16[1504,128]{1,0:T(8,128)(2,1)S(1)} %collective-permute-done.24.two_came) | copy-start | bytes 1155076
  186.8 8.7 %collective-permute-start.35 = (bf16[2,1152,128]{2,1,0:T(8,128)(2,1)}, bf16[2,1152,128]{2,1,0:T(8,128)(2,1)S(1)}, u32[]{:S(2)}, u32[]{:S(2)}) collective-permute-start(bf16[2,1152,128]{2,1,0:T(8,128)(2,1)} %get-tuple-element.168), channel_id=1, source_target_pairs={{0,8},{1,9},{2,10},{3,11},{4,12},{5,13},{6,14},{7,15},{8,0},{9,1},... | collective-permute-start | bytes 1769480 | tf_op jit(solution)/shard_map/ppermute | solution.py:40
  189.5 6.0 %copy-start.22 = (bf16[2,1152,128]{2,1,0:T(8,128)(2,1)S(1)}, bf16[2,1152,128]{2,1,0:T(8,128)(2,1)}, u32[]{:S(2)}) copy-start(bf16[2,1152,128]{2,1,0:T(8,128)(2,1)} %get-tuple-element.167) | copy-start | bytes 1769476
  189.5 26.1 %all-to-all-start.2 = ((bf16[4,752,128]{2,1,0:T(8,128)(2,1)}), bf16[4,752,128]{2,1,0:T(8,128)(2,1)S(1)}, u32[]{:S(2)}, u32[]{:S(2)}) async-start(bf16[4,752,128]{2,1,0:T(8,128)(2,1)} %bitcast.35), calls=%async_computation.2 | async-start | bytes 1540096 | tf_op jit(solution)/shard_map/all_to_all | solution.py:751
  195.6 9.5 %collective-permute-start.36 = (bf16[1152,128]{1,0:T(8,128)(2,1)S(1)}, bf16[1152,128]{1,0:T(8,128)(2,1)S(1)}, u32[]{:S(2)}, u32[]{:S(2)}) collective-permute-start(bf16[1152,128]{1,0:T(8,128)(2,1)S(1)} %fusion.1), channel_id=1, source_target_pairs={{0,16},{1,17},{2,18},{3,19},{4,20},{5,21},{6,22},{7,23},{8,24},{9,... | collective-permute-start | bytes 884744 | tf_op jit(solution)/shard_map/ppermute | solution.py:40
  215.7 12.5 %all-to-all-start = ((bf16[8,144,128]{2,1,0:T(8,128)(2,1)}), bf16[8,144,128]{2,1,0:T(8,128)(2,1)S(1)}, u32[]{:S(2)}, u32[]{:S(2)}) async-start(bf16[8,144,128]{2,1,0:T(8,128)(2,1)} %bitcast.20), calls=%async_computation | async-start | bytes 589824 | tf_op jit(solution)/shard_map/all_to_all | solution.py:751
  219.1 14.2 %copy-start.43 = (bf16[576,256]{1,0:T(8,128)(2,1)S(1)}, bf16[576,256]{1,0:T(8,128)(2,1)}, u32[]{:S(2)}) copy-start(bf16[576,256]{1,0:T(8,128)(2,1)} %get-tuple-element.166) | copy-start | bytes 884740
  228.2 10.3 %copy-start.16 = (bf16[8,144,128]{2,1,0:T(8,128)(2,1)}, bf16[8,144,128]{2,1,0:T(8,128)(2,1)S(1)}, u32[]{:S(2)}) copy-start(bf16[8,144,128]{2,1,0:T(8,128)(2,1)S(1)} %all-to-all-done.got) | copy-start | bytes 884740
  228.2 34.3 %all-to-all-start.3 = ((bf16[4,752,128]{2,1,0:T(8,128)(2,1)}), bf16[4,752,128]{2,1,0:T(8,128)(2,1)S(1)}, u32[]{:S(2)}, u32[]{:S(2)}) async-start(bf16[4,752,128]{2,1,0:T(8,128)(2,1)} %shard_map.219), calls=%async_computation.3 | async-start | bytes 1540096 | tf_op jit(solution)/shard_map/all_to_all | solution.py:753
  231.7 37.0 %collective-permute-start.33 = (bf16[576,256]{1,0:T(8,128)(2,1)}, bf16[576,256]{1,0:T(8,128)(2,1)S(1)}, u32[]{:S(2)}, u32[]{:S(2)}) collective-permute-start(bf16[576,256]{1,0:T(8,128)(2,1)} %get-tuple-element.165), channel_id=1, source_target_pairs={{0,0},{8,1},{14,2},{6,3},{2,4},{10,5},{12,6},{4,7},{1,8},{9,9},{15... | collective-permute-start | bytes 884744 | tf_op jit(solution)/shard_map/ppermute | solution.py:40
  233.3 35.4 %collective-permute-start.34 = (bf16[576,256]{1,0:T(8,128)(2,1)S(1)}, bf16[576,256]{1,0:T(8,128)(2,1)S(1)}, u32[]{:S(2)}, u32[]{:S(2)}) collective-permute-start(bf16[576,256]{1,0:T(8,128)(2,1)S(1)} %copy-done.43), channel_id=1, source_target_pairs={{6,0},{14,1},{8,2},{0,3},{4,4},{12,5},{10,6},{2,7},{7,8},{15,9},{9... | collective-permute-start | bytes 884744 | tf_op jit(solution)/shard_map/ppermute | solution.py:40
  262.4 6.3 %copy-start.2 = (bf16[4,752,128]{2,1,0:T(8,128)(2,1)}, bf16[4,752,128]{2,1,0:T(8,128)(2,1)S(1)}, u32[]{:S(2)}) copy-start(bf16[4,752,128]{2,1,0:T(8,128)(2,1)S(1)} %all-to-all-done.3) | copy-start | bytes 2310148
  262.4 12.4 %all-to-all-start.1 = ((bf16[8,144,128]{2,1,0:T(8,128)(2,1)}), bf16[8,144,128]{2,1,0:T(8,128)(2,1)S(1)}, u32[]{:S(2)}, u32[]{:S(2)}) async-start(bf16[8,144,128]{2,1,0:T(8,128)(2,1)} %shard_map.216), calls=%async_computation.1 | async-start | bytes 589824 | tf_op jit(solution)/shard_map/all_to_all | solution.py:753
  265.9 21.5 %collective-permute-start.37 = (bf16[3008,128]{1,0:T(8,128)(2,1)S(1)}, bf16[3008,128]{1,0:T(8,128)(2,1)S(1)}, u32[]{:S(2)}, u32[]{:S(2)}) collective-permute-start(bf16[3008,128]{1,0:T(8,128)(2,1)S(1)} %bitcast.36), channel_id=1, source_target_pairs={{0,1},{1,0},{2,3},{3,2},{4,5},{5,4},{6,7},{7,6},{8,9},{9,8},{10,11... | collective-permute-start | bytes 2310152 | tf_op jit(solution)/shard_map/ppermute | solution.py:40
  (22 other events, 31.0 us)
where the time goes:
time: 293 us; the launch traced here: 291 us
  starting transfers between devices  93.3 us (32%)
  Pallas kernels  93.2 us (32%)
  waiting for transfers between devices  81.1 us (28%)
  local copies, waits for them, and re-layouts  14 us (5%)
  other arithmetic  8.5 us (3%)
    ppermute x38, starting transfers between devices, along(): return lambda a: lax.ppermute(a, AXES, pairs)  77 us
    ppermute x38, waiting for transfers between devices, along(): return lambda a: lax.ppermute(a, AXES, pairs)  37.1 us
    all_to_all x2, waiting for transfers between devices, sum_over(): return lax.all_to_all(spread, axes, 0, 0, tiled=True).reshape(-1, 128)  27.5 us
    pallas_call x1, Pallas kernels, feed(): pl.pallas_call(functools.partial(feed_kernel, fsdp, len(parts), ff // 4 i...  20.5 us
    pallas_call x3, Pallas kernels, attend_backward(): pl.pallas_call(functools.partial(backward_kernel, stage, first, own_type)...  19.5 us
    pallas_call x3, Pallas kernels, attend_forward(): pl.pallas_call(functools.partial(forward_kernel, stage, last), out_shape=...  16.8 us
    all_to_all x2, waiting for transfers between devices, sum_over(): got = lax.all_to_all(parts, axes, 0, 0, tiled=True)  16.6 us
    pallas_call x5, Pallas kernels, simple_call(): pl.pallas_call(kernel, out_shape=out_shape, grid=(1,), in_specs=wholes(*g...  10.4 us
  transfers between devices with their start and end apart: 42, of which 16 were waited for; matrix products, arithmetic and copies ran while one was open for 3% of the time, Pallas kernels for 20%

commit v1 on v0

--- a/solution.py
+++ b/solution.py
@@ -219,8 +219,11 @@
     return [whole(a) for a in arrays]
 
 
-FREE = pl.CostEstimate(flops=0, bytes_accessed=0, transcendentals=0)
-LIMIT = pltpu.CompilerParams(vmem_limit_bytes=60 << 20)
+def takes(us):
+    return pl.CostEstimate(flops=int(us * 1.15e9), bytes_accessed=0, transcendentals=0)
+
+
+LIMIT = pltpu.CompilerParams(vmem_limit_bytes=(64 << 20) - (256 << 10))
 
 
 def attend_forward(stage, sc, pos, qz, pieces, carried, last):
@@ -251,7 +254,7 @@
         scratch_shapes=scratch,
         input_output_aliases=aliases,
         compiler_params=LIMIT,
-        cost_estimate=FREE,
+        cost_estimate=takes((10, 12)[stage] if stage < 2 else 3),
     )(*given)
 
 
@@ -281,7 +284,7 @@
         ],
         input_output_aliases={} if first else {len(given) - 1: 0},
         compiler_params=LIMIT,
-        cost_estimate=FREE,
+        cost_estimate=takes((12, 14)[stage] if stage < 2 else 4),
     )(*given)
 
 
@@ -303,6 +306,37 @@
 
 def norm_scale(v):
     return lax.rsqrt(jnp.mean(v * v, axis=0, keepdims=True) + EPSILON)
+
+
+def prepare_kernel(sc, tokens, positions, first, second):
+    width, count = tokens.shape
+    rows = count // 2
+    p = positions[:, pl.ds(pl.multiple_of(sc[0], 128), count)]
+    row = lax.broadcasted_iota(jnp.int32, (16, count), 0)
+    p = jnp.where(row == 0, p >> 6, jnp.where(row == 1, p & 63, 0)).astype(F32).astype(BF16)
+    for parity in range(2):
+
+        @pl.when(sc[1] == parity)
+        def _(parity=parity):
+            for half, out in enumerate((first, second)):
+                half = half ^ parity
+                out[:width] = tokens[:, half * rows : (half + 1) * rows]
+                out[width:] = p[:, half * rows : (half + 1) * rows]
+
+
+def prepare(at, h, tokens, positions):
+    width, count = tokens.shape
+    out = jax.ShapeDtypeStruct((width + 16, count // 2), BF16)
+    sc = jnp.stack([at, lax.rem(h, 2)]).astype(jnp.int32)
+    return pl.pallas_call(
+        prepare_kernel,
+        out_shape=(out, out),
+        grid=(1,),
+        in_specs=[SM] + wholes(tokens, positions),
+        out_specs=wholes(out, out),
+        compiler_params=LIMIT,
+        cost_estimate=takes(2),
+    )(sc, tokens, positions)
 
 
 def project_kernel(pieces, *refs):
@@ -378,7 +412,7 @@
             pltpu.SemaphoreType.DMA((len(parts),)),
         ],
         compiler_params=LIMIT,
-        cost_estimate=FREE,
+        cost_estimate=takes(5),
     )(sc, *xs, cos, sin, *parts)
 
 
@@ -456,9 +490,20 @@
     if rows_all > used:
         packed[:, :, used:] = jnp.zeros((2, fsdp // 2, rows_all - used, 128), BF16)
 
-    def step(j, _):
-        cols = pl.ds(pl.multiple_of(j * chunk, 128), chunk)
-        up_cols = pl.ds(pl.multiple_of(ff + j * chunk, 128), chunk)
+    sends = []
+
+    def send(at, n):
+        for k, to in enumerate((mine, give)):
+            span = pl.ds(at, n)
+            copy = pltpu.make_async_copy(
+                packed.at[k, :, span], to.at[:, span], grad_sems.at[len(sends)]
+            )
+            copy.start()
+            sends.append(copy)
+
+    for j in range(ff // chunk):
+        cols = slice(j * chunk, (j + 1) * chunk)
+        up_cols = slice(ff + j * chunk, ff + (j + 1) * chunk)
         gate_w, up_w, down_w = full[:, cols], full[:, up_cols], down[:, cols]
         gate = jnp.dot(n2[...], gate_w, preferred_element_type=F32)
         up = jnp.dot(n2[...], up_w, preferred_element_type=F32)
@@ -470,7 +515,7 @@
         d_gate = (d_hidden * up * (sig * (1.0 + gate * (1.0 - sig)))).astype(BF16)
         d_up = (d_hidden * silu).astype(BF16)
         d_second[...] += dot(gate_w, d_gate, 1, 1) + dot(up_w, d_up, 1, 1)
-        slab = pl.multiple_of(j * (chunk // 128) * shard, 8)
+        slab = j * (chunk // 128) * shard
         put_slabs(packed, sc, fsdp, slab, jnp.dot(n2_t[...], d_gate, preferred_element_type=F32))
         put_slabs(
             packed, sc, fsdp, up_at + slab, jnp.dot(n2_t[...], d_up, preferred_element_type=F32)
@@ -487,24 +532,13 @@
         else:
             for n in range(chunk // 128):
                 slab = j * (chunk // 128) + n
-                slot_k, slot_y = slot_of(sc, fsdp, lax.div(slab, down_shard // 128))
-                at = pl.multiple_of(down_at + lax.rem(slab, down_shard // 128) * width, 16)
-                packed[slot_k, slot_y, pl.ds(at, width)] = down_g[:, n * 128 : (n + 1) * 128]
-        return 0
-
-    lax.fori_loop(0, ff // chunk, step, 0)
-    spans = [(0, out_at), (down_at, rows_all - down_at), (out_at, down_at - out_at)]
-    sends = [
-        [
-            pltpu.make_async_copy(
-                packed.at[k, :, pl.ds(at, n)], to.at[:, pl.ds(at, n)], grad_sems.at[k, i]
-            )
-            for k, to in enumerate((mine, give))
-        ]
-        for i, (at, n) in enumerate(spans)
-    ]
-    for copy in sends[0] + sends[1]:
-        copy.start()
+                slot_k, slot_y = slot_of(sc, fsdp, slab // (down_shard // 128))
+                at = down_at + slab % (down_shard // 128) * width
+                packed[slot_k, slot_y, at : at + width] = down_g[:, n * 128 : (n + 1) * 128]
+        send(j * (chunk // 128) * shard, chunk // 128 * shard)
+        send(up_at + j * (chunk // 128) * shard, chunk // 128 * shard)
+
+    send(down_at, rows_all - down_at)
     res_a[...] = res[:, :rows].astype(BF16)
     res_b[...] = res[:, rows:].astype(BF16)
     d_v, gain_grad = norm_back(mid[...], gain, d_second[...])
@@ -513,8 +547,7 @@
     d_middle[...] = d_mid
     branch = d_mid.astype(BF16)
     put_slabs(packed, sc, fsdp, out_at, dot(att_t[...], branch, 1, 1))
-    for copy in sends[2]:
-        copy.start()
+    send(out_at, down_at - out_at)
     d_mix = jnp.dot(out_w[...], branch, preferred_element_type=F32).astype(BF16)
     for q in range(2):
         for h in range(HEADS):
@@ -528,7 +561,7 @@
                 axis=0,
                 keepdims=True,
             )
-    for copy in sends[0] + sends[1] + sends[2]:
+    for copy in sends:
         copy.wait()
 
 
@@ -575,10 +608,10 @@
             pltpu.SemaphoreType.DMA((len(parts),)),
             pltpu.SemaphoreType.DMA((len(parts),)),
             pltpu.SemaphoreType.DMA((len(parts),)),
-            pltpu.SemaphoreType.DMA((2, 3)),
+            pltpu.SemaphoreType.DMA((24,)),
         ],
         compiler_params=LIMIT,
-        cost_estimate=FREE,
+        cost_estimate=takes(19),
     )(sc, *xs, *cots, mix, gains, *parts, *downs)
 
 
@@ -659,7 +692,7 @@
             pltpu.SemaphoreType.DMA((len(parts),)),
         ],
         compiler_params=LIMIT,
-        cost_estimate=FREE,
+        cost_estimate=takes(0),
     )(sc, *given, *parts)
 
 
@@ -696,7 +729,7 @@
         in_specs=wholes(flat),
         out_specs=wholes(*out_shape),
         compiler_params=LIMIT,
-        cost_estimate=FREE,
+        cost_estimate=takes(2),
     )(flat)
 
 
@@ -710,7 +743,7 @@
         out_specs=wholes(*out_shape),
         scratch_shapes=[pltpu.VMEM((2 * near.shape[0], 128), BF16)],
         compiler_params=LIMIT,
-        cost_estimate=FREE,
+        cost_estimate=takes(3),
     )(x, near, far)
 
 
@@ -742,14 +775,20 @@
         in_specs=wholes(*given),
         out_specs=whole(out_shape),
         compiler_params=LIMIT,
-        cost_estimate=FREE,
+        cost_estimate=takes(0),
     )(*given)
 
 
-def sum_over(total, axes, size):
+def exchange(total, axes, size):
     parts = total.reshape(size, total.shape[0] // size, 128)
-    got = lax.all_to_all(parts, axes, 0, 0, tiled=True)
-    spread = simple_call(spread_kernel, jax.ShapeDtypeStruct(got.shape, BF16), got)
+    return lax.all_to_all(parts, axes, 0, 0, tiled=True)
+
+
+def spread(got):
+    return simple_call(spread_kernel, jax.ShapeDtypeStruct(got.shape, BF16), got)
+
+
+def gather_over(spread, axes):
     return lax.all_to_all(spread, axes, 0, 0, tiled=True).reshape(-1, 128)
 
 
@@ -768,86 +807,71 @@
     out[n:] = (two[...].astype(F32) + two_came[...].astype(F32)).astype(BF16)
 
 
-def first_kernel(x, mine, got, to_y, to_x):
-    i = pl.program_id(0)
-    total = (mine[...].astype(F32) + got[...].astype(F32)).astype(BF16)
-
-    @pl.when(i < 2)
-    def _():
-        to_y[...] = total
-
-    @pl.when(i >= 2)
-    def _():
-        to_x[...] = total
+def first_kernel(x, *refs):
+    mine, got, (to_y, to_x) = refs[:4], refs[4:8], refs[8:]
+    for i in range(4):
+        out = to_y if i < 2 else to_x
+        out[i % 2] = (mine[i][0].astype(F32) + got[i][0].astype(F32)).astype(BF16)
 
 
 def first_sums(x, mine, got):
     n = mine.shape[1] // 4
     block = (1, n, 128)
-
-    def at(i, x):
-        return jnp.where(i == 2, 0, 1), jnp.where(i < 2, i, 3 - x[0]), 0
-
-    shapes = (jax.ShapeDtypeStruct((2, n, 128), BF16),) * 2
+    places = [
+        lambda i, x: (1, 0, 0),
+        lambda i, x: (1, 1, 0),
+        lambda i, x: (0, 3 - x[0], 0),
+        lambda i, x: (1, 3 - x[0], 0),
+    ]
+    out = pl.BlockSpec((2, n, 128), lambda i, x: (0, 0, 0))
     return pl.pallas_call(
         first_kernel,
-        out_shape=shapes,
+        out_shape=(jax.ShapeDtypeStruct((2, n, 128), BF16),) * 2,
         grid_spec=pltpu.PrefetchScalarGridSpec(
             num_scalar_prefetch=1,
-            grid=(4,),
-            in_specs=[pl.BlockSpec(block, at)] * 2,
-            out_specs=[
-                pl.BlockSpec(block, lambda i, x: (jnp.minimum(i, 1), 0, 0)),
-                pl.BlockSpec(block, lambda i, x: (jnp.maximum(i - 2, 0), 0, 0)),
-            ],
+            grid=(1,),
+            in_specs=[pl.BlockSpec(block, at) for at in places] * 2,
+            out_specs=[out, out],
         ),
         compiler_params=LIMIT,
-        cost_estimate=FREE,
-    )(x, mine, got)
-
-
-def second_kernel(x, mine, got, came_y, came_x, *outs):
-    i = pl.program_id(0)
-    total = mine[...].astype(F32) + got[...].astype(F32)
-    came = jnp.where(i < 2, came_y[...].astype(F32), came_x[...].astype(F32))
-    total = (total + came).astype(BF16)[0]
-    for n, out in enumerate(outs):
-
-        @pl.when(i == n)
-        def _(out=out):
-            out[...] = total
+        cost_estimate=takes(0),
+    )(x, *[mine] * 4, *[got] * 4)
+
+
+def second_kernel(x, *refs):
+    mine, got, came, outs = refs[:4], refs[4:8], refs[8:12], refs[12:]
+    for i in range(4):
+        total = mine[i][0].astype(F32) + got[i][0].astype(F32) + came[i][0].astype(F32)
+        outs[i][...] = total.astype(BF16)
 
 
 def second_sums(x, mine, got, came_y, came_x):
     n = mine.shape[1] // 4
     block = (1, n, 128)
-
-    def own(i, x):
-        return (i == 2) * 1, jnp.where(i == 0, 1 - x[0], jnp.where(i == 1, x[0], 2 + x[0])), 0
-
-    def from_y(i, x):
-        return jnp.where(i == 0, 1 - x[0], x[0]), 0, 0
-
-    def from_x(i, x):
-        return jnp.where(i == 3, 0, 1), 0, 0
-
+    own = [
+        lambda i, x: (0, 1 - x[0], 0),
+        lambda i, x: (0, x[0], 0),
+        lambda i, x: (1, 2 + x[0], 0),
+        lambda i, x: (0, 2 + x[0], 0),
+    ]
+    came = [
+        lambda i, x: (1 - x[0], 0, 0),
+        lambda i, x: (x[0], 0, 0),
+        lambda i, x: (1, 0, 0),
+        lambda i, x: (0, 0, 0),
+    ]
     return pl.pallas_call(
         second_kernel,
         out_shape=(jax.ShapeDtypeStruct((n, 128), BF16),) * 4,
         grid_spec=pltpu.PrefetchScalarGridSpec(
             num_scalar_prefetch=1,
-            grid=(4,),
-            in_specs=[
-                pl.BlockSpec(block, own),
-                pl.BlockSpec(block, own),
-                pl.BlockSpec(block, from_y),
-                pl.BlockSpec(block, from_x),
-            ],
+            grid=(1,),
+            in_specs=[pl.BlockSpec(block, at) for at in own + own + came],
             out_specs=[pl.BlockSpec((n, 128), lambda i, x: (0, 0))] * 4,
         ),
         compiler_params=LIMIT,
-        cost_estimate=FREE,
-    )(x, mine, got, came_y, came_x)
+        cost_estimate=takes(0),
+    )(x, *[mine] * 4, *[got] * 4, came_y, came_y, came_x, came_x)
 
 
 def gather_y(own, send, fsdp):
@@ -903,12 +927,10 @@
     order = jnp.stack([core, y, 4 * h] + piece_order(fsdp, core, y)).astype(jnp.int32)
     shard = gate_weight.shape[0]
     join = shard % 16 != 0
-    own_pos = lax.dynamic_slice_in_dim(positions, ci * count, count, 1)
-    pos_rows = jnp.concatenate(
-        [lax.div(own_pos, 64), lax.rem(own_pos, 64), jnp.zeros((14, count), jnp.int32)], axis=0
-    )
-    carried = jnp.concatenate([tokens.reshape(count, width).T, pos_rows.astype(BF16)], axis=0)
-    *pair, query_weight = tie(*pick_home(carried, h), query_weight)
+    x_pair = prepare(2 * count * h + count * x, h, tokens.reshape(count, width).T, positions)
+    *pair, query_weight, norm_first, norm_second = tie(
+        *x_pair, query_weight, norm_first, norm_second
+    )
     xs = send_home(send, pair)
     packed = jnp.concatenate(
         [
@@ -923,6 +945,8 @@
     )
     first_parts = gather_y(packed, send, fsdp)
     first_parts = gather_pieces(first_parts, send, fsdp, core, y, join, 0)
+    cot_t, _ = tie(cotangent.reshape(count, width).T, first_parts[-1])
+    cots = send_home(send, pick_home(cot_t, h))
     pos_f = jnp.concatenate([a[width : width + 2] for a in xs], axis=1).astype(F32)
     pos_f = pos_f[0:1] * 64.0 + pos_f[1:2]
     frequency = jnp.exp(
@@ -936,7 +960,6 @@
     feed_own, down_own, _ = tie(feed_own, down_weight.T, first_parts[-1])
     feed_got = gather_y(feed_own, send, fsdp)
     down_got = gather_y(down_own, send, fsdp)
-    cot_t, _ = tie(cotangent.reshape(count, width).T, kv)
     stages = []
     carried = None
     for s in range(reach + 1):
@@ -947,26 +970,27 @@
         if s < reach:
             kv, *carried = tie(kv, *carried)
     mixed, lse = carried
-    cots = send_home(send, pick_home(cot_t, h))
     feed_parts = gather_pieces(feed_got, send, fsdp, core, y, join, 0)
     down_parts = gather_pieces(down_got, send, fsdp, core, y, join, 1)
     res_a, res_b, d_middle, gz, delta, mine, give, second = feed(
         fsdp, ctx, order, xs, cots, mixed, gains, feed_parts, down_parts
     )
 
-    got = send["core"](give)
     crossed = ys == 2
     x_ref = x.astype(jnp.int32).reshape(1)
-    if crossed:
-        first_y, first_x = first_sums(x_ref, mine, got)
     dq = None
     came = None
     for s in range(reach, -1, -1):
         sc = ids
+        if s == reach - 1:
+            give, dq = tie(give, dq)
+            got = send["core"](give)
         if s == reach - 1 and crossed:
+            first_y, first_x = first_sums(x_ref, mine, got)
             sc, first_y, first_x = tie(sc, first_y, first_x)
             came_y, came_x = send["shift"][1](first_y), send["across"](first_x)
         if s == 0 and crossed:
+            came_y, came_x, dq = tie(came_y, came_x, dq)
             give_one, keep_one, give_two, keep_two = second_sums(x_ref, mine, got, came_y, came_x)
             sc, give_one, give_two = tie(sc, give_one, give_two)
             came_one, came_two = send["across"](give_one), send["shift"][1](give_two)
@@ -978,21 +1002,16 @@
         )
         twin = tuple(send["core"](o) for o in other)
         if s > 0:
-            if s < reach:
+            if s == reach - 1:
+                *twin, came, dq, res_a, res_b = tie(*twin, came, dq, *result)
+            elif s < reach:
                 *twin, came, dq = tie(*twin, came, dq)
             given = (own, *twin) if came is None else (own, *twin, came)
             came = simple_call(came_kernel, jax.ShapeDtypeStruct(own.shape, BF16), *given)
+            if s == reach:
+                came, res_a, res_b = tie(came, res_a, res_b)
+                result = send_back(send, res_a, res_b)
     dkv = (own, *twin) if came is None else (own, *twin, came)
-    result = send_back(send, res_a, res_b)
-    if crossed:
-        *result, came_one, came_two, dq = tie(*result, came_one, came_two, dq)
-    else:
-        *result, dq = tie(*result, dq)
-    tok_a, tok_b, mine_front, give_front = last(
-        fsdp, ctx, order, xs, cos, sin, normed_t, gains, second, d_middle, dq, dkv, first_parts
-    )
-    got_front = send["core"](give_front)
-    front = sum_y(mine_front, got_front, send)
     if crossed:
         late = simple_call(
             halves_kernel,
@@ -1002,11 +1021,21 @@
             keep_two,
             came_two,
         )
-        late = sum_over(late, ("h",), hs)
+        late = exchange(late, ("h",), hs)
+    else:
+        late = exchange(sum_y(mine, got, send), CTX, ctx)
+    late, dq = tie(spread(late), dq)
+    late = gather_over(late, ("h",) if crossed else CTX)
+    tok_a, tok_b, mine_front, give_front = last(
+        fsdp, ctx, order, xs, cos, sin, normed_t, gains, second, d_middle, dq, dkv, first_parts
+    )
+    got_front = send["core"](give_front)
+    front = sum_y(mine_front, got_front, send)
+    front, late, tok_a, tok_b = tie(front, late, tok_a, tok_b)
+    front = spread(exchange(front, CTX, ctx))
+    if crossed:
         late_far = send["across"](late)
-    else:
-        late = sum_over(sum_y(mine, got, send), CTX, ctx)
-    front = sum_over(front, CTX, ctx)
+    front = gather_over(front, CTX)
     tokens_grad = send_back(send, tok_a, tok_b)
 
     ff = gate_weight.shape[1]
@@ -1033,7 +1062,7 @@
         ],
     )
     return (
-        low_high(*result, h).T[None],
+        low_high(res_a, res_b, h).T[None],
         low_high(*tokens_grad, h).T[None],
         ends[:, 0],
         query_grad,

time: 293 us -> 280 us (0.956)
  local copies, waits for them, and re-layouts: 14 us -> 5.48 us
  starting transfers between devices: 93.3 us -> 87 us
  other arithmetic: 8.5 us -> 11.5 us
    ppermute x38, waiting for transfers between devices: 37.1 us -> 61.3 us  [along(): return lambda a: lax.ppermute(a, AXES, pairs)]
    all_to_all x4, waiting for transfers between devices: 44.1 us -> 20.5 us  [the longest x2 10.3 us: gather_over(): return lax.all_to_all(spread, axes, 0, 0, tiled=True).reshape(-1, 128)]
    ppermute x38, starting transfers between devices: 77 us -> 67.4 us  [along(): return lambda a: lax.ppermute(a, AXES, pairs)]
    unnamed x88 -> x36, local copies, waits for them, and re-layouts: 9.89 us -> 1.87 us
    all_to_all x4, starting transfers between devices: 16.3 us -> 19.6 us  [the longest x2 11 us: exchange(): return lax.all_to_all(parts, axes, 0, 0, tiled=True)]
  transfers between devices with their start and end apart: 42 -> 42, of which waited for: 16 -> 20; matrix products, arithmetic and copies ran while one was open for 3% -> 5% of each run, Pallas kernels for 20% -> 18%
where the time goes in v1:
time: 280 us; the launch traced here: 278 us
  Pallas kernels  91.5 us (33%)
  starting transfers between devices  87 us (31%)
  waiting for transfers between devices  81.8 us (29%)
  other arithmetic  11.5 us (4%)
  local copies, waits for them, and re-layouts  5.48 us (2%)
    ppermute x38, starting transfers between devices, along(): return lambda a: lax.ppermute(a, AXES, pairs)  67.4 us
    ppermute x38, waiting for transfers between devices, along(): return lambda a: lax.ppermute(a, AXES, pairs)  61.3 us
    pallas_call x3, Pallas kernels, attend_backward(): pl.pallas_call(functools.partial(backward_kernel, stage, first, own_type)...  19.6 us
    pallas_call x1, Pallas kernels, feed(): pl.pallas_call(functools.partial(feed_kernel, fsdp, len(parts), ff // 4 i...  18.9 us
    pallas_call x3, Pallas kernels, attend_forward(): pl.pallas_call(functools.partial(forward_kernel, stage, last), out_shape=...  16.9 us
    all_to_all x2, starting transfers between devices, exchange(): return lax.all_to_all(parts, axes, 0, 0, tiled=True)  11 us
    pallas_call x5, Pallas kernels, simple_call(): pl.pallas_call(kernel, out_shape=out_shape, grid=(1,), in_specs=wholes(*g...  10.4 us
    all_to_all x2, waiting for transfers between devices, gather_over(): return lax.all_to_all(spread, axes, 0, 0, tiled=True).reshape(-1, 128)  10.3 us
  transfers between devices with their start and end apart: 42, of which 20 were waited for; matrix products, arithmetic and copies ran while one was open for 5% of the time, Pallas kernels for 18%

profile of v1, /device:TPU:0, one launch (start us, length us, event | category | flops | bytes accessed | tf_op | source)
XLA Modules:
  0.0 278.3 jit_solution(12812007345130327136)
XLA Ops:
  1.2 2.0 shard_map.203
  3.2 1.6 collective-permute-start
  4.8 7.3 %collective-permute-start.1 = (bf16[592,256]{1,0:T(8,128)(2,1)}, bf16[592,256]{1,0:T(8,128)(2,1)S(1)}, u32[]{:S(2)}, u32[]{:S(2)}) collective-permute-start(bf16[592,256]{1,0:T(8,128)(2,1)} %get-tuple-element.114), channel_id=1, source_target_pairs={{0,6},{1,14},{2,8},{3,0},{4,4},{5,12},{6,10},{7,2},{8,7},{9,15},{1... | collective-permute-start | bytes 909320 | tf_op jit(solution)/shard_map/ppermute | solution.py:40
  13.4 1.6 collective-permute-start.2
  16.8 6.2 %collective-permute-done.2.refs_6_.refs_15_ = bf16[144,1024]{1,0:T(8,128)(2,1)S(1)} collective-permute-done((bf16[144,1024]{1,0:T(8,128)(2,1)S(1)}, bf16[144,1024]{1,0:T(8,128)(2,1)S(1)}, u32[]{:S(2)}, u32[]{:S(2)}) %collective-permute-start.2) | collective-permute-done | bytes 294944 | tf_op jit(solution)/shard_map/ppermute | solution.py:40
  25.3 5.1 %shard_map.204 = (bf16[2,3,128,768]{3,2,1,0:T(8,128)(2,1)}, bf16[2,3,256,128]{3,2,1,0:T(8,128)(2,1)}, bf16[576,512]{1,0:T(8,128)(2,1)}, bf16[576,128]{1,0:T(8,12...) custom-call(s32[7]{0:T(128)} %stack.40.refs_0_, bf16[592,256]{1,0:T(8,128)(2,1)} %copy-done.4, bf16[592,256]{1,0:T(8,128)(2,1)} %copy-done.5, ...), custom_call_target="tpu_custom_call" | custom-call | flops 5750000128 | tf_op jit(solution)/shard_map/pallas_call | solution.py:404
  30.7 2.2 pad_maximum_fusion.refs_7_
  32.9 5.2 %collective-permute-start.7 = (bf16[2,3,256,128]{3,2,1,0:T(8,128)(2,1)}, bf16[2,3,256,128]{3,2,1,0:T(8,128)(2,1)}, u32[]{:S(2)}, u32[]{:S(2)}) collective-permute-start(bf16[2,3,256,128]{3,2,1,0:T(8,128)(2,1)} %get-tuple-element.122.refs_3_.refs_6_), channel_id=1, source_target_pairs={{0,2},{1,3},{2,4},{3,5},{4,6},{5,7},{8,10},{9,11},{10,12},{11,13},... | collective-permute-start | bytes 1179656 | tf_op jit(solution)/shard_map/ppermute | solution.py:40
  38.2 1.5 collective-permute-start.12
  39.7 10.4 %shard_map.205 = (f32[2,3,1,768]{3,2,1,0:T(1,128)}, f32[2,3,1,768]{3,2,1,0:T(1,128)}, f32[2,3,64,768]{3,2,1,0:T(8,128)}) custom-call(s32[8]{0:T(128)} %get-tuple-element.186.refs_0_, s32[2,1,256]{2,1,0:T(1,128)} %get-tuple-element.120.refs_1_, bf16[2,3,128,768]{3,2,1,0:T(8,128)(2,1)} %get-tuple-element.121.refs_2_, ...), custom_call_target="tpu_custom_call" | custom-call | flops 11500000256 | tf_op jit(solution)/shard_map/pallas_call | solution.py:248
  50.6 1.9 broadcast_select_fusion.4
  52.5 2.9 %collective-permute-start.6 = (bf16[576,256]{1,0:T(8,128)(2,1)}, bf16[576,256]{1,0:T(8,128)(2,1)}, u32[]{:S(2)}, u32[]{:S(2)}) collective-permute-start(bf16[576,256]{1,0:T(8,128)(2,1)} %get-tuple-element.217), channel_id=1, source_target_pairs={{0,6},{1,14},{2,8},{3,0},{4,4},{5,12},{6,10},{7,2},{8,7},{9,15},{1... | collective-permute-start | bytes 884744 | tf_op jit(solution)/shard_map/ppermute | solution.py:40
  55.5 1.6 collective-permute-start.15
  57.1 2.3 collective-permute-start.9
  59.4 5.6 %collective-permute-done.12.refs_8_ = bf16[144,3648]{1,0:T(8,128)(2,1)} collective-permute-done((bf16[144,3648]{1,0:T(8,128)(2,1)}, bf16[144,3648]{1,0:T(8,128)(2,1)}, u32[]{:S(2)}, u32[]{:S(2)}) %collective-permute-start.12) | collective-permute-done | bytes 1050656 | tf_op jit(solution)/shard_map/ppermute | solution.py:40
  64.9 3.2 %shard_map.206 = (f32[2,3,1,768]{3,2,1,0:T(1,128)}, f32[2,3,1,768]{3,2,1,0:T(1,128)}, f32[2,3,64,768]{3,2,1,0:T(8,128)}) custom-call(s32[8]{0:T(128)} %get-tuple-element.186.refs_0_, s32[2,1,256]{2,1,0:T(1,128)} %get-tuple-element.120.refs_1_, ...), custom_call_target="tpu_custom_call", output_to_operand_aliasing={{0}: (5, {}), {1}: (6, {}), {2}: (7, {})} | custom-call | flops 13799999488 | tf_op jit(solution)/shard_map/pallas_call | solution.py:248
  68.2 2.4 collective-permute-done.9.refs_3_.refs_6_
  71.1 2.6 collective-permute-done.15.refs_12_
  73.7 3.7 %collective-permute-start.5 = (bf16[576,256]{1,0:T(8,128)(2,1)}, bf16[576,256]{1,0:T(8,128)(2,1)}, u32[]{:S(2)}, u32[]{:S(2)}) collective-permute-start(bf16[576,256]{1,0:T(8,128)(2,1)} %get-tuple-element.218), channel_id=1, source_target_pairs={{0,0},{1,8},{2,14},{3,6},{4,2},{5,10},{6,12},{7,4},{8,1},{9,9},{10... | collective-permute-start | bytes 884744 | tf_op jit(solution)/shard_map/ppermute | solution.py:40
  77.4 3.3 %shard_map.207 = (bf16[2,3,64,768]{3,2,1,0:T(8,128)(2,1)}, f32[2,3,1,768]{3,2,1,0:T(1,128)}) custom-call(s32[8]{0:T(128)} %get-tuple-element.186.refs_0_, s32[2,1,256]{2,1,0:T(1,128)} %get-tuple-element.120.refs_1_, bf16[2,3,128,768]{3,2,1,0:T(8,128)(2,1)} %get-tuple-element.121.refs_2_, bf16[2,3,256,128]{3,2,1,0:T(8,128)(2,1)} %collective-permute-done.9.refs_3_.refs_6_, ...), custom_call_target="tpu_custom_call" | custom-call | flops 3449999872 | tf_op jit(solution)/shard_map/pallas_call | solution.py:248
  80.7 18.9 %shard_map.208 = (bf16[576,256]{1,0:T(8,128)(2,1)}, bf16[576,256]{1,0:T(8,128)(2,1)}, f32[576,512]{1,0:T(8,128)}, bf16[2,3,128,768]{3,2,1,0:T(8,128)(2,1)}, f32[...) custom-call(s32[7]{0:T(128)} %stack.40.refs_0_, ...), custom_call_target="tpu_custom_call" | custom-call | flops 21849999360 | tf_op jit(solution)/shard_map/pallas_call | solution.py:589
  99.6 3.7 %shard_map.209 = (f32[2,3,64,768]{3,2,1,0:T(8,128)}, bf16[2,3,256,128]{3,2,1,0:T(8,128)(2,1)}, bf16[3,256,128]{2,1,0:T(8,128)(2,1)}, bf16[3,256,128]{2,1,0:T(8,128)(2,1)}) custom-call(s32[8]{0:T(128)} %get-tuple-element.186.refs_0_, s32[2,1,256]{2,1,0:T(1,128)} %get-tuple-element.120.refs_1_, bf16[2,3,128,768]{3,2,1,0:T(8,128)(2,1)} %get-tuple-element.121.refs_2_, ...), custom_call_target="tpu_custom_call" | custom-call | flops 4600000000 | tf_op jit(solution)/shard_map/pallas_call | solution.py:274
  103.3 1.8 collective-permute-start.18
  105.7 5.3 %collective-permute-done.19.twin_a = bf16[3,256,128]{2,1,0:T(8,128)(2,1)S(1)} collective-permute-done((bf16[3,256,128]{2,1,0:T(8,128)(2,1)}, bf16[3,256,128]{2,1,0:T(8,128)(2,1)S(1)}, u32[]{:S(2)}, u32[]{:S(2)}) %collective-permute-start.19) | collective-permute-done | bytes 196640 | tf_op jit(solution)/shard_map/ppermute | solution.py:40
  111.7 2.0 shard_map.211
  113.7 3.7 %collective-permute-start.24 = (bf16[576,256]{1,0:T(8,128)(2,1)}, bf16[576,256]{1,0:T(8,128)(2,1)}, u32[]{:S(2)}, u32[]{:S(2)}) collective-permute-start(bf16[576,256]{1,0:T(8,128)(2,1)} %get-tuple-element.163), channel_id=1, source_target_pairs={{0,0},{8,1},{14,2},{6,3},{2,4},{10,5},{12,6},{4,7},{1,8},{9,9},{15... | collective-permute-start | bytes 884744 | tf_op jit(solution)/shard_map/ppermute | solution.py:40
  117.4 12.1 %collective-permute-start.25 = (bf16[576,256]{1,0:T(8,128)(2,1)}, bf16[576,256]{1,0:T(8,128)(2,1)}, u32[]{:S(2)}, u32[]{:S(2)}) collective-permute-start(bf16[576,256]{1,0:T(8,128)(2,1)} %get-tuple-element.164), channel_id=1, source_target_pairs={{6,0},{14,1},{8,2},{0,3},{4,4},{12,5},{10,6},{2,7},{7,8},{15,9},{9... | collective-permute-start | bytes 884744 | tf_op jit(solution)/shard_map/ppermute | solution.py:40
  129.5 3.1 %shard_map.210 = (bf16[2,1504,128]{2,1,0:T(8,128)(2,1)}, bf16[2,1504,128]{2,1,0:T(8,128)(2,1)}) custom-call(s32[1]{0:T(128)} %bitcast.12.x.sc, bf16[2,6016,128]{2,1,0:T(8,128)(2,1)} %get-tuple-element.141.refs_0_.refs_1_.refs_2_.refs_3_, bf16[2,6016,128]{2,1,0:T(8,128)(2,1)} %get-tuple-element.141.refs_0_.refs_1_.refs_2_.refs_3_, ...), custom_call_target="tpu_custom_call" | custom-call | tf_op jit(solution)/shard_map/pallas_call | solution.py:827
  132.6 1.3 collective-permute-start.23
  133.9 4.9 %collective-permute-start.26 = (bf16[2,1504,128]{2,1,0:T(8,128)(2,1)}, bf16[2,1504,128]{2,1,0:T(8,128)(2,1)}, u32[]{:S(2)}, u32[]{:S(2)}) collective-permute-start(bf16[2,1504,128]{2,1,0:T(8,128)(2,1)} %get-tuple-element.170), channel_id=1, source_target_pairs={{0,16},{1,17},{2,18},{3,19},{4,20},{5,21},{6,22},{7,23},{8,24},{9,... | collective-permute-start | bytes 2310152 | tf_op jit(solution)/shard_map/ppermute | solution.py:40
  138.9 3.9 %shard_map.212 = (f32[2,3,64,768]{3,2,1,0:T(8,128)}, bf16[2,3,256,128]{3,2,1,0:T(8,128)(2,1)}, bf16[3,256,128]{2,1,0:T(8,128)(2,1)}, bf16[3,256,128]{2,1,0:T(8,128)(2,1)}) custom-call(s32[8]{0:T(128)} %get-tuple-element.186.refs_0_, s32[2,1,256]{2,1,0:T(1,128)} %get-tuple-element.120.refs_1_, ...), custom_call_target="tpu_custom_call", output_to_operand_aliasing={{0}: (8, {})} | custom-call | flops 16099999744 | tf_op jit(solution)/shard_map/pallas_call | solution.py:274
  142.9 1.9 collective-permute-done.25
  144.8 1.8 collective-permute-done.22.twin_b
  146.6 6.0 %collective-permute-done.23.refs_0_ = bf16[2,3,256,128]{3,2,1,0:T(8,128)(2,1)} collective-permute-done((bf16[2,3,256,128]{3,2,1,0:T(8,128)(2,1)}, bf16[2,3,256,128]{3,2,1,0:T(8,128)(2,1)}, u32[]{:S(2)}, u32[]{:S(2)}) %collective-permute-start.23) | collective-permute-done | bytes 393248 | tf_op jit(solution)/shard_map/ppermute | solution.py:40
  152.6 3.5 %collective-permute-done.26.refs_8_.refs_9_ = bf16[2,1504,128]{2,1,0:T(8,128)(2,1)} collective-permute-done((bf16[2,1504,128]{2,1,0:T(8,128)(2,1)}, bf16[2,1504,128]{2,1,0:T(8,128)(2,1)}, u32[]{:S(2)}, u32[]{:S(2)}) %collective-permute-start.26) | collective-permute-done | bytes 770080 | tf_op jit(solution)/shard_map/ppermute | solution.py:40
  156.0 1.5 collective-permute-done.27.refs_10_.refs_11_
  157.5 3.6 %shard_map.213 = (bf16[1504,128]{1,0:T(8,128)(2,1)}, bf16[1504,128]{1,0:T(8,128)(2,1)}, bf16[1504,128]{1,0:T(8,128)(2,1)}, bf16[1504,128]{1,0:T(8,128)(2,1)}) custom-call(s32[1]{0:T(128)} %bitcast.12.x.sc, bf16[2,6016,128]{2,1,0:T(8,128)(2,1)} %get-tuple-element.141.refs_0_.refs_1_.refs_2_.refs_3_, ...), custom_call_target="tpu_custom_call" | custom-call | tf_op jit(solution)/shard_map/pallas_call | solution.py:863
  161.1 2.3 collective-permute-start.28
  164.3 2.2 shard_map.216
  167.8 4.4 %collective-permute-done.28.one_came = bf16[1504,128]{1,0:T(8,128)(2,1)} collective-permute-done((bf16[1504,128]{1,0:T(8,128)(2,1)}, bf16[1504,128]{1,0:T(8,128)(2,1)}, u32[]{:S(2)}, u32[]{:S(2)}) %collective-permute-start.28) | collective-permute-done | bytes 385056 | tf_op jit(solution)/shard_map/ppermute | solution.py:40
  172.2 1.5 collective-permute-done.29.two_came
  173.6 2.4 shard_map.214
  176.0 5.1 %all-to-all-start = ((bf16[4,752,128]{2,1,0:T(8,128)(2,1)}), bf16[4,752,128]{2,1,0:T(8,128)(2,1)}, u32[]{:S(2)}, u32[]{:S(2)}) async-start(bf16[4,752,128]{2,1,0:T(8,128)(2,1)} %bitcast.37), calls=%async_computation | async-start | bytes 1540096 | tf_op jit(solution)/shard_map/all_to_all | solution.py:784
  181.1 12.0 %shard_map.217 = (f32[2,3,64,768]{3,2,1,0:T(8,128)}, f32[2,3,256,128]{3,2,1,0:T(8,128)}, bf16[3,256,128]{2,1,0:T(8,128)(2,1)}, bf16[3,256,128]{2,1,0:T(8,128)(2,1)}) custom-call(s32[8]{0:T(128)} %get-tuple-element.186.refs_0_, s32[2,1,256]{2,1,0:T(1,128)} %get-tuple-element.120.refs_1_, ...), custom_call_target="tpu_custom_call", output_to_operand_aliasing={{0}: (8, {})} | custom-call | flops 13799999488 | tf_op jit(solution)/shard_map/pallas_call | solution.py:274
  193.6 6.8 %all-to-all-done.got = bf16[4,752,128]{2,1,0:T(8,128)(2,1)} async-done(((bf16[4,752,128]{2,1,0:T(8,128)(2,1)}), bf16[4,752,128]{2,1,0:T(8,128)(2,1)}, u32[]{:S(2)}, u32[]{:S(2)}) %all-to-all-start) | async-done | bytes 770080 | tf_op jit(solution)/shard_map/all_to_all | solution.py:784
  200.3 2.1 shard_map.215
  203.1 6.9 %shard_map.218 = (bf16[576,256]{1,0:T(8,128)(2,1)}, bf16[576,256]{1,0:T(8,128)(2,1)}, bf16[2,1152,128]{2,1,0:T(8,128)(2,1)}, bf16[2,1152,128]{2,1,0:T(8,128)(2,1)}) custom-call(s32[7]{0:T(128)} %stack.40.refs_0_, bf16[592,256]{1,0:T(8,128)(2,1)} %copy-done.4, bf16[592,256]{1,0:T(8,128)(2,1)} %copy-done.5, f32[32,512]{1,0:T(8,128)} %get-tuple-element.220.refs_3_, ...), custom_call_target="tpu_custom_call" | custom-call | tf_op jit(solution)/shard_map/pallas_call | solution.py:682
  210.1 4.3 %all-to-all-start.1 = ((bf16[4,752,128]{2,1,0:T(8,128)(2,1)}), bf16[4,752,128]{2,1,0:T(8,128)(2,1)}, u32[]{:S(2)}, u32[]{:S(2)}) async-start(bf16[4,752,128]{2,1,0:T(8,128)(2,1)} %shard_map.215), calls=%async_computation.1 | async-start | bytes 1540096 | tf_op jit(solution)/shard_map/all_to_all | solution.py:792
  214.6 1.5 collective-permute-start.34
  216.0 7.8 %collective-permute-done.34 = bf16[1152,128]{1,0:T(8,128)(2,1)S(1)} collective-permute-done((bf16[1152,128]{1,0:T(8,128)(2,1)S(1)}, bf16[1152,128]{1,0:T(8,128)(2,1)S(1)}, u32[]{:S(2)}, u32[]{:S(2)}) %collective-permute-start.34) | collective-permute-done | bytes 294944 | tf_op jit(solution)/shard_map/ppermute | solution.py:40
  224.7 10.3 %all-to-all-done.1 = bf16[4,752,128]{2,1,0:T(8,128)(2,1)} async-done(((bf16[4,752,128]{2,1,0:T(8,128)(2,1)}), bf16[4,752,128]{2,1,0:T(8,128)(2,1)}, u32[]{:S(2)}, u32[]{:S(2)}) %all-to-all-start.1) | async-done | bytes 770080 | tf_op jit(solution)/shard_map/all_to_all | solution.py:792
  235.7 3.3 %collective-permute-start.36 = (bf16[576,256]{1,0:T(8,128)(2,1)S(1)}, bf16[576,256]{1,0:T(8,128)(2,1)S(1)}, u32[]{:S(2)}, u32[]{:S(2)}) collective-permute-start(bf16[576,256]{1,0:T(8,128)(2,1)S(1)} %copy-done.16), channel_id=1, source_target_pairs={{6,0},{14,1},{8,2},{0,3},{4,4},{12,5},{10,6},{2,7},{7,8},{15,9},{9... | collective-permute-start | bytes 884744 | tf_op jit(solution)/shard_map/ppermute | solution.py:40
  239.0 6.0 %all-to-all-start.2 = ((bf16[8,144,128]{2,1,0:T(8,128)(2,1)}), bf16[8,144,128]{2,1,0:T(8,128)(2,1)}, u32[]{:S(2)}, u32[]{:S(2)}) async-start(bf16[8,144,128]{2,1,0:T(8,128)(2,1)} %bitcast.24), calls=%async_computation.2 | async-start | bytes 589824 | tf_op jit(solution)/shard_map/all_to_all | solution.py:784
  245.0 2.0 collective-permute-start.37
  247.1 5.4 %collective-permute-done.36 = bf16[576,256]{1,0:T(8,128)(2,1)S(1)} collective-permute-done((bf16[576,256]{1,0:T(8,128)(2,1)S(1)}, bf16[576,256]{1,0:T(8,128)(2,1)S(1)}, u32[]{:S(2)}, u32[]{:S(2)}) %collective-permute-start.36) | collective-permute-done | bytes 294944 | tf_op jit(solution)/shard_map/ppermute | solution.py:40
  252.5 2.1 broadcast_select_fusion.1
  254.6 3.4 %all-to-all-done.2.got = bf16[8,144,128]{2,1,0:T(8,128)(2,1)} async-done(((bf16[8,144,128]{2,1,0:T(8,128)(2,1)}), bf16[8,144,128]{2,1,0:T(8,128)(2,1)}, u32[]{:S(2)}, u32[]{:S(2)}) %all-to-all-start.2) | async-done | bytes 294944 | tf_op jit(solution)/shard_map/all_to_all | solution.py:784
  258.0 1.7 shard_map.219
  259.7 4.2 %all-to-all-start.3 = ((bf16[8,144,128]{2,1,0:T(8,128)(2,1)}), bf16[8,144,128]{2,1,0:T(8,128)(2,1)}, u32[]{:S(2)}, u32[]{:S(2)}) async-start(bf16[8,144,128]{2,1,0:T(8,128)(2,1)} %shard_map.219), calls=%async_computation.3 | async-start | bytes 589824 | tf_op jit(solution)/shard_map/all_to_all | solution.py:792
  263.9 1.9 maximum_bitcast_fusion.1
  266.7 4.9 %collective-permute-done.37.far = bf16[3008,128]{1,0:T(8,128)(2,1)} collective-permute-done((bf16[3008,128]{1,0:T(8,128)(2,1)}, bf16[3008,128]{1,0:T(8,128)(2,1)}, u32[]{:S(2)}, u32[]{:S(2)}) %collective-permute-start.37) | collective-permute-done | bytes 770080 | tf_op jit(solution)/shard_map/ppermute | solution.py:40
  271.6 3.2 %shard_map.221 = (f32[144,1536]{1,0:T(8,128)}, f32[144,1536]{1,0:T(8,128)}, f32[144,576]{1,0:T(8,128)}, f32[576,384]{1,0:T(8,128)}) custom-call(s32[1]{0:T(128)} %bitcast.12.x.sc, bf16[3008,128]{1,0:T(8,128)(2,1)} %bitcast.21.near, bf16[3008,128]{1,0:T(8,128)(2,1)} %collective-permute-done.37.far), custom_call_target="tpu_custom_call" | custom-call | flops 3449999872 | tf_op jit(solution)/shard_map/pallas_call | solution.py:738
  274.7 1.8 shard_map.220
  276.6 1.7 slice_reduce_fusion
  (95 shorter events, 14.4 us)
Async XLA Ops:
  1.2 10.9 %copy-start.14 = (bf16[144]{0:T(256)(128)(2,1)S(1)}, bf16[144]{0:T(256)(128)(2,1)}, u32[]{:S(2)}) copy-start(bf16[144]{0:T(256)(128)(2,1)} %param.16) | copy-start | bytes 868
  1.2 11.0 %copy-start.15 = (bf16[144]{0:T(256)(128)(2,1)S(1)}, bf16[144]{0:T(256)(128)(2,1)}, u32[]{:S(2)}) copy-start(bf16[144]{0:T(256)(128)(2,1)} %param.21) | copy-start | bytes 868
  1.2 11.1 %copy-start.12 = (bf16[144,576]{1,0:T(8,128)(2,1)S(1)}, bf16[144,576]{1,0:T(8,128)(2,1)}, u32[]{:S(2)}) copy-start(bf16[144,576]{1,0:T(8,128)(2,1)} %param.17) | copy-start | bytes 497668
  3.2 20.0 %collective-permute-start = (bf16[592,256]{1,0:T(8,128)(2,1)}, bf16[592,256]{1,0:T(8,128)(2,1)S(1)}, u32[]{:S(2)}, u32[]{:S(2)}) collective-permute-start(bf16[592,256]{1,0:T(8,128)(2,1)} %get-tuple-element.113), channel_id=1, source_target_pairs={{0,0},{1,8},{2,14},{3,6},{4,2},{5,10},{6,12},{7,4},{8,1},{9,9},{10... | collective-permute-start | bytes 909320 | tf_op jit(solution)/shard_map/ppermute | solution.py:40
  4.8 18.4 %collective-permute-start.1 = (bf16[592,256]{1,0:T(8,128)(2,1)}, bf16[592,256]{1,0:T(8,128)(2,1)S(1)}, u32[]{:S(2)}, u32[]{:S(2)}) collective-permute-start(bf16[592,256]{1,0:T(8,128)(2,1)} %get-tuple-element.114), channel_id=1, source_target_pairs={{0,6},{1,14},{2,8},{3,0},{4,4},{5,12},{6,10},{7,2},{8,7},{9,15},{1... | collective-permute-start | bytes 909320 | tf_op jit(solution)/shard_map/ppermute | solution.py:40
  13.4 1.6 copy-start
  13.4 9.5 %collective-permute-start.2 = (bf16[144,1024]{1,0:T(8,128)(2,1)S(1)}, bf16[144,1024]{1,0:T(8,128)(2,1)S(1)}, u32[]{:S(2)}, u32[]{:S(2)}) collective-permute-start(bf16[144,1024]{1,0:T(8,128)(2,1)S(1)} %concatenate.16.refs_5_.refs_14_), channel_id=1, source_target_pairs={{0,16},{1,17},{2,18},{3,19},{4,20},{5,21},{6,22},{7,23},{8,24},{9,... | collective-permute-start | bytes 884744 | tf_op jit(solution)/shard_map/ppermute | solution.py:40
  15.0 9.2 %collective-permute-start.3 = (bf16[144,1024]{1,0:T(8,128)(2,1)S(1)}, bf16[144,1024]{1,0:T(8,128)(2,1)S(1)}, u32[]{:S(2)}, u32[]{:S(2)}) collective-permute-start(bf16[144,1024]{1,0:T(8,128)(2,1)S(1)} %concatenate.16.refs_5_.refs_14_), channel_id=1, source_target_pairs={{0,8},{1,9},{2,10},{3,11},{4,12},{5,13},{6,14},{7,15},{8,0},{9,1},... | collective-permute-start | bytes 884744 | tf_op jit(solution)/shard_map/ppermute | solution.py:40
  23.0 1.6 copy-start.6
  23.0 1.6 collective-permute-start.4
  23.2 1.0 copy-start.4
  23.2 1.3 copy-start.5
  24.2 0.7 copy-start.7
  24.6 0.7 copy-start.8
  25.3 5.4 %copy-start.13 = (bf16[144,576]{1,0:T(8,128)(2,1)S(1)}, bf16[144,576]{1,0:T(8,128)(2,1)}, u32[]{:S(2)}) copy-start(bf16[144,576]{1,0:T(8,128)(2,1)} %param.20) | copy-start | bytes 497668
  30.4 9.3 %collective-permute-start.8 = (bf16[2,3,256,128]{3,2,1,0:T(8,128)(2,1)}, bf16[2,3,256,128]{3,2,1,0:T(8,128)(2,1)}, u32[]{:S(2)}, u32[]{:S(2)}) collective-permute-start(bf16[2,3,256,128]{3,2,1,0:T(8,128)(2,1)} %get-tuple-element.122.refs_3_.refs_6_), channel_id=1, source_target_pairs={{0,8},{1,9},{2,10},{3,11},{4,12},{5,13},{6,14},{7,15},{8,0},{9,1},... | collective-permute-start | bytes 1179656 | tf_op jit(solution)/shard_map/ppermute | solution.py:40
  32.9 17.2 %collective-permute-start.7 = (bf16[2,3,256,128]{3,2,1,0:T(8,128)(2,1)}, bf16[2,3,256,128]{3,2,1,0:T(8,128)(2,1)}, u32[]{:S(2)}, u32[]{:S(2)}) collective-permute-start(bf16[2,3,256,128]{3,2,1,0:T(8,128)(2,1)} %get-tuple-element.122.refs_3_.refs_6_), channel_id=1, source_target_pairs={{0,2},{1,3},{2,4},{3,5},{4,6},{5,7},{8,10},{9,11},{10,12},{11,13},... | collective-permute-start | bytes 1179656 | tf_op jit(solution)/shard_map/ppermute | solution.py:40
  38.2 26.8 %collective-permute-start.12 = (bf16[144,3648]{1,0:T(8,128)(2,1)}, bf16[144,3648]{1,0:T(8,128)(2,1)}, u32[]{:S(2)}, u32[]{:S(2)}) collective-permute-start(bf16[144,3648]{1,0:T(8,128)(2,1)} %pad_maximum_fusion.refs_7_), channel_id=1, source_target_pairs={{0,16},{1,17},{2,18},{3,19},{4,20},{5,21},{6,22},{7,23},{8,24},{9,... | collective-permute-start | bytes 3151880 | tf_op jit(solution)/shard_map/ppermute | solution.py:40
  50.1 6.9 %collective-permute-start.10 = (bf16[2,3,256,128]{3,2,1,0:T(8,128)(2,1)}, bf16[2,3,256,128]{3,2,1,0:T(8,128)(2,1)}, u32[]{:S(2)}, u32[]{:S(2)}) collective-permute-start(bf16[2,3,256,128]{3,2,1,0:T(8,128)(2,1)} %collective-permute-done.7.refs_3_.refs_6_), channel_id=1, source_target_pairs={{0,8},{1,9},{2,10},{3,11},{4,12},{5,13},{6,14},{7,15},{8,0},{9,1},... | collective-permute-start | bytes 1179656 | tf_op jit(solution)/shard_map/ppermute | solution.py:40
  50.1 30.6 %collective-permute-start.13 = (bf16[144,3648]{1,0:T(8,128)(2,1)}, bf16[144,3648]{1,0:T(8,128)(2,1)}, u32[]{:S(2)}, u32[]{:S(2)}) collective-permute-start(bf16[144,3648]{1,0:T(8,128)(2,1)} %pad_maximum_fusion.refs_7_), channel_id=1, source_target_pairs={{0,8},{1,9},{2,10},{3,11},{4,12},{5,13},{6,14},{7,15},{8,0},{9,1},... | collective-permute-start | bytes 3151880 | tf_op jit(solution)/shard_map/ppermute | solution.py:40
  52.5 18.1 %collective-permute-start.6 = (bf16[576,256]{1,0:T(8,128)(2,1)}, bf16[576,256]{1,0:T(8,128)(2,1)}, u32[]{:S(2)}, u32[]{:S(2)}) collective-permute-start(bf16[576,256]{1,0:T(8,128)(2,1)} %get-tuple-element.217), channel_id=1, source_target_pairs={{0,6},{1,14},{2,8},{3,0},{4,4},{5,12},{6,10},{7,2},{8,7},{9,15},{1... | collective-permute-start | bytes 884744 | tf_op jit(solution)/shard_map/ppermute | solution.py:40
  55.5 18.2 %collective-permute-start.15 = (bf16[576,384]{1,0:T(8,128)(2,1)}, bf16[576,384]{1,0:T(8,128)(2,1)}, u32[]{:S(2)}, u32[]{:S(2)}) collective-permute-start(bf16[576,384]{1,0:T(8,128)(2,1)} %bitcast.15.refs_11_), channel_id=1, source_target_pairs={{0,16},{1,17},{2,18},{3,19},{4,20},{5,21},{6,22},{7,23},{8,24},{9,... | collective-permute-start | bytes 1327112 | tf_op jit(solution)/shard_map/ppermute | solution.py:40
  57.1 13.5 %collective-permute-start.9 = (bf16[2,3,256,128]{3,2,1,0:T(8,128)(2,1)}, bf16[2,3,256,128]{3,2,1,0:T(8,128)(2,1)}, u32[]{:S(2)}, u32[]{:S(2)}) collective-permute-start(bf16[2,3,256,128]{3,2,1,0:T(8,128)(2,1)} %collective-permute-done.7.refs_3_.refs_6_), channel_id=1, source_target_pairs={{0,2},{1,3},{2,4},{3,5},{4,6},{5,7},{8,10},{9,11},{10,12},{11,13},... | collective-permute-start | bytes 1179656 | tf_op jit(solution)/shard_map/ppermute | solution.py:40
  64.9 15.8 %collective-permute-start.14 = (bf16[144,3648]{1,0:T(8,128)(2,1)}, bf16[144,3648]{1,0:T(8,128)(2,1)}, u32[]{:S(2)}, u32[]{:S(2)}) collective-permute-start(bf16[144,3648]{1,0:T(8,128)(2,1)} %collective-permute-done.12.refs_8_), channel_id=1, source_target_pairs={{0,8},{1,9},{2,10},{3,11},{4,12},{5,13},{6,14},{7,15},{8,0},{9,1},... | collective-permute-start | bytes 3151880 | tf_op jit(solution)/shard_map/ppermute | solution.py:40
  70.6 3.1 %collective-permute-start.11 = (bf16[2,3,256,128]{3,2,1,0:T(8,128)(2,1)}, bf16[2,3,256,128]{3,2,1,0:T(8,128)(2,1)}, u32[]{:S(2)}, u32[]{:S(2)}) collective-permute-start(bf16[2,3,256,128]{3,2,1,0:T(8,128)(2,1)} %collective-permute-done.9.refs_3_.refs_6_), channel_id=1, source_target_pairs={{0,8},{1,9},{2,10},{3,11},{4,12},{5,13},{6,14},{7,15},{8,0},{9,1},... | collective-permute-start | bytes 1179656 | tf_op jit(solution)/shard_map/ppermute | solution.py:40
  70.6 10.1 %collective-permute-start.16 = (bf16[576,384]{1,0:T(8,128)(2,1)}, bf16[576,384]{1,0:T(8,128)(2,1)}, u32[]{:S(2)}, u32[]{:S(2)}) collective-permute-start(bf16[576,384]{1,0:T(8,128)(2,1)} %bitcast.15.refs_11_), channel_id=1, source_target_pairs={{0,8},{1,9},{2,10},{3,11},{4,12},{5,13},{6,14},{7,15},{8,0},{9,1},... | collective-permute-start | bytes 1327112 | tf_op jit(solution)/shard_map/ppermute | solution.py:40
  73.7 7.0 %collective-permute-start.17 = (bf16[576,384]{1,0:T(8,128)(2,1)}, bf16[576,384]{1,0:T(8,128)(2,1)}, u32[]{:S(2)}, u32[]{:S(2)}) collective-permute-start(bf16[576,384]{1,0:T(8,128)(2,1)} %collective-permute-done.15.refs_12_), channel_id=1, source_target_pairs={{0,8},{1,9},{2,10},{3,11},{4,12},{5,13},{6,14},{7,15},{8,0},{9,1},... | collective-permute-start | bytes 1327112 | tf_op jit(solution)/shard_map/ppermute | solution.py:40
  73.7 7.0 %collective-permute-start.5 = (bf16[576,256]{1,0:T(8,128)(2,1)}, bf16[576,256]{1,0:T(8,128)(2,1)}, u32[]{:S(2)}, u32[]{:S(2)}) collective-permute-start(bf16[576,256]{1,0:T(8,128)(2,1)} %get-tuple-element.218), channel_id=1, source_target_pairs={{0,0},{1,8},{2,14},{3,6},{4,2},{5,10},{6,12},{7,4},{8,1},{9,9},{10... | collective-permute-start | bytes 884744 | tf_op jit(solution)/shard_map/ppermute | solution.py:40
  103.3 26.2 %collective-permute-start.18 = (bf16[2,6016,128]{2,1,0:T(8,128)(2,1)}, bf16[2,6016,128]{2,1,0:T(8,128)(2,1)}, u32[]{:S(2)}, u32[]{:S(2)}) collective-permute-start(bf16[2,6016,128]{2,1,0:T(8,128)(2,1)} %get-tuple-element.147), channel_id=1, source_target_pairs={{0,8},{1,9},{2,10},{3,11},{4,12},{5,13},{6,14},{7,15},{8,0},{9,1},... | collective-permute-start | bytes 9240584 | tf_op jit(solution)/shard_map/ppermute | solution.py:40
  105.2 5.8 %collective-permute-start.19 = (bf16[3,256,128]{2,1,0:T(8,128)(2,1)}, bf16[3,256,128]{2,1,0:T(8,128)(2,1)S(1)}, u32[]{:S(2)}, u32[]{:S(2)}) collective-permute-start(bf16[3,256,128]{2,1,0:T(8,128)(2,1)} %get-tuple-element.152), channel_id=1, source_target_pairs={{0,8},{1,9},{2,10},{3,11},{4,12},{5,13},{6,14},{7,15},{8,0},{9,1},... | collective-permute-start | bytes 589832 | tf_op jit(solution)/shard_map/ppermute | solution.py:40
  105.2 6.1 %collective-permute-start.20 = (bf16[3,256,128]{2,1,0:T(8,128)(2,1)}, bf16[3,256,128]{2,1,0:T(8,128)(2,1)}, u32[]{:S(2)}, u32[]{:S(2)}) collective-permute-start(bf16[3,256,128]{2,1,0:T(8,128)(2,1)} %get-tuple-element.153), channel_id=1, source_target_pairs={{0,8},{1,9},{2,10},{3,11},{4,12},{5,13},{6,14},{7,15},{8,0},{9,1},... | collective-permute-start | bytes 589832 | tf_op jit(solution)/shard_map/ppermute | solution.py:40
  111.0 0.7 copy-start.11
  113.7 29.1 %collective-permute-start.24 = (bf16[576,256]{1,0:T(8,128)(2,1)}, bf16[576,256]{1,0:T(8,128)(2,1)}, u32[]{:S(2)}, u32[]{:S(2)}) collective-permute-start(bf16[576,256]{1,0:T(8,128)(2,1)} %get-tuple-element.163), channel_id=1, source_target_pairs={{0,0},{8,1},{14,2},{6,3},{2,4},{10,5},{12,6},{4,7},{1,8},{9,9},{15... | collective-permute-start | bytes 884744 | tf_op jit(solution)/shard_map/ppermute | solution.py:40
  117.4 27.4 %collective-permute-start.25 = (bf16[576,256]{1,0:T(8,128)(2,1)}, bf16[576,256]{1,0:T(8,128)(2,1)}, u32[]{:S(2)}, u32[]{:S(2)}) collective-permute-start(bf16[576,256]{1,0:T(8,128)(2,1)} %get-tuple-element.164), channel_id=1, source_target_pairs={{6,0},{14,1},{8,2},{0,3},{4,4},{12,5},{10,6},{2,7},{7,8},{15,9},{9... | collective-permute-start | bytes 884744 | tf_op jit(solution)/shard_map/ppermute | solution.py:40
  132.6 19.9 %collective-permute-start.23 = (bf16[2,3,256,128]{3,2,1,0:T(8,128)(2,1)}, bf16[2,3,256,128]{3,2,1,0:T(8,128)(2,1)}, u32[]{:S(2)}, u32[]{:S(2)}) collective-permute-start(bf16[2,3,256,128]{3,2,1,0:T(8,128)(2,1)} %shard_map.211), channel_id=1, source_target_pairs={{2,0},{3,1},{4,2},{5,3},{6,4},{7,5},{10,8},{11,9},{12,10},{13,11},... | collective-permute-start | bytes 1179656 | tf_op jit(solution)/shard_map/ppermute | solution.py:40
  133.9 22.1 %collective-permute-start.26 = (bf16[2,1504,128]{2,1,0:T(8,128)(2,1)}, bf16[2,1504,128]{2,1,0:T(8,128)(2,1)}, u32[]{:S(2)}, u32[]{:S(2)}) collective-permute-start(bf16[2,1504,128]{2,1,0:T(8,128)(2,1)} %get-tuple-element.170), channel_id=1, source_target_pairs={{0,16},{1,17},{2,18},{3,19},{4,20},{5,21},{6,22},{7,23},{8,24},{9,... | collective-permute-start | bytes 2310152 | tf_op jit(solution)/shard_map/ppermute | solution.py:40
  138.9 18.6 %collective-permute-start.27 = (bf16[2,1504,128]{2,1,0:T(8,128)(2,1)}, bf16[2,1504,128]{2,1,0:T(8,128)(2,1)}, u32[]{:S(2)}, u32[]{:S(2)}) collective-permute-start(bf16[2,1504,128]{2,1,0:T(8,128)(2,1)} %get-tuple-element.171), channel_id=1, source_target_pairs={{0,1},{1,0},{2,3},{3,2},{4,5},{5,4},{6,7},{7,6},{8,9},{9,8},{10,11... | collective-permute-start | bytes 2310152 | tf_op jit(solution)/shard_map/ppermute | solution.py:40
  142.8 2.0 collective-permute-start.21
  144.8 1.8 collective-permute-start.22
  144.8 16.3 %copy-start.10 = (bf16[3,256,128]{2,1,0:T(8,128)(2,1)}, bf16[3,256,128]{2,1,0:T(8,128)(2,1)S(1)}, u32[]{:S(2)}) copy-start(bf16[3,256,128]{2,1,0:T(8,128)(2,1)S(1)} %collective-permute-done.21.twin_a) | copy-start | bytes 589828
  161.1 11.1 %collective-permute-start.28 = (bf16[1504,128]{1,0:T(8,128)(2,1)}, bf16[1504,128]{1,0:T(8,128)(2,1)}, u32[]{:S(2)}, u32[]{:S(2)}) collective-permute-start(bf16[1504,128]{1,0:T(8,128)(2,1)} %get-tuple-element.178), channel_id=1, source_target_pairs={{0,1},{1,0},{2,3},{3,2},{4,5},{5,4},{6,7},{7,6},{8,9},{9,8},{10,11... | collective-permute-start | bytes 1155080 | tf_op jit(solution)/shard_map/ppermute | solution.py:40
  163.4 10.2 %collective-permute-start.29 = (bf16[1504,128]{1,0:T(8,128)(2,1)}, bf16[1504,128]{1,0:T(8,128)(2,1)}, u32[]{:S(2)}, u32[]{:S(2)}) collective-permute-start(bf16[1504,128]{1,0:T(8,128)(2,1)} %get-tuple-element.180), channel_id=1, source_target_pairs={{0,16},{1,17},{2,18},{3,19},{4,20},{5,21},{6,22},{7,23},{8,24},{9,... | collective-permute-start | bytes 1155080 | tf_op jit(solution)/shard_map/ppermute | solution.py:40
  166.5 36.0 %collective-permute-start.32 = (bf16[2,3,256,128]{3,2,1,0:T(8,128)(2,1)}, bf16[2,3,256,128]{3,2,1,0:T(8,128)(2,1)}, u32[]{:S(2)}, u32[]{:S(2)}) collective-permute-start(bf16[2,3,256,128]{3,2,1,0:T(8,128)(2,1)} %shard_map.216), channel_id=1, source_target_pairs={{2,0},{3,1},{4,2},{5,3},{6,4},{7,5},{10,8},{11,9},{12,10},{13,11},... | collective-permute-start | bytes 1179656 | tf_op jit(solution)/shard_map/ppermute | solution.py:40
  176.0 24.3 %all-to-all-start = ((bf16[4,752,128]{2,1,0:T(8,128)(2,1)}), bf16[4,752,128]{2,1,0:T(8,128)(2,1)}, u32[]{:S(2)}, u32[]{:S(2)}) async-start(bf16[4,752,128]{2,1,0:T(8,128)(2,1)} %bitcast.37), calls=%async_computation | async-start | bytes 1540096 | tf_op jit(solution)/shard_map/all_to_all | solution.py:784
  193.1 9.4 %collective-permute-start.30 = (bf16[3,256,128]{2,1,0:T(8,128)(2,1)}, bf16[3,256,128]{2,1,0:T(8,128)(2,1)S(1)}, u32[]{:S(2)}, u32[]{:S(2)}) collective-permute-start(bf16[3,256,128]{2,1,0:T(8,128)(2,1)} %get-tuple-element.191), channel_id=1, source_target_pairs={{0,8},{1,9},{2,10},{3,11},{4,12},{5,13},{6,14},{7,15},{8,0},{9,1},... | collective-permute-start | bytes 589832 | tf_op jit(solution)/shard_map/ppermute | solution.py:40
  193.1 9.4 %collective-permute-start.31 = (bf16[3,256,128]{2,1,0:T(8,128)(2,1)}, bf16[3,256,128]{2,1,0:T(8,128)(2,1)}, u32[]{:S(2)}, u32[]{:S(2)}) collective-permute-start(bf16[3,256,128]{2,1,0:T(8,128)(2,1)} %get-tuple-element.192), channel_id=1, source_target_pairs={{0,8},{1,9},{2,10},{3,11},{4,12},{5,13},{6,14},{7,15},{8,0},{9,1},... | collective-permute-start | bytes 589832 | tf_op jit(solution)/shard_map/ppermute | solution.py:40
  202.4 0.7 copy-start.9
  210.0 4.5 %copy-start.3 = (bf16[2,1152,128]{2,1,0:T(8,128)(2,1)S(1)}, bf16[2,1152,128]{2,1,0:T(8,128)(2,1)}, u32[]{:S(2)}) copy-start(bf16[2,1152,128]{2,1,0:T(8,128)(2,1)} %get-tuple-element.194) | copy-start | bytes 1769476
  210.0 4.5 %collective-permute-start.33 = (bf16[2,1152,128]{2,1,0:T(8,128)(2,1)}, bf16[2,1152,128]{2,1,0:T(8,128)(2,1)S(1)}, u32[]{:S(2)}, u32[]{:S(2)}) collective-permute-start(bf16[2,1152,128]{2,1,0:T(8,128)(2,1)} %get-tuple-element.195), channel_id=1, source_target_pairs={{0,8},{1,9},{2,10},{3,11},{4,12},{5,13},{6,14},{7,15},{8,0},{9,1},... | collective-permute-start | bytes 1769480 | tf_op jit(solution)/shard_map/ppermute | solution.py:40
  210.1 25.0 %all-to-all-start.1 = ((bf16[4,752,128]{2,1,0:T(8,128)(2,1)}), bf16[4,752,128]{2,1,0:T(8,128)(2,1)}, u32[]{:S(2)}, u32[]{:S(2)}) async-start(bf16[4,752,128]{2,1,0:T(8,128)(2,1)} %shard_map.215), calls=%async_computation.1 | async-start | bytes 1540096 | tf_op jit(solution)/shard_map/all_to_all | solution.py:792
  214.4 20.6 %copy-start.17 = (bf16[576,256]{1,0:T(8,128)(2,1)S(1)}, bf16[576,256]{1,0:T(8,128)(2,1)}, u32[]{:S(2)}) copy-start(bf16[576,256]{1,0:T(8,128)(2,1)} %get-tuple-element.199) | copy-start | bytes 884740
  214.4 21.3 %copy-start.16 = (bf16[576,256]{1,0:T(8,128)(2,1)S(1)}, bf16[576,256]{1,0:T(8,128)(2,1)}, u32[]{:S(2)}) copy-start(bf16[576,256]{1,0:T(8,128)(2,1)} %get-tuple-element.200) | copy-start | bytes 884740
  214.6 9.3 %collective-permute-start.34 = (bf16[1152,128]{1,0:T(8,128)(2,1)S(1)}, bf16[1152,128]{1,0:T(8,128)(2,1)S(1)}, u32[]{:S(2)}, u32[]{:S(2)}) collective-permute-start(bf16[1152,128]{1,0:T(8,128)(2,1)S(1)} %fusion.1), channel_id=1, source_target_pairs={{0,16},{1,17},{2,18},{3,19},{4,20},{5,21},{6,22},{7,23},{8,24},{9,... | collective-permute-start | bytes 884744 | tf_op jit(solution)/shard_map/ppermute | solution.py:40
  235.0 12.0 %collective-permute-start.35 = (bf16[576,256]{1,0:T(8,128)(2,1)S(1)}, bf16[576,256]{1,0:T(8,128)(2,1)S(1)}, u32[]{:S(2)}, u32[]{:S(2)}) collective-permute-start(bf16[576,256]{1,0:T(8,128)(2,1)S(1)} %copy-done.17), channel_id=1, source_target_pairs={{0,0},{8,1},{14,2},{6,3},{2,4},{10,5},{12,6},{4,7},{1,8},{9,9},{15... | collective-permute-start | bytes 884744 | tf_op jit(solution)/shard_map/ppermute | solution.py:40
  235.7 16.7 %collective-permute-start.36 = (bf16[576,256]{1,0:T(8,128)(2,1)S(1)}, bf16[576,256]{1,0:T(8,128)(2,1)S(1)}, u32[]{:S(2)}, u32[]{:S(2)}) collective-permute-start(bf16[576,256]{1,0:T(8,128)(2,1)S(1)} %copy-done.16), channel_id=1, source_target_pairs={{6,0},{14,1},{8,2},{0,3},{4,4},{12,5},{10,6},{2,7},{7,8},{15,9},{9... | collective-permute-start | bytes 884744 | tf_op jit(solution)/shard_map/ppermute | solution.py:40
  239.0 18.9 %all-to-all-start.2 = ((bf16[8,144,128]{2,1,0:T(8,128)(2,1)}), bf16[8,144,128]{2,1,0:T(8,128)(2,1)}, u32[]{:S(2)}, u32[]{:S(2)}) async-start(bf16[8,144,128]{2,1,0:T(8,128)(2,1)} %bitcast.24), calls=%async_computation.2 | async-start | bytes 589824 | tf_op jit(solution)/shard_map/all_to_all | solution.py:784
  245.0 26.5 %collective-permute-start.37 = (bf16[3008,128]{1,0:T(8,128)(2,1)}, bf16[3008,128]{1,0:T(8,128)(2,1)}, u32[]{:S(2)}, u32[]{:S(2)}) collective-permute-start(bf16[3008,128]{1,0:T(8,128)(2,1)} %bitcast.21.near), channel_id=1, source_target_pairs={{0,1},{1,0},{2,3},{3,2},{4,5},{5,4},{6,7},{7,6},{8,9},{9,8},{10,11... | collective-permute-start | bytes 2310152 | tf_op jit(solution)/shard_map/ppermute | solution.py:40
  259.7 6.1 %copy-start.1 = (bf16[576,256]{1,0:T(8,128)(2,1)S(1)}, bf16[576,256]{1,0:T(8,128)(2,1)}, u32[]{:S(2)}) copy-start(bf16[576,256]{1,0:T(8,128)(2,1)} %get-tuple-element.221) | copy-start | bytes 884740
  259.7 6.1 %copy-start.2 = (bf16[576,256]{1,0:T(8,128)(2,1)S(1)}, bf16[576,256]{1,0:T(8,128)(2,1)}, u32[]{:S(2)}) copy-start(bf16[576,256]{1,0:T(8,128)(2,1)} %get-tuple-element.222) | copy-start | bytes 884740
  259.7 15.0 %all-to-all-start.3 = ((bf16[8,144,128]{2,1,0:T(8,128)(2,1)}), bf16[8,144,128]{2,1,0:T(8,128)(2,1)}, u32[]{:S(2)}, u32[]{:S(2)}) async-start(bf16[8,144,128]{2,1,0:T(8,128)(2,1)} %shard_map.219), calls=%async_computation.3 | async-start | bytes 589824 | tf_op jit(solution)/shard_map/all_to_all | solution.py:792

commit v2 on v1

--- a/solution.py
+++ b/solution.py
@@ -60,6 +60,7 @@
         across=by(lambda y, k, h, x: (y, k, h, 1 - x)),
         up=by(lambda y, k, h, x: (y, k, h + 1, x) if h + 1 < hs else None),
         down=by(lambda y, k, h, x: (y, k, h - 1, x) if h > 0 else None),
+        around=[by(lambda y, k, h, x, s=s: (y, k, (h + s) % hs, x)) for s in range(hs)],
         shift=[by(lambda y, k, h, x, s=s: ((y + s) % ys, k, h, x)) for s in range(ys)],
     )
 
@@ -254,7 +255,7 @@
         scratch_shapes=scratch,
         input_output_aliases=aliases,
         compiler_params=LIMIT,
-        cost_estimate=takes((10, 12)[stage] if stage < 2 else 3),
+        cost_estimate=takes(0),
     )(*given)
 
 
@@ -412,7 +413,7 @@
             pltpu.SemaphoreType.DMA((len(parts),)),
         ],
         compiler_params=LIMIT,
-        cost_estimate=takes(5),
+        cost_estimate=takes(0),
     )(sc, *xs, cos, sin, *parts)
 
 
@@ -692,7 +693,7 @@
             pltpu.SemaphoreType.DMA((len(parts),)),
         ],
         compiler_params=LIMIT,
-        cost_estimate=takes(0),
+        cost_estimate=takes(7),
     )(sc, *given, *parts)
 
 
@@ -709,14 +710,15 @@
             done += n
 
 
-def join_unpack_kernel(places, sc, near, far, *refs):
-    *outs, flat = refs
-    part = near.shape[0] // 2
-    for half in range(2):
-        for x in range(2):
-            piece = near if x == 0 else far
-            at = pl.multiple_of(part * (2 * half + lax.rem(sc[0] + x, 2)), 16)
-            flat[pl.ds(at, part)] = piece[half * part : (half + 1) * part]
+def join_unpack_kernel(places, parts, sc, *refs):
+    pieces, outs, flat = refs[: 2 * parts], refs[2 * parts : -1], refs[-1]
+    n = pieces[0].shape[0]
+    half = parts // 2
+    for i, piece in enumerate(pieces):
+        x = lax.rem(sc[0] + i // parts, 2)
+        p = lax.rem(sc[1] + parts - i % parts, parts)
+        at = lax.div(p, half) * (parts * n) + x * (half * n) + lax.rem(p, half) * n
+        flat[pl.ds(pl.multiple_of(at, 16), n)] = piece[...]
     unpack_kernel(places, flat, *outs)
 
 
@@ -733,18 +735,19 @@
     )(flat)
 
 
-def join_unpack(x, near, far, places):
+def join_unpack(place, near, far, places):
+    pieces = (*near, *far)
     out_shape = tuple(jax.ShapeDtypeStruct((p[1], p[3]), F32) for p in places)
     return pl.pallas_call(
-        functools.partial(join_unpack_kernel, [p[:3] for p in places]),
+        functools.partial(join_unpack_kernel, [p[:3] for p in places], len(near)),
         out_shape=out_shape,
         grid=(1,),
-        in_specs=[SM] + wholes(near, far),
+        in_specs=[SM] + wholes(*pieces),
         out_specs=wholes(*out_shape),
-        scratch_shapes=[pltpu.VMEM((2 * near.shape[0], 128), BF16)],
+        scratch_shapes=[pltpu.VMEM((len(pieces) * near[0].shape[0], 128), BF16)],
         compiler_params=LIMIT,
         cost_estimate=takes(3),
-    )(x, near, far)
+    )(place, *pieces)
 
 
 def chip_sum(mine, got, i):
@@ -765,6 +768,13 @@
     total = total.astype(BF16)
     for i in range(got.shape[0]):
         out[i] = total
+
+
+def sum_kernel(got, out):
+    total = got[0].astype(F32)
+    for i in range(1, got.shape[0]):
+        total = total + got[i].astype(F32)
+    out[...] = total.astype(BF16)
 
 
 def simple_call(kernel, out_shape, *given):
@@ -954,12 +964,13 @@
     )
     angle = frequency[:, None] * pos_f
     cos, sin = jnp.cos(angle), jnp.sin(angle)
-    qz, kv, normed_t, gains, pos, ids = project(order, xs, cos, sin, first_parts)
-
     feed_own = jnp.concatenate([gate_weight, up_weight, output_weight], axis=1)
     feed_own, down_own, _ = tie(feed_own, down_weight.T, first_parts[-1])
     feed_got = gather_y(feed_own, send, fsdp)
     down_got = gather_y(down_own, send, fsdp)
+    feed_got[0], *xs = tie(feed_got[0], *xs)
+    qz, kv, normed_t, gains, pos, ids = project(order, xs, cos, sin, first_parts)
+
     stages = []
     carried = None
     for s in range(reach + 1):
@@ -976,15 +987,13 @@
         fsdp, ctx, order, xs, cots, mixed, gains, feed_parts, down_parts
     )
 
+    got = send["core"](give)
     crossed = ys == 2
     x_ref = x.astype(jnp.int32).reshape(1)
     dq = None
     came = None
     for s in range(reach, -1, -1):
         sc = ids
-        if s == reach - 1:
-            give, dq = tie(give, dq)
-            got = send["core"](give)
         if s == reach - 1 and crossed:
             first_y, first_x = first_sums(x_ref, mine, got)
             sc, first_y, first_x = tie(sc, first_y, first_x)
@@ -1021,20 +1030,24 @@
             keep_two,
             came_two,
         )
+        late, dq = tie(late, dq)
         late = exchange(late, ("h",), hs)
     else:
         late = exchange(sum_y(mine, got, send), CTX, ctx)
-    late, dq = tie(spread(late), dq)
-    late = gather_over(late, ("h",) if crossed else CTX)
     tok_a, tok_b, mine_front, give_front = last(
         fsdp, ctx, order, xs, cos, sin, normed_t, gains, second, d_middle, dq, dkv, first_parts
     )
     got_front = send["core"](give_front)
+    late, got_front = tie(late, got_front)
     front = sum_y(mine_front, got_front, send)
-    front, late, tok_a, tok_b = tie(front, late, tok_a, tok_b)
+    if crossed:
+        piece = simple_call(sum_kernel, jax.ShapeDtypeStruct(late.shape[1:], BF16), late)
+        near = [piece] + [send["around"][s](piece) for s in range(1, hs)]
+        far = [send["across"](p) for p in near]
+        *near, tok_a, tok_b = tie(*near, tok_a, tok_b)
+    else:
+        late = gather_over(spread(late), CTX)
     front = spread(exchange(front, CTX, ctx))
-    if crossed:
-        late_far = send["across"](late)
     front = gather_over(front, CTX)
     tokens_grad = send_back(send, tok_a, tok_b)
 
@@ -1048,7 +1061,7 @@
         (2 * gate_rows + out_rows, width, 0, down_shard),
     ]
     if crossed:
-        late_grads = join_unpack(x_ref, late, late_far, places)
+        late_grads = join_unpack(jnp.stack([x, h]).astype(jnp.int32), near, far, places)
     else:
         late_grads = unpack(late, places)
     gate_grad, up_grad, output_grad, down_grad = late_grads

time: 280 us -> 268 us (0.957)
  waiting for transfers between devices: 81.8 us -> 63.4 us
  starting transfers between devices: 87 us -> 95.6 us
  Pallas kernels: 91.5 us -> 85.2 us
    ppermute x38 -> x44, waiting for transfers between devices: 61.3 us -> 37.4 us  [along(): return lambda a: lax.ppermute(a, AXES, pairs)]
    ppermute x38 -> x44, starting transfers between devices: 67.4 us -> 78.3 us  [along(): return lambda a: lax.ppermute(a, AXES, pairs)]
    all_to_all x2, waiting for transfers between devices: 10.2 us -> 20.6 us  [exchange(): return lax.all_to_all(parts, axes, 0, 0, tiled=True)]
    all_to_all x2 -> x1, waiting for transfers between devices: 10.3 us -> 5.4 us  [gather_over(): return lax.all_to_all(spread, axes, 0, 0, tiled=True).reshape(-1, 128)]
    all_to_all x2 -> x1, starting transfers between devices: 8.53 us -> 4.06 us  [gather_over(): return lax.all_to_all(spread, axes, 0, 0, tiled=True).reshape(-1, 128)]
    pallas_call x3, Pallas kernels: 19.6 us -> 16.4 us  [attend_backward(): pl.pallas_call(functools.partial(backward_kernel, stage, first, own_type)...]
    pallas_call x3, Pallas kernels: 16.9 us -> 13.9 us  [attend_forward(): pl.pallas_call(functools.partial(forward_kernel, stage, last), out_shape=...]
    unnamed x36 -> x38, local copies, waits for them, and re-layouts: 1.87 us -> 4.69 us
  transfers between devices with their start and end apart: 42 -> 47, of which waited for: 20 -> 16; matrix products, arithmetic and copies ran while one was open for 5% -> 4% of each run, Pallas kernels for 18% -> 22%
where the time goes in v2:
time: 268 us; the launch traced here: 267 us
  starting transfers between devices  95.6 us (36%)
  Pallas kernels  85.2 us (32%)
  waiting for transfers between devices  63.4 us (24%)
  other arithmetic  13.1 us (5%)
  local copies, waits for them, and re-layouts  8.28 us (3%)
    ppermute x44, starting transfers between devices, along(): return lambda a: lax.ppermute(a, AXES, pairs)  78.3 us
    ppermute x44, waiting for transfers between devices, along(): return lambda a: lax.ppermute(a, AXES, pairs)  37.4 us
    all_to_all x2, waiting for transfers between devices, exchange(): return lax.all_to_all(parts, axes, 0, 0, tiled=True)  20.6 us
    pallas_call x1, Pallas kernels, feed(): pl.pallas_call(functools.partial(feed_kernel, fsdp, len(parts), ff // 4 i...  18.9 us
    pallas_call x3, Pallas kernels, attend_backward(): pl.pallas_call(functools.partial(backward_kernel, stage, first, own_type)...  16.4 us
    pallas_call x3, Pallas kernels, attend_forward(): pl.pallas_call(functools.partial(forward_kernel, stage, last), out_shape=...  13.9 us
    all_to_all x2, starting transfers between devices, exchange(): return lax.all_to_all(parts, axes, 0, 0, tiled=True)  13.2 us
    pallas_call x5, Pallas kernels, simple_call(): pl.pallas_call(kernel, out_shape=out_shape, grid=(1,), in_specs=wholes(*g...  10.2 us
  transfers between devices with their start and end apart: 47, of which 16 were waited for; matrix products, arithmetic and copies ran while one was open for 4% of the time, Pallas kernels for 22%

profile of v2, /device:TPU:0, one launch (start us, length us, event | category | flops | bytes accessed | tf_op | source)
XLA Modules:
  0.0 266.7 jit_solution(12307531370677523456)
XLA Ops:
  1.2 2.0 shard_map.203
  3.4 1.1 concatenate.16.refs_5_.refs_14_
  4.5 3.0 %collective-permute-start = (bf16[144,1024]{1,0:T(8,128)(2,1)S(1)}, bf16[144,1024]{1,0:T(8,128)(2,1)S(1)}, u32[]{:S(2)}, u32[]{:S(2)}) collective-permute-start(bf16[144,1024]{1,0:T(8,128)(2,1)S(1)} %concatenate.16.refs_5_.refs_14_), channel_id=1, source_target_pairs={{0,16},{1,17},{2,18},{3,19},{4,20},{5,21},{6,22},{7,23},{8,24},{9,... | collective-permute-start | bytes 884744 | tf_op jit(solution)/shard_map/ppermute | solution.py:40
  7.6 1.6 collective-permute-start.2
  9.2 6.4 %collective-permute-start.3 = (bf16[592,256]{1,0:T(8,128)(2,1)}, bf16[592,256]{1,0:T(8,128)(2,1)S(1)}, u32[]{:S(2)}, u32[]{:S(2)}) collective-permute-start(bf16[592,256]{1,0:T(8,128)(2,1)} %get-tuple-element.123), channel_id=1, source_target_pairs={{0,6},{1,14},{2,8},{3,0},{4,4},{5,12},{6,10},{7,2},{8,7},{9,15},{1... | collective-permute-start | bytes 909320 | tf_op jit(solution)/shard_map/ppermute | solution.py:40
  17.2 2.3 pad_maximum_fusion.refs_7_
  21.3 2.8 %collective-permute-done.3.refs_2_ = bf16[592,256]{1,0:T(8,128)(2,1)S(1)} collective-permute-done((bf16[592,256]{1,0:T(8,128)(2,1)}, bf16[592,256]{1,0:T(8,128)(2,1)S(1)}, u32[]{:S(2)}, u32[]{:S(2)}) %collective-permute-start.3) | collective-permute-done | bytes 303136 | tf_op jit(solution)/shard_map/ppermute | solution.py:40
  24.2 1.0 multiply_sine_fusion
  25.9 5.1 %shard_map.204 = (bf16[2,3,128,768]{3,2,1,0:T(8,128)(2,1)}, bf16[2,3,256,128]{3,2,1,0:T(8,128)(2,1)}, bf16[576,512]{1,0:T(8,128)(2,1)}, bf16[576,128]{1,0:T(8,12...) custom-call(s32[7]{0:T(128)} %stack.47.refs_0_, bf16[592,256]{1,0:T(8,128)(2,1)} %copy-done.2, bf16[592,256]{1,0:T(8,128)(2,1)} %copy-done.3, ...), custom_call_target="tpu_custom_call" | custom-call | tf_op jit(solution)/shard_map/pallas_call | solution.py:405
  31.1 7.7 %collective-permute-start.7 = (bf16[2,3,256,128]{3,2,1,0:T(8,128)(2,1)}, bf16[2,3,256,128]{3,2,1,0:T(8,128)(2,1)}, u32[]{:S(2)}, u32[]{:S(2)}) collective-permute-start(bf16[2,3,256,128]{3,2,1,0:T(8,128)(2,1)} %get-tuple-element.130.refs_3_.refs_6_), channel_id=1, source_target_pairs={{0,2},{1,3},{2,4},{3,5},{4,6},{5,7},{8,10},{9,11},{10,12},{11,13},... | collective-permute-start | bytes 1179656 | tf_op jit(solution)/shard_map/ppermute | solution.py:40
  38.7 7.4 %shard_map.205 = (f32[2,3,1,768]{3,2,1,0:T(1,128)}, f32[2,3,1,768]{3,2,1,0:T(1,128)}, f32[2,3,64,768]{3,2,1,0:T(8,128)}) custom-call(s32[8]{0:T(128)} %get-tuple-element.189.refs_0_, s32[2,1,256]{2,1,0:T(1,128)} %get-tuple-element.128.refs_1_, bf16[2,3,128,768]{3,2,1,0:T(8,128)(2,1)} %get-tuple-element.129.refs_2_, ...), custom_call_target="tpu_custom_call" | custom-call | tf_op jit(solution)/shard_map/pallas_call | solution.py:249
  46.1 1.2 collective-permute-done.7.refs_3_.refs_6_
  47.3 2.1 collective-permute-start.10
  49.4 3.1 %collective-permute-start.9 = (bf16[2,3,256,128]{3,2,1,0:T(8,128)(2,1)}, bf16[2,3,256,128]{3,2,1,0:T(8,128)(2,1)}, u32[]{:S(2)}, u32[]{:S(2)}) collective-permute-start(bf16[2,3,256,128]{3,2,1,0:T(8,128)(2,1)} %collective-permute-done.7.refs_3_.refs_6_), channel_id=1, source_target_pairs={{0,2},{1,3},{2,4},{3,5},{4,6},{5,7},{8,10},{9,11},{10,12},{11,13},... | collective-permute-start | bytes 1179656 | tf_op jit(solution)/shard_map/ppermute | solution.py:40
  53.5 1.9 broadcast_select_fusion.4
  55.4 2.6 collective-permute-start.6
  58.0 3.2 %shard_map.206 = (f32[2,3,1,768]{3,2,1,0:T(1,128)}, f32[2,3,1,768]{3,2,1,0:T(1,128)}, f32[2,3,64,768]{3,2,1,0:T(8,128)}) custom-call(s32[8]{0:T(128)} %get-tuple-element.189.refs_0_, s32[2,1,256]{2,1,0:T(1,128)} %get-tuple-element.128.refs_1_, ...), custom_call_target="tpu_custom_call", output_to_operand_aliasing={{0}: (5, {}), {1}: (6, {}), {2}: (7, {})} | custom-call | tf_op jit(solution)/shard_map/pallas_call | solution.py:249
  61.4 6.0 %collective-permute-done.6.refs_4_ = bf16[576,256]{1,0:T(8,128)(2,1)} collective-permute-done((bf16[576,256]{1,0:T(8,128)(2,1)}, bf16[576,256]{1,0:T(8,128)(2,1)}, u32[]{:S(2)}, u32[]{:S(2)}) %collective-permute-start.6) | collective-permute-done | bytes 294944 | tf_op jit(solution)/shard_map/ppermute | solution.py:40
  67.9 3.7 %collective-permute-start.5 = (bf16[576,256]{1,0:T(8,128)(2,1)}, bf16[576,256]{1,0:T(8,128)(2,1)}, u32[]{:S(2)}, u32[]{:S(2)}) collective-permute-start(bf16[576,256]{1,0:T(8,128)(2,1)} %get-tuple-element.228), channel_id=1, source_target_pairs={{0,0},{1,8},{2,14},{3,6},{4,2},{5,10},{6,12},{7,4},{8,1},{9,9},{10... | collective-permute-start | bytes 884744 | tf_op jit(solution)/shard_map/ppermute | solution.py:40
  71.7 3.3 %shard_map.207 = (bf16[2,3,64,768]{3,2,1,0:T(8,128)(2,1)}, f32[2,3,1,768]{3,2,1,0:T(1,128)}) custom-call(s32[8]{0:T(128)} %get-tuple-element.189.refs_0_, s32[2,1,256]{2,1,0:T(1,128)} %get-tuple-element.128.refs_1_, bf16[2,3,128,768]{3,2,1,0:T(8,128)(2,1)} %get-tuple-element.129.refs_2_, bf16[2,3,256,128]{3,2,1,0:T(8,128)(2,1)} %collective-permute-done.9.refs_3_.refs_6_, ...), custom_call_target="tpu_custom_call" | custom-call | tf_op jit(solution)/shard_map/pallas_call | solution.py:249
  75.0 18.9 %shard_map.208 = (bf16[576,256]{1,0:T(8,128)(2,1)}, bf16[576,256]{1,0:T(8,128)(2,1)}, f32[576,512]{1,0:T(8,128)}, bf16[2,3,128,768]{3,2,1,0:T(8,128)(2,1)}, f32[...) custom-call(s32[7]{0:T(128)} %stack.47.refs_0_, ...), custom_call_target="tpu_custom_call" | custom-call | flops 21849999360 | tf_op jit(solution)/shard_map/pallas_call | solution.py:590
  93.8 1.4 collective-permute-start.18
  95.2 3.7 %shard_map.210 = (f32[2,3,64,768]{3,2,1,0:T(8,128)}, bf16[2,3,256,128]{3,2,1,0:T(8,128)(2,1)}, bf16[3,256,128]{2,1,0:T(8,128)(2,1)}, bf16[3,256,128]{2,1,0:T(8,128)(2,1)}) custom-call(s32[8]{0:T(128)} %get-tuple-element.189.refs_0_, s32[2,1,256]{2,1,0:T(1,128)} %get-tuple-element.128.refs_1_, bf16[2,3,128,768]{3,2,1,0:T(8,128)(2,1)} %get-tuple-element.129.refs_2_, ...), custom_call_target="tpu_custom_call" | custom-call | flops 4600000000 | tf_op jit(solution)/shard_map/pallas_call | solution.py:275
  99.5 1.7 collective-permute-done.19.twin_a
  101.9 2.0 shard_map.211
  103.9 3.8 %collective-permute-start.24 = (bf16[576,256]{1,0:T(8,128)(2,1)}, bf16[576,256]{1,0:T(8,128)(2,1)}, u32[]{:S(2)}, u32[]{:S(2)}) collective-permute-start(bf16[576,256]{1,0:T(8,128)(2,1)} %get-tuple-element.169), channel_id=1, source_target_pairs={{0,0},{8,1},{14,2},{6,3},{2,4},{10,5},{12,6},{4,7},{1,8},{9,9},{15... | collective-permute-start | bytes 884744 | tf_op jit(solution)/shard_map/ppermute | solution.py:40
  107.6 14.2 %collective-permute-start.25 = (bf16[576,256]{1,0:T(8,128)(2,1)}, bf16[576,256]{1,0:T(8,128)(2,1)}, u32[]{:S(2)}, u32[]{:S(2)}) collective-permute-start(bf16[576,256]{1,0:T(8,128)(2,1)} %get-tuple-element.170), channel_id=1, source_target_pairs={{6,0},{14,1},{8,2},{0,3},{4,4},{12,5},{10,6},{2,7},{7,8},{15,9},{9... | collective-permute-start | bytes 884744 | tf_op jit(solution)/shard_map/ppermute | solution.py:40
  121.9 3.1 %shard_map.209 = (bf16[2,1504,128]{2,1,0:T(8,128)(2,1)}, bf16[2,1504,128]{2,1,0:T(8,128)(2,1)}) custom-call(s32[1]{0:T(128)} %bitcast.13.x, bf16[2,6016,128]{2,1,0:T(8,128)(2,1)} %get-tuple-element.149.refs_0_.refs_1_.refs_2_.refs_3_, bf16[2,6016,128]{2,1,0:T(8,128)(2,1)} %get-tuple-element.149.refs_0_.refs_1_.refs_2_.refs_3_, ...), custom_call_target="tpu_custom_call" | custom-call | tf_op jit(solution)/shard_map/pallas_call | solution.py:837
  125.0 1.3 collective-permute-start.23
  126.7 3.9 %shard_map.212 = (f32[2,3,64,768]{3,2,1,0:T(8,128)}, bf16[2,3,256,128]{3,2,1,0:T(8,128)(2,1)}, bf16[3,256,128]{2,1,0:T(8,128)(2,1)}, bf16[3,256,128]{2,1,0:T(8,128)(2,1)}) custom-call(s32[8]{0:T(128)} %get-tuple-element.189.refs_0_, s32[2,1,256]{2,1,0:T(1,128)} %get-tuple-element.128.refs_1_, ...), custom_call_target="tpu_custom_call", output_to_operand_aliasing={{0}: (8, {})} | custom-call | flops 16099999744 | tf_op jit(solution)/shard_map/pallas_call | solution.py:275
  130.7 6.1 %collective-permute-done.25 = bf16[576,256]{1,0:T(8,128)(2,1)} collective-permute-done((bf16[576,256]{1,0:T(8,128)(2,1)}, bf16[576,256]{1,0:T(8,128)(2,1)}, u32[]{:S(2)}, u32[]{:S(2)}) %collective-permute-start.25) | collective-permute-done | bytes 294944 | tf_op jit(solution)/shard_map/ppermute | solution.py:40
  136.8 1.8 collective-permute-done.22.twin_b
  138.6 4.9 %collective-permute-done.23.refs_0_ = bf16[2,3,256,128]{3,2,1,0:T(8,128)(2,1)} collective-permute-done((bf16[2,3,256,128]{3,2,1,0:T(8,128)(2,1)}, bf16[2,3,256,128]{3,2,1,0:T(8,128)(2,1)}, u32[]{:S(2)}, u32[]{:S(2)}) %collective-permute-start.23) | collective-permute-done | bytes 393248 | tf_op jit(solution)/shard_map/ppermute | solution.py:40
  143.5 2.2 shard_map.215
  145.7 2.3 collective-permute-done.27.refs_10_.refs_11_
  148.0 3.6 %shard_map.213 = (bf16[1504,128]{1,0:T(8,128)(2,1)}, bf16[1504,128]{1,0:T(8,128)(2,1)}, bf16[1504,128]{1,0:T(8,128)(2,1)}, bf16[1504,128]{1,0:T(8,128)(2,1)}) custom-call(s32[1]{0:T(128)} %bitcast.13.x, bf16[2,6016,128]{2,1,0:T(8,128)(2,1)} %get-tuple-element.149.refs_0_.refs_1_.refs_2_.refs_3_, ...), custom_call_target="tpu_custom_call" | custom-call | tf_op jit(solution)/shard_map/pallas_call | solution.py:873
  152.3 1.3 collective-permute-start.32
  153.6 8.8 %shard_map.216 = (f32[2,3,64,768]{3,2,1,0:T(8,128)}, f32[2,3,256,128]{3,2,1,0:T(8,128)}, bf16[3,256,128]{2,1,0:T(8,128)(2,1)}, bf16[3,256,128]{2,1,0:T(8,128)(2,1)}) custom-call(s32[8]{0:T(128)} %get-tuple-element.189.refs_0_, s32[2,1,256]{2,1,0:T(1,128)} %get-tuple-element.128.refs_1_, ...), custom_call_target="tpu_custom_call", output_to_operand_aliasing={{0}: (8, {})} | custom-call | flops 13799999488 | tf_op jit(solution)/shard_map/pallas_call | solution.py:275
  162.4 2.5 collective-permute-start.30
  165.0 2.4 shard_map.214
  167.4 8.7 %all-to-all-start = ((bf16[4,752,128]{2,1,0:T(8,128)(2,1)}), bf16[4,752,128]{2,1,0:T(8,128)(2,1)}, u32[]{:S(2)}, u32[]{:S(2)}) async-start(bf16[4,752,128]{2,1,0:T(8,128)(2,1)} %bitcast.37), calls=%async_computation | async-start | bytes 1540096 | tf_op jit(solution)/shard_map/all_to_all | solution.py:794
  176.8 6.9 %shard_map.217 = (bf16[576,256]{1,0:T(8,128)(2,1)}, bf16[576,256]{1,0:T(8,128)(2,1)}, bf16[2,1152,128]{2,1,0:T(8,128)(2,1)}, bf16[2,1152,128]{2,1,0:T(8,128)(2,1)}) custom-call(s32[7]{0:T(128)} %stack.47.refs_0_, bf16[592,256]{1,0:T(8,128)(2,1)} %copy-done.2, bf16[592,256]{1,0:T(8,128)(2,1)} %copy-done.3, f32[32,512]{1,0:T(8,128)} %get-tuple-element.230.refs_3_, ...), custom_call_target="tpu_custom_call" | custom-call | flops 8049999872 | tf_op jit(solution)/shard_map/pallas_call | solution.py:683
  183.7 2.2 collective-permute-done.33
  185.9 10.8 %all-to-all-done.got = bf16[4,752,128]{2,1,0:T(8,128)(2,1)} async-done(((bf16[4,752,128]{2,1,0:T(8,128)(2,1)}), bf16[4,752,128]{2,1,0:T(8,128)(2,1)}, u32[]{:S(2)}, u32[]{:S(2)}) %all-to-all-start) | async-done | bytes 770080 | tf_op jit(solution)/shard_map/all_to_all | solution.py:794
  196.7 1.8 fusion.1
  198.5 1.9 shard_map.218.refs_0_
  200.4 1.2 collective-permute-start.36
  202.4 3.8 %collective-permute-start.40 = (bf16[752,128]{1,0:T(8,128)(2,1)}, bf16[752,128]{1,0:T(8,128)(2,1)S(1)}, u32[]{:S(2)}, u32[]{:S(2)}) collective-permute-start(bf16[752,128]{1,0:T(8,128)(2,1)} %shard_map.218.refs_0_), channel_id=1, source_target_pairs={{0,1},{1,0},{2,3},{3,2},{4,5},{5,4},{6,7},{7,6},{8,9},{9,8},{10,11... | collective-permute-start | bytes 577544 | tf_op jit(solution)/shard_map/ppermute | solution.py:40
  206.2 2.1 collective-permute-done.36.refs_3_
  208.3 3.0 %collective-permute-start.43 = (bf16[752,128]{1,0:T(8,128)(2,1)S(1)}, bf16[752,128]{1,0:T(8,128)(2,1)S(1)}, u32[]{:S(2)}, u32[]{:S(2)}) collective-permute-start(bf16[752,128]{1,0:T(8,128)(2,1)S(1)} %collective-permute-done.36.refs_3_), channel_id=1, source_target_pairs={{0,1},{1,0},{2,3},{3,2},{4,5},{5,4},{6,7},{7,6},{8,9},{9,8},{10,11... | collective-permute-start | bytes 577544 | tf_op jit(solution)/shard_map/ppermute | solution.py:40
  211.3 5.9 %collective-permute-done.35.refs_2_ = bf16[752,128]{1,0:T(8,128)(2,1)S(1)} collective-permute-done((bf16[752,128]{1,0:T(8,128)(2,1)}, bf16[752,128]{1,0:T(8,128)(2,1)S(1)}, u32[]{:S(2)}, u32[]{:S(2)}) %collective-permute-start.35) | collective-permute-done | bytes 192544 | tf_op jit(solution)/shard_map/ppermute | solution.py:40
  217.2 3.3 %collective-permute-start.42 = (bf16[752,128]{1,0:T(8,128)(2,1)S(1)}, bf16[752,128]{1,0:T(8,128)(2,1)S(1)}, u32[]{:S(2)}, u32[]{:S(2)}) collective-permute-start(bf16[752,128]{1,0:T(8,128)(2,1)S(1)} %collective-permute-done.35.refs_2_), channel_id=1, source_target_pairs={{0,1},{1,0},{2,3},{3,2},{4,5},{5,4},{6,7},{7,6},{8,9},{9,8},{10,11... | collective-permute-start | bytes 577544 | tf_op jit(solution)/shard_map/ppermute | solution.py:40
  220.6 2.0 fusion
  222.5 4.5 %all-to-all-start.1 = ((bf16[8,144,128]{2,1,0:T(8,128)(2,1)}), bf16[8,144,128]{2,1,0:T(8,128)(2,1)}, u32[]{:S(2)}, u32[]{:S(2)}) async-start(bf16[8,144,128]{2,1,0:T(8,128)(2,1)} %bitcast.23), calls=%async_computation.1 | async-start | bytes 589824 | tf_op jit(solution)/shard_map/all_to_all | solution.py:794
  227.6 3.8 %collective-permute-start.37 = (bf16[576,256]{1,0:T(8,128)(2,1)}, bf16[576,256]{1,0:T(8,128)(2,1)}, u32[]{:S(2)}, u32[]{:S(2)}) collective-permute-start(bf16[576,256]{1,0:T(8,128)(2,1)} %get-tuple-element.205), channel_id=1, source_target_pairs={{0,0},{8,1},{14,2},{6,3},{2,4},{10,5},{12,6},{4,7},{1,8},{9,9},{15... | collective-permute-start | bytes 884744 | tf_op jit(solution)/shard_map/ppermute | solution.py:40
  231.4 3.0 %collective-permute-start.38 = (bf16[576,256]{1,0:T(8,128)(2,1)}, bf16[576,256]{1,0:T(8,128)(2,1)}, u32[]{:S(2)}, u32[]{:S(2)}) collective-permute-start(bf16[576,256]{1,0:T(8,128)(2,1)} %get-tuple-element.206), channel_id=1, source_target_pairs={{6,0},{14,1},{8,2},{0,3},{4,4},{12,5},{10,6},{2,7},{7,8},{15,9},{9... | collective-permute-start | bytes 884744 | tf_op jit(solution)/shard_map/ppermute | solution.py:40
  235.8 3.3 %shard_map.221 = (f32[144,1536]{1,0:T(8,128)}, f32[144,1536]{1,0:T(8,128)}, f32[144,576]{1,0:T(8,128)}, f32[576,384]{1,0:T(8,128)}) custom-call(s32[2]{0:T(128)} %pad_add_fusion.1.sc, bf16[752,128]{1,0:T(8,128)(2,1)} %shard_map.218.refs_0_, bf16[752,128]{1,0:T(8,128)(2,1)} %copy-done.15, bf16[752,128]{1,0:T(8,128)(2,1)} %copy-done.14, ...), custom_call_target="tpu_custom_call" | custom-call | flops 3449999872 | tf_op jit(solution)/shard_map/pallas_call | solution.py:741
  239.1 9.8 %all-to-all-done.1.got = bf16[8,144,128]{2,1,0:T(8,128)(2,1)} async-done(((bf16[8,144,128]{2,1,0:T(8,128)(2,1)}), bf16[8,144,128]{2,1,0:T(8,128)(2,1)}, u32[]{:S(2)}, u32[]{:S(2)}) %all-to-all-start.1) | async-done | bytes 294944 | tf_op jit(solution)/shard_map/all_to_all | solution.py:794
  248.8 1.7 shard_map.219
  250.6 4.1 %all-to-all-start.2 = ((bf16[8,144,128]{2,1,0:T(8,128)(2,1)}), bf16[8,144,128]{2,1,0:T(8,128)(2,1)}, u32[]{:S(2)}, u32[]{:S(2)}) async-start(bf16[8,144,128]{2,1,0:T(8,128)(2,1)} %shard_map.219), calls=%async_computation.2 | async-start | bytes 589824 | tf_op jit(solution)/shard_map/all_to_all | solution.py:802
  254.6 1.3 broadcast_select_fusion.1
  257.7 5.4 %all-to-all-done.2 = bf16[8,144,128]{2,1,0:T(8,128)(2,1)} async-done(((bf16[8,144,128]{2,1,0:T(8,128)(2,1)}), bf16[8,144,128]{2,1,0:T(8,128)(2,1)}, u32[]{:S(2)}, u32[]{:S(2)}) %all-to-all-start.2) | async-done | bytes 294944 | tf_op jit(solution)/shard_map/all_to_all | solution.py:802
  263.1 1.8 shard_map.220
  264.9 1.7 slice_reduce_fusion
  (108 shorter events, 14.5 us)
Async XLA Ops:
  1.2 2.0 copy-start.10
  1.2 2.1 copy-start.11
  1.2 2.2 copy-start.9
  4.5 20.6 %copy-start = (bf16[144,1024]{1,0:T(8,128)(2,1)}, bf16[144,1024]{1,0:T(8,128)(2,1)S(1)}, u32[]{:S(2)}) copy-start(bf16[144,1024]{1,0:T(8,128)(2,1)S(1)} %concatenate.16.refs_5_.refs_14_) | copy-start | bytes 884740
  4.5 11.0 %collective-permute-start = (bf16[144,1024]{1,0:T(8,128)(2,1)S(1)}, bf16[144,1024]{1,0:T(8,128)(2,1)S(1)}, u32[]{:S(2)}, u32[]{:S(2)}) collective-permute-start(bf16[144,1024]{1,0:T(8,128)(2,1)S(1)} %concatenate.16.refs_5_.refs_14_), channel_id=1, source_target_pairs={{0,16},{1,17},{2,18},{3,19},{4,20},{5,21},{6,22},{7,23},{8,24},{9,... | collective-permute-start | bytes 884744 | tf_op jit(solution)/shard_map/ppermute | solution.py:40
  7.6 17.6 %collective-permute-start.4 = (bf16[144,1024]{1,0:T(8,128)(2,1)S(1)}, bf16[144,1024]{1,0:T(8,128)(2,1)S(1)}, u32[]{:S(2)}, u32[]{:S(2)}) collective-permute-start(bf16[144,1024]{1,0:T(8,128)(2,1)S(1)} %concatenate.16.refs_5_.refs_14_), channel_id=1, source_target_pairs={{0,8},{1,9},{2,10},{3,11},{4,12},{5,13},{6,14},{7,15},{8,0},{9,1},... | collective-permute-start | bytes 884744 | tf_op jit(solution)/shard_map/ppermute | solution.py:40
  7.6 13.8 %collective-permute-start.2 = (bf16[592,256]{1,0:T(8,128)(2,1)}, bf16[592,256]{1,0:T(8,128)(2,1)S(1)}, u32[]{:S(2)}, u32[]{:S(2)}) collective-permute-start(bf16[592,256]{1,0:T(8,128)(2,1)} %get-tuple-element.122), channel_id=1, source_target_pairs={{0,0},{1,8},{2,14},{3,6},{4,2},{5,10},{6,12},{7,4},{8,1},{9,9},{10... | collective-permute-start | bytes 909320 | tf_op jit(solution)/shard_map/ppermute | solution.py:40
  9.2 15.0 %collective-permute-start.3 = (bf16[592,256]{1,0:T(8,128)(2,1)}, bf16[592,256]{1,0:T(8,128)(2,1)S(1)}, u32[]{:S(2)}, u32[]{:S(2)}) collective-permute-start(bf16[592,256]{1,0:T(8,128)(2,1)} %get-tuple-element.123), channel_id=1, source_target_pairs={{0,6},{1,14},{2,8},{3,0},{4,4},{5,12},{6,10},{7,2},{8,7},{9,15},{1... | collective-permute-start | bytes 909320 | tf_op jit(solution)/shard_map/ppermute | solution.py:40
  15.6 0.7 copy-start.4
  16.3 3.2 %collective-permute-start.1 = (bf16[144,1024]{1,0:T(8,128)(2,1)S(1)}, bf16[144,1024]{1,0:T(8,128)(2,1)S(1)}, u32[]{:S(2)}, u32[]{:S(2)}) collective-permute-start(bf16[144,1024]{1,0:T(8,128)(2,1)S(1)} %collective-permute-done.refs_6_.refs_15_), channel_id=1, source_target_pairs={{0,8},{1,9},{2,10},{3,11},{4,12},{5,13},{6,14},{7,15},{8,0},{9,1},... | collective-permute-start | bytes 884744 | tf_op jit(solution)/shard_map/ppermute | solution.py:40
  19.5 0.7 copy-start.6
  20.2 32.5 %collective-permute-start.12 = (bf16[144,3648]{1,0:T(8,128)(2,1)}, bf16[144,3648]{1,0:T(8,128)(2,1)}, u32[]{:S(2)}, u32[]{:S(2)}) collective-permute-start(bf16[144,3648]{1,0:T(8,128)(2,1)} %pad_maximum_fusion.refs_7_), channel_id=1, source_target_pairs={{0,16},{1,17},{2,18},{3,19},{4,20},{5,21},{6,22},{7,23},{8,24},{9,... | collective-permute-start | bytes 3151880 | tf_op jit(solution)/shard_map/ppermute | solution.py:40
  21.3 3.8 %copy-start.2 = (bf16[592,256]{1,0:T(8,128)(2,1)}, bf16[592,256]{1,0:T(8,128)(2,1)S(1)}, u32[]{:S(2)}) copy-start(bf16[592,256]{1,0:T(8,128)(2,1)S(1)} %collective-permute-done.2.refs_1_) | copy-start | bytes 909316
  24.2 1.0 copy-start.3
  25.2 0.7 copy-start.5
  31.0 7.8 %collective-permute-start.8 = (bf16[2,3,256,128]{3,2,1,0:T(8,128)(2,1)}, bf16[2,3,256,128]{3,2,1,0:T(8,128)(2,1)}, u32[]{:S(2)}, u32[]{:S(2)}) collective-permute-start(bf16[2,3,256,128]{3,2,1,0:T(8,128)(2,1)} %get-tuple-element.130.refs_3_.refs_6_), channel_id=1, source_target_pairs={{0,8},{1,9},{2,10},{3,11},{4,12},{5,13},{6,14},{7,15},{8,0},{9,1},... | collective-permute-start | bytes 1179656 | tf_op jit(solution)/shard_map/ppermute | solution.py:40
  31.1 16.2 %collective-permute-start.7 = (bf16[2,3,256,128]{3,2,1,0:T(8,128)(2,1)}, bf16[2,3,256,128]{3,2,1,0:T(8,128)(2,1)}, u32[]{:S(2)}, u32[]{:S(2)}) collective-permute-start(bf16[2,3,256,128]{3,2,1,0:T(8,128)(2,1)} %get-tuple-element.130.refs_3_.refs_6_), channel_id=1, source_target_pairs={{0,2},{1,3},{2,4},{3,5},{4,6},{5,7},{8,10},{9,11},{10,12},{11,13},... | collective-permute-start | bytes 1179656 | tf_op jit(solution)/shard_map/ppermute | solution.py:40
  47.3 8.1 %collective-permute-start.10 = (bf16[2,3,256,128]{3,2,1,0:T(8,128)(2,1)}, bf16[2,3,256,128]{3,2,1,0:T(8,128)(2,1)}, u32[]{:S(2)}, u32[]{:S(2)}) collective-permute-start(bf16[2,3,256,128]{3,2,1,0:T(8,128)(2,1)} %collective-permute-done.7.refs_3_.refs_6_), channel_id=1, source_target_pairs={{0,8},{1,9},{2,10},{3,11},{4,12},{5,13},{6,14},{7,15},{8,0},{9,1},... | collective-permute-start | bytes 1179656 | tf_op jit(solution)/shard_map/ppermute | solution.py:40
  49.4 12.0 %collective-permute-start.9 = (bf16[2,3,256,128]{3,2,1,0:T(8,128)(2,1)}, bf16[2,3,256,128]{3,2,1,0:T(8,128)(2,1)}, u32[]{:S(2)}, u32[]{:S(2)}) collective-permute-start(bf16[2,3,256,128]{3,2,1,0:T(8,128)(2,1)} %collective-permute-done.7.refs_3_.refs_6_), channel_id=1, source_target_pairs={{0,2},{1,3},{2,4},{3,5},{4,6},{5,7},{8,10},{9,11},{10,12},{11,13},... | collective-permute-start | bytes 1179656 | tf_op jit(solution)/shard_map/ppermute | solution.py:40
  52.5 22.5 %collective-permute-start.13 = (bf16[144,3648]{1,0:T(8,128)(2,1)}, bf16[144,3648]{1,0:T(8,128)(2,1)}, u32[]{:S(2)}, u32[]{:S(2)}) collective-permute-start(bf16[144,3648]{1,0:T(8,128)(2,1)} %pad_maximum_fusion.refs_7_), channel_id=1, source_target_pairs={{0,8},{1,9},{2,10},{3,11},{4,12},{5,13},{6,14},{7,15},{8,0},{9,1},... | collective-permute-start | bytes 3151880 | tf_op jit(solution)/shard_map/ppermute | solution.py:40
  52.7 22.3 %collective-permute-start.14 = (bf16[144,3648]{1,0:T(8,128)(2,1)}, bf16[144,3648]{1,0:T(8,128)(2,1)}, u32[]{:S(2)}, u32[]{:S(2)}) collective-permute-start(bf16[144,3648]{1,0:T(8,128)(2,1)} %collective-permute-done.12.refs_8_), channel_id=1, source_target_pairs={{0,8},{1,9},{2,10},{3,11},{4,12},{5,13},{6,14},{7,15},{8,0},{9,1},... | collective-permute-start | bytes 3151880 | tf_op jit(solution)/shard_map/ppermute | solution.py:40
  53.0 14.4 %collective-permute-start.15 = (bf16[576,384]{1,0:T(8,128)(2,1)}, bf16[576,384]{1,0:T(8,128)(2,1)}, u32[]{:S(2)}, u32[]{:S(2)}) collective-permute-start(bf16[576,384]{1,0:T(8,128)(2,1)} %bitcast.41), channel_id=1, source_target_pairs={{0,16},{1,17},{2,18},{3,19},{4,20},{5,21},{6,22},{7,23},{8,24},{9,... | collective-permute-start | bytes 1327112 | tf_op jit(solution)/shard_map/ppermute | solution.py:40
  55.4 12.0 %collective-permute-start.6 = (bf16[576,256]{1,0:T(8,128)(2,1)}, bf16[576,256]{1,0:T(8,128)(2,1)}, u32[]{:S(2)}, u32[]{:S(2)}) collective-permute-start(bf16[576,256]{1,0:T(8,128)(2,1)} %get-tuple-element.227), channel_id=1, source_target_pairs={{0,6},{1,14},{2,8},{3,0},{4,4},{5,12},{6,10},{7,2},{8,7},{9,15},{1... | collective-permute-start | bytes 884744 | tf_op jit(solution)/shard_map/ppermute | solution.py:40
  61.4 6.5 %collective-permute-start.11 = (bf16[2,3,256,128]{3,2,1,0:T(8,128)(2,1)}, bf16[2,3,256,128]{3,2,1,0:T(8,128)(2,1)}, u32[]{:S(2)}, u32[]{:S(2)}) collective-permute-start(bf16[2,3,256,128]{3,2,1,0:T(8,128)(2,1)} %collective-permute-done.9.refs_3_.refs_6_), channel_id=1, source_target_pairs={{0,8},{1,9},{2,10},{3,11},{4,12},{5,13},{6,14},{7,15},{8,0},{9,1},... | collective-permute-start | bytes 1179656 | tf_op jit(solution)/shard_map/ppermute | solution.py:40
  67.4 7.5 %collective-permute-start.16 = (bf16[576,384]{1,0:T(8,128)(2,1)}, bf16[576,384]{1,0:T(8,128)(2,1)}, u32[]{:S(2)}, u32[]{:S(2)}) collective-permute-start(bf16[576,384]{1,0:T(8,128)(2,1)} %bitcast.42), channel_id=1, source_target_pairs={{0,8},{1,9},{2,10},{3,11},{4,12},{5,13},{6,14},{7,15},{8,0},{9,1},... | collective-permute-start | bytes 1327112 | tf_op jit(solution)/shard_map/ppermute | solution.py:40
  67.4 7.5 %collective-permute-start.17 = (bf16[576,384]{1,0:T(8,128)(2,1)}, bf16[576,384]{1,0:T(8,128)(2,1)}, u32[]{:S(2)}, u32[]{:S(2)}) collective-permute-start(bf16[576,384]{1,0:T(8,128)(2,1)} %collective-permute-done.15.refs_12_), channel_id=1, source_target_pairs={{0,8},{1,9},{2,10},{3,11},{4,12},{5,13},{6,14},{7,15},{8,0},{9,1},... | collective-permute-start | bytes 1327112 | tf_op jit(solution)/shard_map/ppermute | solution.py:40
  67.9 7.0 %collective-permute-start.5 = (bf16[576,256]{1,0:T(8,128)(2,1)}, bf16[576,256]{1,0:T(8,128)(2,1)}, u32[]{:S(2)}, u32[]{:S(2)}) collective-permute-start(bf16[576,256]{1,0:T(8,128)(2,1)} %get-tuple-element.228), channel_id=1, source_target_pairs={{0,0},{1,8},{2,14},{3,6},{4,2},{5,10},{6,12},{7,4},{8,1},{9,9},{10... | collective-permute-start | bytes 884744 | tf_op jit(solution)/shard_map/ppermute | solution.py:40
  93.8 28.0 %collective-permute-start.18 = (bf16[2,6016,128]{2,1,0:T(8,128)(2,1)}, bf16[2,6016,128]{2,1,0:T(8,128)(2,1)}, u32[]{:S(2)}, u32[]{:S(2)}) collective-permute-start(bf16[2,6016,128]{2,1,0:T(8,128)(2,1)} %get-tuple-element.150), channel_id=1, source_target_pairs={{0,8},{1,9},{2,10},{3,11},{4,12},{5,13},{6,14},{7,15},{8,0},{9,1},... | collective-permute-start | bytes 9240584 | tf_op jit(solution)/shard_map/ppermute | solution.py:40
  99.0 2.2 collective-permute-start.19
  99.0 2.3 collective-permute-start.20
  101.2 0.7 copy-start.8
  103.9 26.7 %collective-permute-start.24 = (bf16[576,256]{1,0:T(8,128)(2,1)}, bf16[576,256]{1,0:T(8,128)(2,1)}, u32[]{:S(2)}, u32[]{:S(2)}) collective-permute-start(bf16[576,256]{1,0:T(8,128)(2,1)} %get-tuple-element.169), channel_id=1, source_target_pairs={{0,0},{8,1},{14,2},{6,3},{2,4},{10,5},{12,6},{4,7},{1,8},{9,9},{15... | collective-permute-start | bytes 884744 | tf_op jit(solution)/shard_map/ppermute | solution.py:40
  107.6 29.2 %collective-permute-start.25 = (bf16[576,256]{1,0:T(8,128)(2,1)}, bf16[576,256]{1,0:T(8,128)(2,1)}, u32[]{:S(2)}, u32[]{:S(2)}) collective-permute-start(bf16[576,256]{1,0:T(8,128)(2,1)} %get-tuple-element.170), channel_id=1, source_target_pairs={{6,0},{14,1},{8,2},{0,3},{4,4},{12,5},{10,6},{2,7},{7,8},{15,9},{9... | collective-permute-start | bytes 884744 | tf_op jit(solution)/shard_map/ppermute | solution.py:40
  125.0 18.6 %collective-permute-start.23 = (bf16[2,3,256,128]{3,2,1,0:T(8,128)(2,1)}, bf16[2,3,256,128]{3,2,1,0:T(8,128)(2,1)}, u32[]{:S(2)}, u32[]{:S(2)}) collective-permute-start(bf16[2,3,256,128]{3,2,1,0:T(8,128)(2,1)} %shard_map.211), channel_id=1, source_target_pairs={{2,0},{3,1},{4,2},{5,3},{6,4},{7,5},{10,8},{11,9},{12,10},{13,11},... | collective-permute-start | bytes 1179656 | tf_op jit(solution)/shard_map/ppermute | solution.py:40
  126.3 19.5 %collective-permute-start.26 = (bf16[2,1504,128]{2,1,0:T(8,128)(2,1)}, bf16[2,1504,128]{2,1,0:T(8,128)(2,1)}, u32[]{:S(2)}, u32[]{:S(2)}) collective-permute-start(bf16[2,1504,128]{2,1,0:T(8,128)(2,1)} %get-tuple-element.173), channel_id=1, source_target_pairs={{0,16},{1,17},{2,18},{3,19},{4,20},{5,21},{6,22},{7,23},{8,24},{9,... | collective-permute-start | bytes 2310152 | tf_op jit(solution)/shard_map/ppermute | solution.py:40
  126.3 21.7 %collective-permute-start.27 = (bf16[2,1504,128]{2,1,0:T(8,128)(2,1)}, bf16[2,1504,128]{2,1,0:T(8,128)(2,1)}, u32[]{:S(2)}, u32[]{:S(2)}) collective-permute-start(bf16[2,1504,128]{2,1,0:T(8,128)(2,1)} %get-tuple-element.174), channel_id=1, source_target_pairs={{0,1},{1,0},{2,3},{3,2},{4,5},{5,4},{6,7},{7,6},{8,9},{9,8},{10,11... | collective-permute-start | bytes 2310152 | tf_op jit(solution)/shard_map/ppermute | solution.py:40
  130.6 6.2 %collective-permute-start.21 = (bf16[3,256,128]{2,1,0:T(8,128)(2,1)}, bf16[3,256,128]{2,1,0:T(8,128)(2,1)S(1)}, u32[]{:S(2)}, u32[]{:S(2)}) collective-permute-start(bf16[3,256,128]{2,1,0:T(8,128)(2,1)} %get-tuple-element.165), channel_id=1, source_target_pairs={{0,8},{1,9},{2,10},{3,11},{4,12},{5,13},{6,14},{7,15},{8,0},{9,1},... | collective-permute-start | bytes 589832 | tf_op jit(solution)/shard_map/ppermute | solution.py:40
  136.8 1.8 collective-permute-start.22
  136.8 6.7 %copy-start.7 = (bf16[3,256,128]{2,1,0:T(8,128)(2,1)}, bf16[3,256,128]{2,1,0:T(8,128)(2,1)S(1)}, u32[]{:S(2)}) copy-start(bf16[3,256,128]{2,1,0:T(8,128)(2,1)S(1)} %collective-permute-done.21.twin_a) | copy-start | bytes 589828
  151.7 13.3 %collective-permute-start.28 = (bf16[1504,128]{1,0:T(8,128)(2,1)}, bf16[1504,128]{1,0:T(8,128)(2,1)}, u32[]{:S(2)}, u32[]{:S(2)}) collective-permute-start(bf16[1504,128]{1,0:T(8,128)(2,1)} %get-tuple-element.181), channel_id=1, source_target_pairs={{0,1},{1,0},{2,3},{3,2},{4,5},{5,4},{6,7},{7,6},{8,9},{9,8},{10,11... | collective-permute-start | bytes 1155080 | tf_op jit(solution)/shard_map/ppermute | solution.py:40
  152.3 12.7 %collective-permute-start.29 = (bf16[1504,128]{1,0:T(8,128)(2,1)}, bf16[1504,128]{1,0:T(8,128)(2,1)}, u32[]{:S(2)}, u32[]{:S(2)}) collective-permute-start(bf16[1504,128]{1,0:T(8,128)(2,1)} %get-tuple-element.183), channel_id=1, source_target_pairs={{0,16},{1,17},{2,18},{3,19},{4,20},{5,21},{6,22},{7,23},{8,24},{9,... | collective-permute-start | bytes 1155080 | tf_op jit(solution)/shard_map/ppermute | solution.py:40
  152.3 23.8 %collective-permute-start.32 = (bf16[2,3,256,128]{3,2,1,0:T(8,128)(2,1)}, bf16[2,3,256,128]{3,2,1,0:T(8,128)(2,1)}, u32[]{:S(2)}, u32[]{:S(2)}) collective-permute-start(bf16[2,3,256,128]{3,2,1,0:T(8,128)(2,1)} %shard_map.215), channel_id=1, source_target_pairs={{2,0},{3,1},{4,2},{5,3},{6,4},{7,5},{10,8},{11,9},{12,10},{13,11},... | collective-permute-start | bytes 1179656 | tf_op jit(solution)/shard_map/ppermute | solution.py:40
  162.4 13.7 %collective-permute-start.30 = (bf16[3,256,128]{2,1,0:T(8,128)(2,1)}, bf16[3,256,128]{2,1,0:T(8,128)(2,1)S(1)}, u32[]{:S(2)}, u32[]{:S(2)}) collective-permute-start(bf16[3,256,128]{2,1,0:T(8,128)(2,1)} %get-tuple-element.198), channel_id=1, source_target_pairs={{0,8},{1,9},{2,10},{3,11},{4,12},{5,13},{6,14},{7,15},{8,0},{9,1},... | collective-permute-start | bytes 589832 | tf_op jit(solution)/shard_map/ppermute | solution.py:40
  164.9 11.2 %collective-permute-start.31 = (bf16[3,256,128]{2,1,0:T(8,128)(2,1)}, bf16[3,256,128]{2,1,0:T(8,128)(2,1)}, u32[]{:S(2)}, u32[]{:S(2)}) collective-permute-start(bf16[3,256,128]{2,1,0:T(8,128)(2,1)} %get-tuple-element.199), channel_id=1, source_target_pairs={{0,8},{1,9},{2,10},{3,11},{4,12},{5,13},{6,14},{7,15},{8,0},{9,1},... | collective-permute-start | bytes 589832 | tf_op jit(solution)/shard_map/ppermute | solution.py:40
  167.4 29.3 %all-to-all-start = ((bf16[4,752,128]{2,1,0:T(8,128)(2,1)}), bf16[4,752,128]{2,1,0:T(8,128)(2,1)}, u32[]{:S(2)}, u32[]{:S(2)}) async-start(bf16[4,752,128]{2,1,0:T(8,128)(2,1)} %bitcast.37), calls=%async_computation | async-start | bytes 1540096 | tf_op jit(solution)/shard_map/all_to_all | solution.py:794
  183.7 2.3 collective-permute-start.33
  185.9 10.8 %copy-start.1 = (bf16[2,1152,128]{2,1,0:T(8,128)(2,1)}, bf16[2,1152,128]{2,1,0:T(8,128)(2,1)S(1)}, u32[]{:S(2)}) copy-start(bf16[2,1152,128]{2,1,0:T(8,128)(2,1)S(1)} %collective-permute-done.33) | copy-start | bytes 1769476
  198.5 22.1 %collective-permute-start.39 = (bf16[1152,128]{1,0:T(8,128)(2,1)}, bf16[1152,128]{1,0:T(8,128)(2,1)}, u32[]{:S(2)}, u32[]{:S(2)}) collective-permute-start(bf16[1152,128]{1,0:T(8,128)(2,1)} %fusion.1), channel_id=1, source_target_pairs={{0,16},{1,17},{2,18},{3,19},{4,20},{5,21},{6,22},{7,23},{8,24},{9,... | collective-permute-start | bytes 884744 | tf_op jit(solution)/shard_map/ppermute | solution.py:40
  200.4 7.9 %collective-permute-start.36 = (bf16[752,128]{1,0:T(8,128)(2,1)}, bf16[752,128]{1,0:T(8,128)(2,1)S(1)}, u32[]{:S(2)}, u32[]{:S(2)}) collective-permute-start(bf16[752,128]{1,0:T(8,128)(2,1)} %shard_map.218.refs_0_), channel_id=1, source_target_pairs={{0,6},{1,7},{2,0},{3,1},{4,2},{5,3},{6,4},{7,5},{8,14},{9,15},{10,... | collective-permute-start | bytes 577544 | tf_op jit(solution)/shard_map/ppermute | solution.py:40
  201.6 15.6 %collective-permute-start.35 = (bf16[752,128]{1,0:T(8,128)(2,1)}, bf16[752,128]{1,0:T(8,128)(2,1)S(1)}, u32[]{:S(2)}, u32[]{:S(2)}) collective-permute-start(bf16[752,128]{1,0:T(8,128)(2,1)} %shard_map.218.refs_0_), channel_id=1, source_target_pairs={{0,4},{1,5},{2,6},{3,7},{4,0},{5,1},{6,2},{7,3},{8,12},{9,13},{10,... | collective-permute-start | bytes 577544 | tf_op jit(solution)/shard_map/ppermute | solution.py:40
  201.6 18.9 %collective-permute-start.34 = (bf16[752,128]{1,0:T(8,128)(2,1)}, bf16[752,128]{1,0:T(8,128)(2,1)S(1)}, u32[]{:S(2)}, u32[]{:S(2)}) collective-permute-start(bf16[752,128]{1,0:T(8,128)(2,1)} %shard_map.218.refs_0_), channel_id=1, source_target_pairs={{0,2},{1,3},{2,4},{3,5},{4,6},{5,7},{6,0},{7,1},{8,10},{9,11},{10,... | collective-permute-start | bytes 577544 | tf_op jit(solution)/shard_map/ppermute | solution.py:40
  202.4 29.0 %collective-permute-start.40 = (bf16[752,128]{1,0:T(8,128)(2,1)}, bf16[752,128]{1,0:T(8,128)(2,1)S(1)}, u32[]{:S(2)}, u32[]{:S(2)}) collective-permute-start(bf16[752,128]{1,0:T(8,128)(2,1)} %shard_map.218.refs_0_), channel_id=1, source_target_pairs={{0,1},{1,0},{2,3},{3,2},{4,5},{5,4},{6,7},{7,6},{8,9},{9,8},{10,11... | collective-permute-start | bytes 577544 | tf_op jit(solution)/shard_map/ppermute | solution.py:40
  208.3 27.5 %copy-start.13 = (bf16[752,128]{1,0:T(8,128)(2,1)}, bf16[752,128]{1,0:T(8,128)(2,1)S(1)}, u32[]{:S(2)}) copy-start(bf16[752,128]{1,0:T(8,128)(2,1)S(1)} %collective-permute-done.36.refs_3_) | copy-start | bytes 577540
  208.3 26.1 %collective-permute-start.43 = (bf16[752,128]{1,0:T(8,128)(2,1)S(1)}, bf16[752,128]{1,0:T(8,128)(2,1)S(1)}, u32[]{:S(2)}, u32[]{:S(2)}) collective-permute-start(bf16[752,128]{1,0:T(8,128)(2,1)S(1)} %collective-permute-done.36.refs_3_), channel_id=1, source_target_pairs={{0,1},{1,0},{2,3},{3,2},{4,5},{5,4},{6,7},{7,6},{8,9},{9,8},{10,11... | collective-permute-start | bytes 577544 | tf_op jit(solution)/shard_map/ppermute | solution.py:40
  217.2 17.2 %copy-start.14 = (bf16[752,128]{1,0:T(8,128)(2,1)}, bf16[752,128]{1,0:T(8,128)(2,1)S(1)}, u32[]{:S(2)}) copy-start(bf16[752,128]{1,0:T(8,128)(2,1)S(1)} %collective-permute-done.35.refs_2_) | copy-start | bytes 577540
  217.2 17.2 %collective-permute-start.42 = (bf16[752,128]{1,0:T(8,128)(2,1)S(1)}, bf16[752,128]{1,0:T(8,128)(2,1)S(1)}, u32[]{:S(2)}, u32[]{:S(2)}) collective-permute-start(bf16[752,128]{1,0:T(8,128)(2,1)S(1)} %collective-permute-done.35.refs_2_), channel_id=1, source_target_pairs={{0,1},{1,0},{2,3},{3,2},{4,5},{5,4},{6,7},{7,6},{8,9},{9,8},{10,11... | collective-permute-start | bytes 577544 | tf_op jit(solution)/shard_map/ppermute | solution.py:40
  220.5 14.0 %copy-start.15 = (bf16[752,128]{1,0:T(8,128)(2,1)}, bf16[752,128]{1,0:T(8,128)(2,1)S(1)}, u32[]{:S(2)}) copy-start(bf16[752,128]{1,0:T(8,128)(2,1)S(1)} %collective-permute-done.34.refs_1_) | copy-start | bytes 577540
  220.5 15.3 %collective-permute-start.41 = (bf16[752,128]{1,0:T(8,128)(2,1)S(1)}, bf16[752,128]{1,0:T(8,128)(2,1)}, u32[]{:S(2)}, u32[]{:S(2)}) collective-permute-start(bf16[752,128]{1,0:T(8,128)(2,1)S(1)} %collective-permute-done.34.refs_1_), channel_id=1, source_target_pairs={{0,1},{1,0},{2,3},{3,2},{4,5},{5,4},{6,7},{7,6},{8,9},{9,8},{10,11... | collective-permute-start | bytes 577544 | tf_op jit(solution)/shard_map/ppermute | solution.py:40
  222.5 26.3 %all-to-all-start.1 = ((bf16[8,144,128]{2,1,0:T(8,128)(2,1)}), bf16[8,144,128]{2,1,0:T(8,128)(2,1)}, u32[]{:S(2)}, u32[]{:S(2)}) async-start(bf16[8,144,128]{2,1,0:T(8,128)(2,1)} %bitcast.23), calls=%async_computation.1 | async-start | bytes 589824 | tf_op jit(solution)/shard_map/all_to_all | solution.py:794
  227.6 27.0 %collective-permute-start.37 = (bf16[576,256]{1,0:T(8,128)(2,1)}, bf16[576,256]{1,0:T(8,128)(2,1)}, u32[]{:S(2)}, u32[]{:S(2)}) collective-permute-start(bf16[576,256]{1,0:T(8,128)(2,1)} %get-tuple-element.205), channel_id=1, source_target_pairs={{0,0},{8,1},{14,2},{6,3},{2,4},{10,5},{12,6},{4,7},{1,8},{9,9},{15... | collective-permute-start | bytes 884744 | tf_op jit(solution)/shard_map/ppermute | solution.py:40
  231.4 3.1 %copy-start.16 = (bf16[752,128]{1,0:T(8,128)(2,1)}, bf16[752,128]{1,0:T(8,128)(2,1)S(1)}, u32[]{:S(2)}) copy-start(bf16[752,128]{1,0:T(8,128)(2,1)S(1)} %collective-permute-done.40.refs_4_) | copy-start | bytes 577540
  231.4 23.2 %collective-permute-start.38 = (bf16[576,256]{1,0:T(8,128)(2,1)}, bf16[576,256]{1,0:T(8,128)(2,1)}, u32[]{:S(2)}, u32[]{:S(2)}) collective-permute-start(bf16[576,256]{1,0:T(8,128)(2,1)} %get-tuple-element.206), channel_id=1, source_target_pairs={{6,0},{14,1},{8,2},{0,3},{4,4},{12,5},{10,6},{2,7},{7,8},{15,9},{9... | collective-permute-start | bytes 884744 | tf_op jit(solution)/shard_map/ppermute | solution.py:40
  235.1 0.7 copy-start.18
  250.6 12.5 %all-to-all-start.2 = ((bf16[8,144,128]{2,1,0:T(8,128)(2,1)}), bf16[8,144,128]{2,1,0:T(8,128)(2,1)}, u32[]{:S(2)}, u32[]{:S(2)}) async-start(bf16[8,144,128]{2,1,0:T(8,128)(2,1)} %shard_map.219), calls=%async_computation.2 | async-start | bytes 589824 | tf_op jit(solution)/shard_map/all_to_all | solution.py:802
  (2 other events, 1.3 us)

commit v3 on v2

--- a/solution.py
+++ b/solution.py
@@ -154,7 +154,7 @@
         place = sc[q] * rows + lax.broadcasted_iota(jnp.int32, (1, rows), 1)
         bias[...] = bias_of(place - pos[q], place, block_id, rows, rows)
         for c in range(KV_HEADS):
-            seen = dot(held[k, c], qz[q, c], 1, 0) + jnp.concatenate([bias[...]] * GROUP, axis=1)
+            seen = dot(held[k, c, :, :HEAD_DIM], qz[q, c], 1, 0) + jnp.concatenate([bias[...]] * GROUP, axis=1)
             old = peak[q, c]
             new = jnp.maximum(old, jnp.max(seen, axis=0, keepdims=True))
             expo = jnp.exp(seen - new)
@@ -192,13 +192,15 @@
     def work(q, k, block_id):
         place = sc[q] * rows + lax.broadcasted_iota(jnp.int32, (1, rows), 1)
         bias[...] = bias_of(place - pos[q], place, block_id, rows, rows)
-        scores = [dot(held[k, c], qz[q, c], 1, 0) for c in range(KV_HEADS)]
         for c in range(KV_HEADS):
-            seen = scores[c] + jnp.concatenate([bias[...]] * GROUP, axis=1)
+            block = held[k, c]
+            keys, values = block[:, :HEAD_DIM], block[:, HEAD_DIM:]
+            seen = dot(keys, qz[q, c], 1, 0) + jnp.concatenate([bias[...]] * GROUP, axis=1)
             probs = jnp.exp(seen - lse[q, c])
-            d_scores = (probs * (dot(held[k, c], gz[q, c], 1, 0) - delta[q, c])).astype(BF16)
-            dkv[k, c] += dot(d_scores, qz[q, c], 1, 1) + dot(probs.astype(BF16), gz[q, c], 1, 1)
-            dq[q, c] += dot(held[k, c].T[:HEAD_DIM], d_scores, 1, 0)
+            d_scores = (probs * (dot(values, gz[q, c], 1, 0) - delta[q, c])).astype(BF16)
+            d_both = [dot(d_scores, qz[q, c], 1, 1), dot(probs.astype(BF16), gz[q, c], 1, 1)]
+            dkv[k, c] += jnp.concatenate(d_both, axis=1)
+            dq[q, c] += dot(block.T[:HEAD_DIM], d_scores, 1, 0)
 
     each_pair(sc, stage, work)
     own[...] = dkv[:2].astype(own_type)
@@ -224,7 +226,7 @@
     return pl.CostEstimate(flops=int(us * 1.15e9), bytes_accessed=0, transcendentals=0)
 
 
-LIMIT = pltpu.CompilerParams(vmem_limit_bytes=(64 << 20) - (256 << 10))
+LIMIT = pltpu.CompilerParams(vmem_limit_bytes=64 << 20)
 
 
 def attend_forward(stage, sc, pos, qz, pieces, carried, last):
@@ -378,8 +380,7 @@
             rb = (b * c + a * s).astype(BF16) * jnp.asarray(HEAD_DIM**-0.5, BF16)
             group, lanes = h // GROUP, slice(h % GROUP * rows, (h % GROUP + 1) * rows)
             qz[q, group, :half, lanes] = ra
-            qz[q, group, half : 2 * half, lanes] = rb
-            qz[q, group, 2 * half :, lanes] = jnp.zeros((2 * half, rows), BF16)
+            qz[q, group, half:, lanes] = rb
         for k in range(KV_HEADS):
             row = width + 64 * k
             a = made[row : row + half]
@@ -395,7 +396,7 @@
     count = 2 * rows
     width = HEADS * HEAD_DIM
     out_shape = (
-        jax.ShapeDtypeStruct((2, KV_HEADS, 2 * HEAD_DIM, GROUP * rows), BF16),
+        jax.ShapeDtypeStruct((2, KV_HEADS, HEAD_DIM, GROUP * rows), BF16),
         jax.ShapeDtypeStruct((2, KV_HEADS, rows, 2 * HEAD_DIM), BF16),
         jax.ShapeDtypeStruct((width, count), BF16),
         jax.ShapeDtypeStruct((width, 128), BF16),
@@ -555,8 +556,7 @@
             at = slice(q * rows, (q + 1) * rows)
             part = d_mix[64 * h : 64 * h + 64, at]
             group, lanes = h // GROUP, slice(h % GROUP * rows, (h % GROUP + 1) * rows)
-            gz[q, group, :64, lanes] = jnp.zeros((64, rows), BF16)
-            gz[q, group, 64:, lanes] = part
+            gz[q, group, :, lanes] = part
             delta[q, group, :, lanes] = jnp.sum(
                 part.astype(F32) * att_t[64 * h : 64 * h + 64, at].astype(F32),
                 axis=0,
@@ -581,7 +581,7 @@
         jax.ShapeDtypeStruct((width, rows), BF16),
         jax.ShapeDtypeStruct((width, rows), BF16),
         jax.ShapeDtypeStruct((width, count), F32),
-        jax.ShapeDtypeStruct((2, KV_HEADS, 2 * HEAD_DIM, GROUP * rows), BF16),
+        jax.ShapeDtypeStruct((2, KV_HEADS, HEAD_DIM, GROUP * rows), BF16),
         jax.ShapeDtypeStruct((2, KV_HEADS, 1, GROUP * rows), F32),
         jax.ShapeDtypeStruct(packed, BF16),
         jax.ShapeDtypeStruct(packed, BF16),
@@ -710,6 +710,30 @@
             done += n
 
 
+def front_unpack_kernel(places, flat, *outs):
+    *outs, first, second = outs
+    unpack_kernel(places, flat, *outs)
+    rows = first.shape[1]
+    ends = flat[7 * rows : 8 * rows].astype(F32).T
+    first[...] = ends[64:65]
+    second[...] = ends[65:66]
+
+
+def front_unpack(flat, shard, widths):
+    places = [(0, shard, sum(widths[:i])) for i in range(len(widths))]
+    out_shape = tuple(jax.ShapeDtypeStruct((shard, n), F32) for n in widths)
+    out_shape += (jax.ShapeDtypeStruct((1, shard), F32),) * 2
+    return pl.pallas_call(
+        functools.partial(front_unpack_kernel, places),
+        out_shape=out_shape,
+        grid=(1,),
+        in_specs=wholes(flat),
+        out_specs=wholes(*out_shape),
+        compiler_params=LIMIT,
+        cost_estimate=takes(2),
+    )(flat)
+
+
 def join_unpack_kernel(places, parts, sc, *refs):
     pieces, outs, flat = refs[: 2 * parts], refs[2 * parts : -1], refs[-1]
     n = pieces[0].shape[0]
@@ -1065,24 +1089,18 @@
     else:
         late_grads = unpack(late, places)
     gate_grad, up_grad, output_grad, down_grad = late_grads
-    query_grad, key_grad, value_grad, ends = unpack(
-        front,
-        [
-            (0, shard, 0, width),
-            (0, shard, width, kv_width),
-            (0, shard, width + kv_width, kv_width),
-            (0, shard, width + 2 * kv_width, 64),
-        ],
+    query_grad, key_grad, value_grad, first_grad, second_grad = front_unpack(
+        front, shard, (width, kv_width, kv_width)
     )
     return (
         low_high(res_a, res_b, h).T[None],
         low_high(*tokens_grad, h).T[None],
-        ends[:, 0],
+        first_grad[0],
         query_grad,
         key_grad,
         value_grad,
         output_grad,
-        ends[:, 1],
+        second_grad[0],
         gate_grad,
         up_grad,
         down_grad.T,

time: 268 us -> 264 us (0.985)
  starting transfers between devices: 95.6 us -> 81.9 us
  waiting for transfers between devices: 63.4 us -> 68.7 us
  Pallas kernels: 85.2 us -> 89 us
    ppermute x44, starting transfers between devices: 78.3 us -> 64.8 us  [along(): return lambda a: lax.ppermute(a, AXES, pairs)]
    ppermute x44, waiting for transfers between devices: 37.4 us -> 42.8 us  [along(): return lambda a: lax.ppermute(a, AXES, pairs)]
  transfers between devices with their start and end apart: 47 -> 47, of which waited for: 16 -> 15; matrix products, arithmetic and copies ran while one was open for 4% -> 4% of each run, Pallas kernels for 22% -> 24%
where the time goes in v3:
time: 264 us; the launch traced here: 261 us
  Pallas kernels  89 us (34%)
  starting transfers between devices  81.9 us (31%)
  waiting for transfers between devices  68.7 us (26%)
  other arithmetic  13.1 us (5%)
  local copies, waits for them, and re-layouts  7.36 us (3%)
    ppermute x44, starting transfers between devices, along(): return lambda a: lax.ppermute(a, AXES, pairs)  64.8 us
    ppermute x44, waiting for transfers between devices, along(): return lambda a: lax.ppermute(a, AXES, pairs)  42.8 us
    all_to_all x2, waiting for transfers between devices, exchange(): return lax.all_to_all(parts, axes, 0, 0, tiled=True)  20.5 us
    pallas_call x1, Pallas kernels, feed(): pl.pallas_call(functools.partial(feed_kernel, fsdp, len(parts), ff // 4 i...  18.5 us
    pallas_call x3, Pallas kernels, attend_backward(): pl.pallas_call(functools.partial(backward_kernel, stage, first, own_type)...  18.4 us
    pallas_call x3, Pallas kernels, attend_forward(): pl.pallas_call(functools.partial(forward_kernel, stage, last), out_shape=...  16.4 us
    all_to_all x2, starting transfers between devices, exchange(): return lax.all_to_all(parts, axes, 0, 0, tiled=True)  13 us
    pallas_call x5, Pallas kernels, simple_call(): pl.pallas_call(kernel, out_shape=out_shape, grid=(1,), in_specs=wholes(*g...  10.2 us
  transfers between devices with their start and end apart: 47, of which 15 were waited for; matrix products, arithmetic and copies ran while one was open for 4% of the time, Pallas kernels for 24%

profile of v3, /device:TPU:0, one launch (start us, length us, event | category | flops | bytes accessed | tf_op | source)
XLA Modules:
  0.0 261.1 jit_solution(12444659480850784910)
XLA Ops:
  1.2 1.9 shard_map.203
  4.7 1.2 concatenate.16.refs_5_.refs_14_
  5.9 3.0 %collective-permute-start = (bf16[144,1024]{1,0:T(8,128)(2,1)S(1)}, bf16[144,1024]{1,0:T(8,128)(2,1)S(1)}, u32[]{:S(2)}, u32[]{:S(2)}) collective-permute-start(bf16[144,1024]{1,0:T(8,128)(2,1)S(1)} %concatenate.16.refs_5_.refs_14_), channel_id=1, source_target_pairs={{0,16},{1,17},{2,18},{3,19},{4,20},{5,21},{6,22},{7,23},{8,24},{9,... | collective-permute-start | bytes 884744 | tf_op jit(solution)/shard_map/ppermute | solution.py:40
  8.9 1.6 collective-permute-start.2
  10.5 6.4 %collective-permute-start.3 = (bf16[592,256]{1,0:T(8,128)(2,1)}, bf16[592,256]{1,0:T(8,128)(2,1)S(1)}, u32[]{:S(2)}, u32[]{:S(2)}) collective-permute-start(bf16[592,256]{1,0:T(8,128)(2,1)} %get-tuple-element.124), channel_id=1, source_target_pairs={{0,6},{1,14},{2,8},{3,0},{4,4},{5,12},{6,10},{7,2},{8,7},{9,15},{1... | collective-permute-start | bytes 909320 | tf_op jit(solution)/shard_map/ppermute | solution.py:40
  17.6 0.9 collective-permute-start.1
  18.5 2.3 pad_maximum_fusion.refs_7_
  22.6 2.8 %collective-permute-done.3.refs_2_ = bf16[592,256]{1,0:T(8,128)(2,1)S(1)} collective-permute-done((bf16[592,256]{1,0:T(8,128)(2,1)}, bf16[592,256]{1,0:T(8,128)(2,1)S(1)}, u32[]{:S(2)}, u32[]{:S(2)}) %collective-permute-start.3) | collective-permute-done | bytes 303136 | tf_op jit(solution)/shard_map/ppermute | solution.py:40
  25.5 1.0 multiply_sine_fusion
  27.2 4.8 %shard_map.204 = (bf16[2,3,64,768]{3,2,1,0:T(8,128)(2,1)}, bf16[2,3,256,128]{3,2,1,0:T(8,128)(2,1)}, bf16[576,512]{1,0:T(8,128)(2,1)}, bf16[576,128]{1,0:T(8,128)(2,1)}, s32[2,1,256]{2,1,0:T(1,128)}, /*index=5*/s32[8]{0:T(128)}) custom-call(s32[7]{0:T(128)} %stack.47.refs_0_, bf16[592,256]{1,0:T(8,128)(2,1)} %copy-done.2, bf16[592,256]{1,0:T(8,128)(2,1)} %copy-done.3, ...), custom_call_target="tpu_custom_call" | custom-call | tf_op jit(solution)/shard_map/pallas_call | solution.py:406
  32.1 7.7 %collective-permute-start.7 = (bf16[2,3,256,128]{3,2,1,0:T(8,128)(2,1)}, bf16[2,3,256,128]{3,2,1,0:T(8,128)(2,1)}, u32[]{:S(2)}, u32[]{:S(2)}) collective-permute-start(bf16[2,3,256,128]{3,2,1,0:T(8,128)(2,1)} %get-tuple-element.131.refs_3_.refs_6_), channel_id=1, source_target_pairs={{0,2},{1,3},{2,4},{3,5},{4,6},{5,7},{8,10},{9,11},{10,12},{11,13},... | collective-permute-start | bytes 1179656 | tf_op jit(solution)/shard_map/ppermute | solution.py:40
  39.8 10.2 %shard_map.205 = (f32[2,3,1,768]{3,2,1,0:T(1,128)}, f32[2,3,1,768]{3,2,1,0:T(1,128)}, f32[2,3,64,768]{3,2,1,0:T(8,128)}) custom-call(s32[8]{0:T(128)} %get-tuple-element.190.refs_0_, s32[2,1,256]{2,1,0:T(1,128)} %get-tuple-element.129.refs_1_, bf16[2,3,64,768]{3,2,1,0:T(8,128)(2,1)} %get-tuple-element.130.refs_2_, ...), custom_call_target="tpu_custom_call" | custom-call | tf_op jit(solution)/shard_map/pallas_call | solution.py:251
  50.2 3.3 %collective-permute-start.9 = (bf16[2,3,256,128]{3,2,1,0:T(8,128)(2,1)}, bf16[2,3,256,128]{3,2,1,0:T(8,128)(2,1)}, u32[]{:S(2)}, u32[]{:S(2)}) collective-permute-start(bf16[2,3,256,128]{3,2,1,0:T(8,128)(2,1)} %collective-permute-done.7.refs_3_.refs_6_), channel_id=1, source_target_pairs={{0,2},{1,3},{2,4},{3,5},{4,6},{5,7},{8,10},{9,11},{10,12},{11,13},... | collective-permute-start | bytes 1179656 | tf_op jit(solution)/shard_map/ppermute | solution.py:40
  54.5 1.9 broadcast_select_fusion.4
  56.4 2.6 %collective-permute-start.6 = (bf16[576,256]{1,0:T(8,128)(2,1)}, bf16[576,256]{1,0:T(8,128)(2,1)}, u32[]{:S(2)}, u32[]{:S(2)}) collective-permute-start(bf16[576,256]{1,0:T(8,128)(2,1)} %get-tuple-element.227), channel_id=1, source_target_pairs={{0,6},{1,14},{2,8},{3,0},{4,4},{5,12},{6,10},{7,2},{8,7},{9,15},{1... | collective-permute-start | bytes 884744 | tf_op jit(solution)/shard_map/ppermute | solution.py:40
  59.1 3.1 %shard_map.206 = (f32[2,3,1,768]{3,2,1,0:T(1,128)}, f32[2,3,1,768]{3,2,1,0:T(1,128)}, f32[2,3,64,768]{3,2,1,0:T(8,128)}) custom-call(s32[8]{0:T(128)} %get-tuple-element.190.refs_0_, s32[2,1,256]{2,1,0:T(1,128)} %get-tuple-element.129.refs_1_, ...), custom_call_target="tpu_custom_call", output_to_operand_aliasing={{0}: (5, {}), {1}: (6, {}), {2}: (7, {})} | custom-call | tf_op jit(solution)/shard_map/pallas_call | solution.py:251
  62.5 5.9 %collective-permute-done.6.refs_4_ = bf16[576,256]{1,0:T(8,128)(2,1)} collective-permute-done((bf16[576,256]{1,0:T(8,128)(2,1)}, bf16[576,256]{1,0:T(8,128)(2,1)}, u32[]{:S(2)}, u32[]{:S(2)}) %collective-permute-start.6) | collective-permute-done | bytes 294944 | tf_op jit(solution)/shard_map/ppermute | solution.py:40
  68.9 3.8 %collective-permute-start.5 = (bf16[576,256]{1,0:T(8,128)(2,1)}, bf16[576,256]{1,0:T(8,128)(2,1)}, u32[]{:S(2)}, u32[]{:S(2)}) collective-permute-start(bf16[576,256]{1,0:T(8,128)(2,1)} %get-tuple-element.228), channel_id=1, source_target_pairs={{0,0},{1,8},{2,14},{3,6},{4,2},{5,10},{6,12},{7,4},{8,1},{9,9},{10... | collective-permute-start | bytes 884744 | tf_op jit(solution)/shard_map/ppermute | solution.py:40
  72.7 3.1 %shard_map.207 = (bf16[2,3,64,768]{3,2,1,0:T(8,128)(2,1)}, f32[2,3,1,768]{3,2,1,0:T(1,128)}) custom-call(s32[8]{0:T(128)} %get-tuple-element.190.refs_0_, s32[2,1,256]{2,1,0:T(1,128)} %get-tuple-element.129.refs_1_, bf16[2,3,64,768]{3,2,1,0:T(8,128)(2,1)} %get-tuple-element.130.refs_2_, bf16[2,3,256,128]{3,2,1,0:T(8,128)(2,1)} %collective-permute-done.9.refs_3_.refs_6_, ...), custom_call_target="tpu_custom_call" | custom-call | tf_op jit(solution)/shard_map/pallas_call | solution.py:251
  75.8 18.5 %shard_map.208 = (bf16[576,256]{1,0:T(8,128)(2,1)}, bf16[576,256]{1,0:T(8,128)(2,1)}, f32[576,512]{1,0:T(8,128)}, bf16[2,3,64,768]{3,2,1,0:T(8,128)(2,1)}, f32[2...) custom-call(s32[7]{0:T(128)} %stack.47.refs_0_, ...), custom_call_target="tpu_custom_call" | custom-call | flops 21849999360 | tf_op jit(solution)/shard_map/pallas_call | solution.py:590
  94.4 1.6 collective-permute-start.18
  95.9 3.4 %shard_map.210 = (f32[2,3,64,768]{3,2,1,0:T(8,128)}, bf16[2,3,256,128]{3,2,1,0:T(8,128)(2,1)}, bf16[3,256,128]{2,1,0:T(8,128)(2,1)}, bf16[3,256,128]{2,1,0:T(8,128)(2,1)}) custom-call(s32[8]{0:T(128)} %get-tuple-element.190.refs_0_, s32[2,1,256]{2,1,0:T(1,128)} %get-tuple-element.129.refs_1_, bf16[2,3,64,768]{3,2,1,0:T(8,128)(2,1)} %get-tuple-element.130.refs_2_, ...), custom_call_target="tpu_custom_call" | custom-call | flops 4600000000 | tf_op jit(solution)/shard_map/pallas_call | solution.py:277
  99.8 1.9 collective-permute-done.19.twin_a
  102.0 2.0 shard_map.211
  104.0 3.8 %collective-permute-start.24 = (bf16[576,256]{1,0:T(8,128)(2,1)}, bf16[576,256]{1,0:T(8,128)(2,1)}, u32[]{:S(2)}, u32[]{:S(2)}) collective-permute-start(bf16[576,256]{1,0:T(8,128)(2,1)} %get-tuple-element.170), channel_id=1, source_target_pairs={{0,0},{8,1},{14,2},{6,3},{2,4},{10,5},{12,6},{4,7},{1,8},{9,9},{15... | collective-permute-start | bytes 884744 | tf_op jit(solution)/shard_map/ppermute | solution.py:40
  107.8 9.3 %collective-permute-start.25 = (bf16[576,256]{1,0:T(8,128)(2,1)}, bf16[576,256]{1,0:T(8,128)(2,1)}, u32[]{:S(2)}, u32[]{:S(2)}) collective-permute-start(bf16[576,256]{1,0:T(8,128)(2,1)} %get-tuple-element.171), channel_id=1, source_target_pairs={{6,0},{14,1},{8,2},{0,3},{4,4},{12,5},{10,6},{2,7},{7,8},{15,9},{9... | collective-permute-start | bytes 884744 | tf_op jit(solution)/shard_map/ppermute | solution.py:40
  117.2 3.1 %shard_map.209 = (bf16[2,1504,128]{2,1,0:T(8,128)(2,1)}, bf16[2,1504,128]{2,1,0:T(8,128)(2,1)}) custom-call(s32[1]{0:T(128)} %bitcast.13.x, bf16[2,6016,128]{2,1,0:T(8,128)(2,1)} %get-tuple-element.150.refs_0_.refs_1_.refs_2_.refs_3_, bf16[2,6016,128]{2,1,0:T(8,128)(2,1)} %get-tuple-element.150.refs_0_.refs_1_.refs_2_.refs_3_, ...), custom_call_target="tpu_custom_call" | custom-call | tf_op jit(solution)/shard_map/pallas_call | solution.py:861
  120.3 1.3 collective-permute-start.23
  121.6 1.7 collective-permute-start.26
  123.2 3.6 %shard_map.212 = (f32[2,3,64,768]{3,2,1,0:T(8,128)}, bf16[2,3,256,128]{3,2,1,0:T(8,128)(2,1)}, bf16[3,256,128]{2,1,0:T(8,128)(2,1)}, bf16[3,256,128]{2,1,0:T(8,128)(2,1)}) custom-call(s32[8]{0:T(128)} %get-tuple-element.190.refs_0_, s32[2,1,256]{2,1,0:T(1,128)} %get-tuple-element.129.refs_1_, ...), custom_call_target="tpu_custom_call", output_to_operand_aliasing={{0}: (8, {})} | custom-call | flops 16099999744 | tf_op jit(solution)/shard_map/pallas_call | solution.py:277
  126.8 0.9 collective-permute-start.21
  127.8 6.7 %collective-permute-done.25 = bf16[576,256]{1,0:T(8,128)(2,1)} collective-permute-done((bf16[576,256]{1,0:T(8,128)(2,1)}, bf16[576,256]{1,0:T(8,128)(2,1)}, u32[]{:S(2)}, u32[]{:S(2)}) %collective-permute-start.25) | collective-permute-done | bytes 294944 | tf_op jit(solution)/shard_map/ppermute | solution.py:40
  134.4 1.8 collective-permute-done.22.twin_b
  136.2 5.5 %collective-permute-done.23.refs_0_ = bf16[2,3,256,128]{3,2,1,0:T(8,128)(2,1)} collective-permute-done((bf16[2,3,256,128]{3,2,1,0:T(8,128)(2,1)}, bf16[2,3,256,128]{3,2,1,0:T(8,128)(2,1)}, u32[]{:S(2)}, u32[]{:S(2)}) %collective-permute-start.23) | collective-permute-done | bytes 393248 | tf_op jit(solution)/shard_map/ppermute | solution.py:40
  141.7 2.2 shard_map.215
  143.9 1.7 collective-permute-done.27.refs_10_.refs_11_
  145.6 3.6 %shard_map.213 = (bf16[1504,128]{1,0:T(8,128)(2,1)}, bf16[1504,128]{1,0:T(8,128)(2,1)}, bf16[1504,128]{1,0:T(8,128)(2,1)}, bf16[1504,128]{1,0:T(8,128)(2,1)}) custom-call(s32[1]{0:T(128)} %bitcast.13.x, bf16[2,6016,128]{2,1,0:T(8,128)(2,1)} %get-tuple-element.150.refs_0_.refs_1_.refs_2_.refs_3_, ...), custom_call_target="tpu_custom_call" | custom-call | tf_op jit(solution)/shard_map/pallas_call | solution.py:897
  149.2 1.0 collective-permute-start.28
  150.6 1.3 collective-permute-start.32
  151.9 11.5 %shard_map.216 = (f32[2,3,64,768]{3,2,1,0:T(8,128)}, f32[2,3,256,128]{3,2,1,0:T(8,128)}, bf16[3,256,128]{2,1,0:T(8,128)(2,1)}, bf16[3,256,128]{2,1,0:T(8,128)(2,1)}) custom-call(s32[8]{0:T(128)} %get-tuple-element.190.refs_0_, s32[2,1,256]{2,1,0:T(1,128)} %get-tuple-element.129.refs_1_, ...), custom_call_target="tpu_custom_call", output_to_operand_aliasing={{0}: (8, {})} | custom-call | flops 13799999488 | tf_op jit(solution)/shard_map/pallas_call | solution.py:277
  163.9 2.4 shard_map.214
  166.3 8.7 %all-to-all-start = ((bf16[4,752,128]{2,1,0:T(8,128)(2,1)}), bf16[4,752,128]{2,1,0:T(8,128)(2,1)}, u32[]{:S(2)}, u32[]{:S(2)}) async-start(bf16[4,752,128]{2,1,0:T(8,128)(2,1)} %bitcast.39), calls=%async_computation | async-start | bytes 1540096 | tf_op jit(solution)/shard_map/all_to_all | solution.py:818
  175.1 6.9 %shard_map.217 = (bf16[576,256]{1,0:T(8,128)(2,1)}, bf16[576,256]{1,0:T(8,128)(2,1)}, bf16[2,1152,128]{2,1,0:T(8,128)(2,1)}, bf16[2,1152,128]{2,1,0:T(8,128)(2,1)}) custom-call(s32[7]{0:T(128)} %stack.47.refs_0_, bf16[592,256]{1,0:T(8,128)(2,1)} %copy-done.2, bf16[592,256]{1,0:T(8,128)(2,1)} %copy-done.3, f32[32,512]{1,0:T(8,128)} %get-tuple-element.230.refs_3_, ...), custom_call_target="tpu_custom_call" | custom-call | flops 8049999872 | tf_op jit(solution)/shard_map/pallas_call | solution.py:683
  182.0 2.2 collective-permute-done.33
  184.2 10.9 %all-to-all-done.got = bf16[4,752,128]{2,1,0:T(8,128)(2,1)} async-done(((bf16[4,752,128]{2,1,0:T(8,128)(2,1)}), bf16[4,752,128]{2,1,0:T(8,128)(2,1)}, u32[]{:S(2)}, u32[]{:S(2)}) %all-to-all-start) | async-done | bytes 770080 | tf_op jit(solution)/shard_map/all_to_all | solution.py:818
  195.1 1.8 fusion.1
  196.9 1.9 shard_map.218.refs_0_
  198.8 1.5 collective-permute-start.36
  200.8 5.6 %collective-permute-done.36.refs_3_ = bf16[752,128]{1,0:T(8,128)(2,1)S(1)} collective-permute-done((bf16[752,128]{1,0:T(8,128)(2,1)}, bf16[752,128]{1,0:T(8,128)(2,1)S(1)}, u32[]{:S(2)}, u32[]{:S(2)}) %collective-permute-start.36) | collective-permute-done | bytes 192544 | tf_op jit(solution)/shard_map/ppermute | solution.py:40
  207.1 8.0 %collective-permute-done.35.refs_2_ = bf16[752,128]{1,0:T(8,128)(2,1)S(1)} collective-permute-done((bf16[752,128]{1,0:T(8,128)(2,1)}, bf16[752,128]{1,0:T(8,128)(2,1)S(1)}, u32[]{:S(2)}, u32[]{:S(2)}) %collective-permute-start.35) | collective-permute-done | bytes 192544 | tf_op jit(solution)/shard_map/ppermute | solution.py:40
  215.1 2.0 collective-permute-start.41
  217.1 2.0 fusion
  219.1 4.3 %all-to-all-start.1 = ((bf16[8,144,128]{2,1,0:T(8,128)(2,1)}), bf16[8,144,128]{2,1,0:T(8,128)(2,1)}, u32[]{:S(2)}, u32[]{:S(2)}) async-start(bf16[8,144,128]{2,1,0:T(8,128)(2,1)} %bitcast.23), calls=%async_computation.1 | async-start | bytes 589824 | tf_op jit(solution)/shard_map/all_to_all | solution.py:818
  224.0 3.7 %collective-permute-start.37 = (bf16[576,256]{1,0:T(8,128)(2,1)}, bf16[576,256]{1,0:T(8,128)(2,1)}, u32[]{:S(2)}, u32[]{:S(2)}) collective-permute-start(bf16[576,256]{1,0:T(8,128)(2,1)} %get-tuple-element.206), channel_id=1, source_target_pairs={{0,0},{8,1},{14,2},{6,3},{2,4},{10,5},{12,6},{4,7},{1,8},{9,9},{15... | collective-permute-start | bytes 884744 | tf_op jit(solution)/shard_map/ppermute | solution.py:40
  227.7 3.0 %collective-permute-start.38 = (bf16[576,256]{1,0:T(8,128)(2,1)}, bf16[576,256]{1,0:T(8,128)(2,1)}, u32[]{:S(2)}, u32[]{:S(2)}) collective-permute-start(bf16[576,256]{1,0:T(8,128)(2,1)} %get-tuple-element.207), channel_id=1, source_target_pairs={{6,0},{14,1},{8,2},{0,3},{4,4},{12,5},{10,6},{2,7},{7,8},{15,9},{9... | collective-permute-start | bytes 884744 | tf_op jit(solution)/shard_map/ppermute | solution.py:40
  232.1 3.3 %shard_map.221 = (f32[144,1536]{1,0:T(8,128)}, f32[144,1536]{1,0:T(8,128)}, f32[144,576]{1,0:T(8,128)}, f32[576,384]{1,0:T(8,128)}) custom-call(s32[2]{0:T(128)} %pad_add_fusion.1.sc, bf16[752,128]{1,0:T(8,128)(2,1)} %shard_map.218.refs_0_, bf16[752,128]{1,0:T(8,128)(2,1)} %copy-done.9, bf16[752,128]{1,0:T(8,128)(2,1)} %copy-done.8, ...), custom_call_target="tpu_custom_call" | custom-call | flops 3449999872 | tf_op jit(solution)/shard_map/pallas_call | solution.py:765
  235.4 9.6 %all-to-all-done.1.got = bf16[8,144,128]{2,1,0:T(8,128)(2,1)} async-done(((bf16[8,144,128]{2,1,0:T(8,128)(2,1)}), bf16[8,144,128]{2,1,0:T(8,128)(2,1)}, u32[]{:S(2)}, u32[]{:S(2)}) %all-to-all-start.1) | async-done | bytes 294944 | tf_op jit(solution)/shard_map/all_to_all | solution.py:818
  245.0 1.7 shard_map.219
  246.7 4.1 %all-to-all-start.2 = ((bf16[8,144,128]{2,1,0:T(8,128)(2,1)}), bf16[8,144,128]{2,1,0:T(8,128)(2,1)}, u32[]{:S(2)}, u32[]{:S(2)}) async-start(bf16[8,144,128]{2,1,0:T(8,128)(2,1)} %shard_map.219), calls=%async_computation.2 | async-start | bytes 589824 | tf_op jit(solution)/shard_map/all_to_all | solution.py:826
  250.8 1.3 broadcast_select_fusion.1
  252.1 0.9 maximum_bitcast_fusion.1
  253.0 0.9 maximum_bitcast_fusion
  253.8 5.4 %all-to-all-done.2 = bf16[8,144,128]{2,1,0:T(8,128)(2,1)} async-done(((bf16[8,144,128]{2,1,0:T(8,128)(2,1)}), bf16[8,144,128]{2,1,0:T(8,128)(2,1)}, u32[]{:S(2)}, u32[]{:S(2)}) %all-to-all-start.2) | async-done | bytes 294944 | tf_op jit(solution)/shard_map/all_to_all | solution.py:826
  259.2 1.9 shard_map.220
  (95 shorter events, 12.6 us)
Async XLA Ops:
  5.8 20.6 %copy-start = (bf16[144,1024]{1,0:T(8,128)(2,1)}, bf16[144,1024]{1,0:T(8,128)(2,1)S(1)}, u32[]{:S(2)}) copy-start(bf16[144,1024]{1,0:T(8,128)(2,1)S(1)} %concatenate.16.refs_5_.refs_14_) | copy-start | bytes 884740
  5.9 11.0 %collective-permute-start = (bf16[144,1024]{1,0:T(8,128)(2,1)S(1)}, bf16[144,1024]{1,0:T(8,128)(2,1)S(1)}, u32[]{:S(2)}, u32[]{:S(2)}) collective-permute-start(bf16[144,1024]{1,0:T(8,128)(2,1)S(1)} %concatenate.16.refs_5_.refs_14_), channel_id=1, source_target_pairs={{0,16},{1,17},{2,18},{3,19},{4,20},{5,21},{6,22},{7,23},{8,24},{9,... | collective-permute-start | bytes 884744 | tf_op jit(solution)/shard_map/ppermute | solution.py:40
  8.9 17.6 %collective-permute-start.4 = (bf16[144,1024]{1,0:T(8,128)(2,1)S(1)}, bf16[144,1024]{1,0:T(8,128)(2,1)S(1)}, u32[]{:S(2)}, u32[]{:S(2)}) collective-permute-start(bf16[144,1024]{1,0:T(8,128)(2,1)S(1)} %concatenate.16.refs_5_.refs_14_), channel_id=1, source_target_pairs={{0,8},{1,9},{2,10},{3,11},{4,12},{5,13},{6,14},{7,15},{8,0},{9,1},... | collective-permute-start | bytes 884744 | tf_op jit(solution)/shard_map/ppermute | solution.py:40
  8.9 13.7 %collective-permute-start.2 = (bf16[592,256]{1,0:T(8,128)(2,1)}, bf16[592,256]{1,0:T(8,128)(2,1)S(1)}, u32[]{:S(2)}, u32[]{:S(2)}) collective-permute-start(bf16[592,256]{1,0:T(8,128)(2,1)} %get-tuple-element.123), channel_id=1, source_target_pairs={{0,0},{1,8},{2,14},{3,6},{4,2},{5,10},{6,12},{7,4},{8,1},{9,9},{10... | collective-permute-start | bytes 909320 | tf_op jit(solution)/shard_map/ppermute | solution.py:40
  10.5 15.0 %collective-permute-start.3 = (bf16[592,256]{1,0:T(8,128)(2,1)}, bf16[592,256]{1,0:T(8,128)(2,1)S(1)}, u32[]{:S(2)}, u32[]{:S(2)}) collective-permute-start(bf16[592,256]{1,0:T(8,128)(2,1)} %get-tuple-element.124), channel_id=1, source_target_pairs={{0,6},{1,14},{2,8},{3,0},{4,4},{5,12},{6,10},{7,2},{8,7},{9,15},{1... | collective-permute-start | bytes 909320 | tf_op jit(solution)/shard_map/ppermute | solution.py:40
  16.9 0.7 copy-start.4
  17.6 3.2 %collective-permute-start.1 = (bf16[144,1024]{1,0:T(8,128)(2,1)S(1)}, bf16[144,1024]{1,0:T(8,128)(2,1)S(1)}, u32[]{:S(2)}, u32[]{:S(2)}) collective-permute-start(bf16[144,1024]{1,0:T(8,128)(2,1)S(1)} %collective-permute-done.refs_6_.refs_15_), channel_id=1, source_target_pairs={{0,8},{1,9},{2,10},{3,11},{4,12},{5,13},{6,14},{7,15},{8,0},{9,1},... | collective-permute-start | bytes 884744 | tf_op jit(solution)/shard_map/ppermute | solution.py:40
  20.8 0.7 copy-start.6
  21.5 32.2 %collective-permute-start.12 = (bf16[144,3648]{1,0:T(8,128)(2,1)}, bf16[144,3648]{1,0:T(8,128)(2,1)}, u32[]{:S(2)}, u32[]{:S(2)}) collective-permute-start(bf16[144,3648]{1,0:T(8,128)(2,1)} %pad_maximum_fusion.refs_7_), channel_id=1, source_target_pairs={{0,16},{1,17},{2,18},{3,19},{4,20},{5,21},{6,22},{7,23},{8,24},{9,... | collective-permute-start | bytes 3151880 | tf_op jit(solution)/shard_map/ppermute | solution.py:40
  22.6 3.8 %copy-start.2 = (bf16[592,256]{1,0:T(8,128)(2,1)}, bf16[592,256]{1,0:T(8,128)(2,1)S(1)}, u32[]{:S(2)}) copy-start(bf16[592,256]{1,0:T(8,128)(2,1)S(1)} %collective-permute-done.2.refs_1_) | copy-start | bytes 909316
  25.5 1.0 copy-start.3
  26.5 0.7 copy-start.5
  32.0 7.8 %collective-permute-start.8 = (bf16[2,3,256,128]{3,2,1,0:T(8,128)(2,1)}, bf16[2,3,256,128]{3,2,1,0:T(8,128)(2,1)}, u32[]{:S(2)}, u32[]{:S(2)}) collective-permute-start(bf16[2,3,256,128]{3,2,1,0:T(8,128)(2,1)} %get-tuple-element.131.refs_3_.refs_6_), channel_id=1, source_target_pairs={{0,8},{1,9},{2,10},{3,11},{4,12},{5,13},{6,14},{7,15},{8,0},{9,1},... | collective-permute-start | bytes 1179656 | tf_op jit(solution)/shard_map/ppermute | solution.py:40
  32.1 17.9 %collective-permute-start.7 = (bf16[2,3,256,128]{3,2,1,0:T(8,128)(2,1)}, bf16[2,3,256,128]{3,2,1,0:T(8,128)(2,1)}, u32[]{:S(2)}, u32[]{:S(2)}) collective-permute-start(bf16[2,3,256,128]{3,2,1,0:T(8,128)(2,1)} %get-tuple-element.131.refs_3_.refs_6_), channel_id=1, source_target_pairs={{0,2},{1,3},{2,4},{3,5},{4,6},{5,7},{8,10},{9,11},{10,12},{11,13},... | collective-permute-start | bytes 1179656 | tf_op jit(solution)/shard_map/ppermute | solution.py:40
  50.0 6.4 %collective-permute-start.10 = (bf16[2,3,256,128]{3,2,1,0:T(8,128)(2,1)}, bf16[2,3,256,128]{3,2,1,0:T(8,128)(2,1)}, u32[]{:S(2)}, u32[]{:S(2)}) collective-permute-start(bf16[2,3,256,128]{3,2,1,0:T(8,128)(2,1)} %collective-permute-done.7.refs_3_.refs_6_), channel_id=1, source_target_pairs={{0,8},{1,9},{2,10},{3,11},{4,12},{5,13},{6,14},{7,15},{8,0},{9,1},... | collective-permute-start | bytes 1179656 | tf_op jit(solution)/shard_map/ppermute | solution.py:40
  50.2 12.3 %collective-permute-start.9 = (bf16[2,3,256,128]{3,2,1,0:T(8,128)(2,1)}, bf16[2,3,256,128]{3,2,1,0:T(8,128)(2,1)}, u32[]{:S(2)}, u32[]{:S(2)}) collective-permute-start(bf16[2,3,256,128]{3,2,1,0:T(8,128)(2,1)} %collective-permute-done.7.refs_3_.refs_6_), channel_id=1, source_target_pairs={{0,2},{1,3},{2,4},{3,5},{4,6},{5,7},{8,10},{9,11},{10,12},{11,13},... | collective-permute-start | bytes 1179656 | tf_op jit(solution)/shard_map/ppermute | solution.py:40
  53.5 22.3 %collective-permute-start.13 = (bf16[144,3648]{1,0:T(8,128)(2,1)}, bf16[144,3648]{1,0:T(8,128)(2,1)}, u32[]{:S(2)}, u32[]{:S(2)}) collective-permute-start(bf16[144,3648]{1,0:T(8,128)(2,1)} %pad_maximum_fusion.refs_7_), channel_id=1, source_target_pairs={{0,8},{1,9},{2,10},{3,11},{4,12},{5,13},{6,14},{7,15},{8,0},{9,1},... | collective-permute-start | bytes 3151880 | tf_op jit(solution)/shard_map/ppermute | solution.py:40
  53.7 22.1 %collective-permute-start.14 = (bf16[144,3648]{1,0:T(8,128)(2,1)}, bf16[144,3648]{1,0:T(8,128)(2,1)}, u32[]{:S(2)}, u32[]{:S(2)}) collective-permute-start(bf16[144,3648]{1,0:T(8,128)(2,1)} %collective-permute-done.12.refs_8_), channel_id=1, source_target_pairs={{0,8},{1,9},{2,10},{3,11},{4,12},{5,13},{6,14},{7,15},{8,0},{9,1},... | collective-permute-start | bytes 3151880 | tf_op jit(solution)/shard_map/ppermute | solution.py:40
  54.0 14.4 %collective-permute-start.15 = (bf16[576,384]{1,0:T(8,128)(2,1)}, bf16[576,384]{1,0:T(8,128)(2,1)}, u32[]{:S(2)}, u32[]{:S(2)}) collective-permute-start(bf16[576,384]{1,0:T(8,128)(2,1)} %bitcast.43), channel_id=1, source_target_pairs={{0,16},{1,17},{2,18},{3,19},{4,20},{5,21},{6,22},{7,23},{8,24},{9,... | collective-permute-start | bytes 1327112 | tf_op jit(solution)/shard_map/ppermute | solution.py:40
  56.4 12.0 %collective-permute-start.6 = (bf16[576,256]{1,0:T(8,128)(2,1)}, bf16[576,256]{1,0:T(8,128)(2,1)}, u32[]{:S(2)}, u32[]{:S(2)}) collective-permute-start(bf16[576,256]{1,0:T(8,128)(2,1)} %get-tuple-element.227), channel_id=1, source_target_pairs={{0,6},{1,14},{2,8},{3,0},{4,4},{5,12},{6,10},{7,2},{8,7},{9,15},{1... | collective-permute-start | bytes 884744 | tf_op jit(solution)/shard_map/ppermute | solution.py:40
  62.5 6.5 %collective-permute-start.11 = (bf16[2,3,256,128]{3,2,1,0:T(8,128)(2,1)}, bf16[2,3,256,128]{3,2,1,0:T(8,128)(2,1)}, u32[]{:S(2)}, u32[]{:S(2)}) collective-permute-start(bf16[2,3,256,128]{3,2,1,0:T(8,128)(2,1)} %collective-permute-done.9.refs_3_.refs_6_), channel_id=1, source_target_pairs={{0,8},{1,9},{2,10},{3,11},{4,12},{5,13},{6,14},{7,15},{8,0},{9,1},... | collective-permute-start | bytes 1179656 | tf_op jit(solution)/shard_map/ppermute | solution.py:40
  68.4 7.4 %collective-permute-start.16 = (bf16[576,384]{1,0:T(8,128)(2,1)}, bf16[576,384]{1,0:T(8,128)(2,1)}, u32[]{:S(2)}, u32[]{:S(2)}) collective-permute-start(bf16[576,384]{1,0:T(8,128)(2,1)} %bitcast.44), channel_id=1, source_target_pairs={{0,8},{1,9},{2,10},{3,11},{4,12},{5,13},{6,14},{7,15},{8,0},{9,1},... | collective-permute-start | bytes 1327112 | tf_op jit(solution)/shard_map/ppermute | solution.py:40
  68.4 7.4 %collective-permute-start.17 = (bf16[576,384]{1,0:T(8,128)(2,1)}, bf16[576,384]{1,0:T(8,128)(2,1)}, u32[]{:S(2)}, u32[]{:S(2)}) collective-permute-start(bf16[576,384]{1,0:T(8,128)(2,1)} %collective-permute-done.15.refs_12_), channel_id=1, source_target_pairs={{0,8},{1,9},{2,10},{3,11},{4,12},{5,13},{6,14},{7,15},{8,0},{9,1},... | collective-permute-start | bytes 1327112 | tf_op jit(solution)/shard_map/ppermute | solution.py:40
  68.9 6.9 %collective-permute-start.5 = (bf16[576,256]{1,0:T(8,128)(2,1)}, bf16[576,256]{1,0:T(8,128)(2,1)}, u32[]{:S(2)}, u32[]{:S(2)}) collective-permute-start(bf16[576,256]{1,0:T(8,128)(2,1)} %get-tuple-element.228), channel_id=1, source_target_pairs={{0,0},{1,8},{2,14},{3,6},{4,2},{5,10},{6,12},{7,4},{8,1},{9,9},{10... | collective-permute-start | bytes 884744 | tf_op jit(solution)/shard_map/ppermute | solution.py:40
  94.4 22.8 %collective-permute-start.18 = (bf16[2,6016,128]{2,1,0:T(8,128)(2,1)}, bf16[2,6016,128]{2,1,0:T(8,128)(2,1)}, u32[]{:S(2)}, u32[]{:S(2)}) collective-permute-start(bf16[2,6016,128]{2,1,0:T(8,128)(2,1)} %get-tuple-element.151), channel_id=1, source_target_pairs={{0,8},{1,9},{2,10},{3,11},{4,12},{5,13},{6,14},{7,15},{8,0},{9,1},... | collective-permute-start | bytes 9240584 | tf_op jit(solution)/shard_map/ppermute | solution.py:40
  99.3 2.4 collective-permute-start.19
  99.3 2.7 %collective-permute-start.20 = (bf16[3,256,128]{2,1,0:T(8,128)(2,1)}, bf16[3,256,128]{2,1,0:T(8,128)(2,1)}, u32[]{:S(2)}, u32[]{:S(2)}) collective-permute-start(bf16[3,256,128]{2,1,0:T(8,128)(2,1)} %get-tuple-element.160), channel_id=1, source_target_pairs={{0,8},{1,9},{2,10},{3,11},{4,12},{5,13},{6,14},{7,15},{8,0},{9,1},... | collective-permute-start | bytes 589832 | tf_op jit(solution)/shard_map/ppermute | solution.py:40
  104.0 22.8 %collective-permute-start.24 = (bf16[576,256]{1,0:T(8,128)(2,1)}, bf16[576,256]{1,0:T(8,128)(2,1)}, u32[]{:S(2)}, u32[]{:S(2)}) collective-permute-start(bf16[576,256]{1,0:T(8,128)(2,1)} %get-tuple-element.170), channel_id=1, source_target_pairs={{0,0},{8,1},{14,2},{6,3},{2,4},{10,5},{12,6},{4,7},{1,8},{9,9},{15... | collective-permute-start | bytes 884744 | tf_op jit(solution)/shard_map/ppermute | solution.py:40
  107.8 26.6 %collective-permute-start.25 = (bf16[576,256]{1,0:T(8,128)(2,1)}, bf16[576,256]{1,0:T(8,128)(2,1)}, u32[]{:S(2)}, u32[]{:S(2)}) collective-permute-start(bf16[576,256]{1,0:T(8,128)(2,1)} %get-tuple-element.171), channel_id=1, source_target_pairs={{6,0},{14,1},{8,2},{0,3},{4,4},{12,5},{10,6},{2,7},{7,8},{15,9},{9... | collective-permute-start | bytes 884744 | tf_op jit(solution)/shard_map/ppermute | solution.py:40
  120.3 21.4 %collective-permute-start.23 = (bf16[2,3,256,128]{3,2,1,0:T(8,128)(2,1)}, bf16[2,3,256,128]{3,2,1,0:T(8,128)(2,1)}, u32[]{:S(2)}, u32[]{:S(2)}) collective-permute-start(bf16[2,3,256,128]{3,2,1,0:T(8,128)(2,1)} %shard_map.211), channel_id=1, source_target_pairs={{2,0},{3,1},{4,2},{5,3},{6,4},{7,5},{10,8},{11,9},{12,10},{13,11},... | collective-permute-start | bytes 1179656 | tf_op jit(solution)/shard_map/ppermute | solution.py:40
  121.6 22.3 %collective-permute-start.26 = (bf16[2,1504,128]{2,1,0:T(8,128)(2,1)}, bf16[2,1504,128]{2,1,0:T(8,128)(2,1)}, u32[]{:S(2)}, u32[]{:S(2)}) collective-permute-start(bf16[2,1504,128]{2,1,0:T(8,128)(2,1)} %get-tuple-element.174), channel_id=1, source_target_pairs={{0,16},{1,17},{2,18},{3,19},{4,20},{5,21},{6,22},{7,23},{8,24},{9,... | collective-permute-start | bytes 2310152 | tf_op jit(solution)/shard_map/ppermute | solution.py:40
  123.2 22.4 %collective-permute-start.27 = (bf16[2,1504,128]{2,1,0:T(8,128)(2,1)}, bf16[2,1504,128]{2,1,0:T(8,128)(2,1)}, u32[]{:S(2)}, u32[]{:S(2)}) collective-permute-start(bf16[2,1504,128]{2,1,0:T(8,128)(2,1)} %get-tuple-element.175), channel_id=1, source_target_pairs={{0,1},{1,0},{2,3},{3,2},{4,5},{5,4},{6,7},{7,6},{8,9},{9,8},{10,11... | collective-permute-start | bytes 2310152 | tf_op jit(solution)/shard_map/ppermute | solution.py:40
  126.8 7.6 %collective-permute-start.21 = (bf16[3,256,128]{2,1,0:T(8,128)(2,1)}, bf16[3,256,128]{2,1,0:T(8,128)(2,1)}, u32[]{:S(2)}, u32[]{:S(2)}) collective-permute-start(bf16[3,256,128]{2,1,0:T(8,128)(2,1)} %get-tuple-element.166), channel_id=1, source_target_pairs={{0,8},{1,9},{2,10},{3,11},{4,12},{5,13},{6,14},{7,15},{8,0},{9,1},... | collective-permute-start | bytes 589832 | tf_op jit(solution)/shard_map/ppermute | solution.py:40
  134.4 1.8 collective-permute-start.22
  149.2 14.7 %collective-permute-start.28 = (bf16[1504,128]{1,0:T(8,128)(2,1)}, bf16[1504,128]{1,0:T(8,128)(2,1)}, u32[]{:S(2)}, u32[]{:S(2)}) collective-permute-start(bf16[1504,128]{1,0:T(8,128)(2,1)} %get-tuple-element.182), channel_id=1, source_target_pairs={{0,1},{1,0},{2,3},{3,2},{4,5},{5,4},{6,7},{7,6},{8,9},{9,8},{10,11... | collective-permute-start | bytes 1155080 | tf_op jit(solution)/shard_map/ppermute | solution.py:40
  150.2 13.7 %collective-permute-start.29 = (bf16[1504,128]{1,0:T(8,128)(2,1)}, bf16[1504,128]{1,0:T(8,128)(2,1)}, u32[]{:S(2)}, u32[]{:S(2)}) collective-permute-start(bf16[1504,128]{1,0:T(8,128)(2,1)} %get-tuple-element.184), channel_id=1, source_target_pairs={{0,16},{1,17},{2,18},{3,19},{4,20},{5,21},{6,22},{7,23},{8,24},{9,... | collective-permute-start | bytes 1155080 | tf_op jit(solution)/shard_map/ppermute | solution.py:40
  150.6 24.4 %collective-permute-start.32 = (bf16[2,3,256,128]{3,2,1,0:T(8,128)(2,1)}, bf16[2,3,256,128]{3,2,1,0:T(8,128)(2,1)}, u32[]{:S(2)}, u32[]{:S(2)}) collective-permute-start(bf16[2,3,256,128]{3,2,1,0:T(8,128)(2,1)} %shard_map.215), channel_id=1, source_target_pairs={{2,0},{3,1},{4,2},{5,3},{6,4},{7,5},{10,8},{11,9},{12,10},{13,11},... | collective-permute-start | bytes 1179656 | tf_op jit(solution)/shard_map/ppermute | solution.py:40
  163.4 11.7 %collective-permute-start.30 = (bf16[3,256,128]{2,1,0:T(8,128)(2,1)}, bf16[3,256,128]{2,1,0:T(8,128)(2,1)}, u32[]{:S(2)}, u32[]{:S(2)}) collective-permute-start(bf16[3,256,128]{2,1,0:T(8,128)(2,1)} %get-tuple-element.199), channel_id=1, source_target_pairs={{0,8},{1,9},{2,10},{3,11},{4,12},{5,13},{6,14},{7,15},{8,0},{9,1},... | collective-permute-start | bytes 589832 | tf_op jit(solution)/shard_map/ppermute | solution.py:40
  163.4 11.7 %collective-permute-start.31 = (bf16[3,256,128]{2,1,0:T(8,128)(2,1)}, bf16[3,256,128]{2,1,0:T(8,128)(2,1)}, u32[]{:S(2)}, u32[]{:S(2)}) collective-permute-start(bf16[3,256,128]{2,1,0:T(8,128)(2,1)} %get-tuple-element.200), channel_id=1, source_target_pairs={{0,8},{1,9},{2,10},{3,11},{4,12},{5,13},{6,14},{7,15},{8,0},{9,1},... | collective-permute-start | bytes 589832 | tf_op jit(solution)/shard_map/ppermute | solution.py:40
  166.3 28.8 %all-to-all-start = ((bf16[4,752,128]{2,1,0:T(8,128)(2,1)}), bf16[4,752,128]{2,1,0:T(8,128)(2,1)}, u32[]{:S(2)}, u32[]{:S(2)}) async-start(bf16[4,752,128]{2,1,0:T(8,128)(2,1)} %bitcast.39), calls=%async_computation | async-start | bytes 1540096 | tf_op jit(solution)/shard_map/all_to_all | solution.py:818
  182.0 2.3 collective-permute-start.33
  184.2 10.9 %copy-start.1 = (bf16[2,1152,128]{2,1,0:T(8,128)(2,1)}, bf16[2,1152,128]{2,1,0:T(8,128)(2,1)S(1)}, u32[]{:S(2)}) copy-start(bf16[2,1152,128]{2,1,0:T(8,128)(2,1)S(1)} %collective-permute-done.33) | copy-start | bytes 1769476
  196.9 20.2 %collective-permute-start.39 = (bf16[1152,128]{1,0:T(8,128)(2,1)}, bf16[1152,128]{1,0:T(8,128)(2,1)}, u32[]{:S(2)}, u32[]{:S(2)}) collective-permute-start(bf16[1152,128]{1,0:T(8,128)(2,1)} %fusion.1), channel_id=1, source_target_pairs={{0,16},{1,17},{2,18},{3,19},{4,20},{5,21},{6,22},{7,23},{8,24},{9,... | collective-permute-start | bytes 884744 | tf_op jit(solution)/shard_map/ppermute | solution.py:40
  198.8 7.6 %collective-permute-start.36 = (bf16[752,128]{1,0:T(8,128)(2,1)}, bf16[752,128]{1,0:T(8,128)(2,1)S(1)}, u32[]{:S(2)}, u32[]{:S(2)}) collective-permute-start(bf16[752,128]{1,0:T(8,128)(2,1)} %shard_map.218.refs_0_), channel_id=1, source_target_pairs={{0,6},{1,7},{2,0},{3,1},{4,2},{5,3},{6,4},{7,5},{8,14},{9,15},{10,... | collective-permute-start | bytes 577544 | tf_op jit(solution)/shard_map/ppermute | solution.py:40
  200.2 14.8 %collective-permute-start.35 = (bf16[752,128]{1,0:T(8,128)(2,1)}, bf16[752,128]{1,0:T(8,128)(2,1)S(1)}, u32[]{:S(2)}, u32[]{:S(2)}) collective-permute-start(bf16[752,128]{1,0:T(8,128)(2,1)} %shard_map.218.refs_0_), channel_id=1, source_target_pairs={{0,4},{1,5},{2,6},{3,7},{4,0},{5,1},{6,2},{7,3},{8,12},{9,13},{10,... | collective-permute-start | bytes 577544 | tf_op jit(solution)/shard_map/ppermute | solution.py:40
  200.2 14.8 %collective-permute-start.34 = (bf16[752,128]{1,0:T(8,128)(2,1)}, bf16[752,128]{1,0:T(8,128)(2,1)S(1)}, u32[]{:S(2)}, u32[]{:S(2)}) collective-permute-start(bf16[752,128]{1,0:T(8,128)(2,1)} %shard_map.218.refs_0_), channel_id=1, source_target_pairs={{0,2},{1,3},{2,4},{3,5},{4,6},{5,7},{6,0},{7,1},{8,10},{9,11},{10,... | collective-permute-start | bytes 577544 | tf_op jit(solution)/shard_map/ppermute | solution.py:40
  200.8 26.9 %collective-permute-start.40 = (bf16[752,128]{1,0:T(8,128)(2,1)}, bf16[752,128]{1,0:T(8,128)(2,1)S(1)}, u32[]{:S(2)}, u32[]{:S(2)}) collective-permute-start(bf16[752,128]{1,0:T(8,128)(2,1)} %shard_map.218.refs_0_), channel_id=1, source_target_pairs={{0,1},{1,0},{2,3},{3,2},{4,5},{5,4},{6,7},{7,6},{8,9},{9,8},{10,11... | collective-permute-start | bytes 577544 | tf_op jit(solution)/shard_map/ppermute | solution.py:40
  206.4 0.7 copy-start.7
  207.1 23.7 %collective-permute-start.43 = (bf16[752,128]{1,0:T(8,128)(2,1)S(1)}, bf16[752,128]{1,0:T(8,128)(2,1)S(1)}, u32[]{:S(2)}, u32[]{:S(2)}) collective-permute-start(bf16[752,128]{1,0:T(8,128)(2,1)S(1)} %collective-permute-done.36.refs_3_), channel_id=1, source_target_pairs={{0,1},{1,0},{2,3},{3,2},{4,5},{5,4},{6,7},{7,6},{8,9},{9,8},{10,11... | collective-permute-start | bytes 577544 | tf_op jit(solution)/shard_map/ppermute | solution.py:40
  215.1 15.7 %copy-start.8 = (bf16[752,128]{1,0:T(8,128)(2,1)}, bf16[752,128]{1,0:T(8,128)(2,1)S(1)}, u32[]{:S(2)}) copy-start(bf16[752,128]{1,0:T(8,128)(2,1)S(1)} %collective-permute-done.35.refs_2_) | copy-start | bytes 577540
  215.1 15.7 %collective-permute-start.42 = (bf16[752,128]{1,0:T(8,128)(2,1)S(1)}, bf16[752,128]{1,0:T(8,128)(2,1)S(1)}, u32[]{:S(2)}, u32[]{:S(2)}) collective-permute-start(bf16[752,128]{1,0:T(8,128)(2,1)S(1)} %collective-permute-done.35.refs_2_), channel_id=1, source_target_pairs={{0,1},{1,0},{2,3},{3,2},{4,5},{5,4},{6,7},{7,6},{8,9},{9,8},{10,11... | collective-permute-start | bytes 577544 | tf_op jit(solution)/shard_map/ppermute | solution.py:40
  215.1 15.7 %copy-start.9 = (bf16[752,128]{1,0:T(8,128)(2,1)}, bf16[752,128]{1,0:T(8,128)(2,1)S(1)}, u32[]{:S(2)}) copy-start(bf16[752,128]{1,0:T(8,128)(2,1)S(1)} %collective-permute-done.34.refs_1_) | copy-start | bytes 577540
  215.1 17.0 %collective-permute-start.41 = (bf16[752,128]{1,0:T(8,128)(2,1)S(1)}, bf16[752,128]{1,0:T(8,128)(2,1)}, u32[]{:S(2)}, u32[]{:S(2)}) collective-permute-start(bf16[752,128]{1,0:T(8,128)(2,1)S(1)} %collective-permute-done.34.refs_1_), channel_id=1, source_target_pairs={{0,1},{1,0},{2,3},{3,2},{4,5},{5,4},{6,7},{7,6},{8,9},{9,8},{10,11... | collective-permute-start | bytes 577544 | tf_op jit(solution)/shard_map/ppermute | solution.py:40
  219.1 25.9 %all-to-all-start.1 = ((bf16[8,144,128]{2,1,0:T(8,128)(2,1)}), bf16[8,144,128]{2,1,0:T(8,128)(2,1)}, u32[]{:S(2)}, u32[]{:S(2)}) async-start(bf16[8,144,128]{2,1,0:T(8,128)(2,1)} %bitcast.23), calls=%async_computation.1 | async-start | bytes 589824 | tf_op jit(solution)/shard_map/all_to_all | solution.py:818
  224.0 26.8 %collective-permute-start.37 = (bf16[576,256]{1,0:T(8,128)(2,1)}, bf16[576,256]{1,0:T(8,128)(2,1)}, u32[]{:S(2)}, u32[]{:S(2)}) collective-permute-start(bf16[576,256]{1,0:T(8,128)(2,1)} %get-tuple-element.206), channel_id=1, source_target_pairs={{0,0},{8,1},{14,2},{6,3},{2,4},{10,5},{12,6},{4,7},{1,8},{9,9},{15... | collective-permute-start | bytes 884744 | tf_op jit(solution)/shard_map/ppermute | solution.py:40
  227.7 3.1 %copy-start.10 = (bf16[752,128]{1,0:T(8,128)(2,1)}, bf16[752,128]{1,0:T(8,128)(2,1)S(1)}, u32[]{:S(2)}) copy-start(bf16[752,128]{1,0:T(8,128)(2,1)S(1)} %collective-permute-done.40.refs_4_) | copy-start | bytes 577540
  227.7 23.1 %collective-permute-start.38 = (bf16[576,256]{1,0:T(8,128)(2,1)}, bf16[576,256]{1,0:T(8,128)(2,1)}, u32[]{:S(2)}, u32[]{:S(2)}) collective-permute-start(bf16[576,256]{1,0:T(8,128)(2,1)} %get-tuple-element.207), channel_id=1, source_target_pairs={{6,0},{14,1},{8,2},{0,3},{4,4},{12,5},{10,6},{2,7},{7,8},{15,9},{9... | collective-permute-start | bytes 884744 | tf_op jit(solution)/shard_map/ppermute | solution.py:40
  230.8 0.7 copy-start.11
  231.4 0.7 copy-start.12
  246.7 12.5 %all-to-all-start.2 = ((bf16[8,144,128]{2,1,0:T(8,128)(2,1)}), bf16[8,144,128]{2,1,0:T(8,128)(2,1)}, u32[]{:S(2)}, u32[]{:S(2)}) async-start(bf16[8,144,128]{2,1,0:T(8,128)(2,1)} %shard_map.219), calls=%async_computation.2 | async-start | bytes 589824 | tf_op jit(solution)/shard_map/all_to_all | solution.py:826

commit v4 on v3

--- a/solution.py
+++ b/solution.py
@@ -311,7 +311,9 @@
     return lax.rsqrt(jnp.mean(v * v, axis=0, keepdims=True) + EPSILON)
 
 
-def prepare_kernel(sc, tokens, positions, first, second):
+def prepare_kernel(sc, tokens, positions, query, key, value, gains, first, second, packed):
+    ends = jnp.concatenate([gains[...], jnp.zeros((56, gains.shape[1]), F32)], axis=0).T
+    packed[...] = jnp.concatenate([query[...], key[...], value[...], ends.astype(BF16)], axis=1)
     width, count = tokens.shape
     rows = count // 2
     p = positions[:, pl.ds(pl.multiple_of(sc[0], 128), count)]
@@ -327,19 +329,22 @@
                 out[width:] = p[:, half * rows : (half + 1) * rows]
 
 
-def prepare(at, h, tokens, positions):
+def prepare(at, h, tokens, positions, query, key, value, gains):
     width, count = tokens.shape
     out = jax.ShapeDtypeStruct((width + 16, count // 2), BF16)
+    given = (tokens, positions, query, key, value, gains)
+    columns = sum(w.shape[1] for w in (query, key, value)) + 64
+    packed = jax.ShapeDtypeStruct((query.shape[0], columns), BF16)
     sc = jnp.stack([at, lax.rem(h, 2)]).astype(jnp.int32)
     return pl.pallas_call(
         prepare_kernel,
-        out_shape=(out, out),
+        out_shape=(out, out, packed),
         grid=(1,),
-        in_specs=[SM] + wholes(tokens, positions),
-        out_specs=wholes(out, out),
+        in_specs=[SM] + wholes(*given),
+        out_specs=wholes(out, out, packed),
         compiler_params=LIMIT,
         cost_estimate=takes(2),
-    )(sc, tokens, positions)
+    )(sc, *given)
 
 
 def project_kernel(pieces, *refs):
@@ -774,15 +779,31 @@
     )(place, *pieces)
 
 
-def chip_sum(mine, got, i):
-    return mine[i].astype(F32) + got[i].astype(F32)
+def chip_kernel(mine, got, *refs):
+    *came, out = refs
+    total = mine[0].astype(F32) + got[0].astype(F32)
+    for c in came:
+        total = total + c[...].astype(F32)
+    out[...] = total.astype(BF16)
+
+
+def chip_sum(mine, got, i, *came):
+    out = jax.ShapeDtypeStruct(mine.shape[1:], BF16)
+    one = pl.BlockSpec((1,) + mine.shape[1:], lambda n: (i, 0, 0))
+    return pl.pallas_call(
+        chip_kernel,
+        out_shape=out,
+        grid=(1,),
+        in_specs=[one, one] + wholes(*came),
+        out_specs=whole(out),
+        compiler_params=LIMIT,
+        cost_estimate=takes(0),
+    )(mine, got, *came)
 
 
 def sum_y(mine, got, send):
-    total = chip_sum(mine, got, 0)
-    for s in range(1, mine.shape[0]):
-        total = total + send["shift"][s](chip_sum(mine, got, s).astype(BF16)).astype(F32)
-    return total.astype(BF16)
+    came = [send["shift"][s](chip_sum(mine, got, s)) for s in range(1, mine.shape[0])]
+    return chip_sum(mine, got, 0, *came)
 
 
 def spread_kernel(got, out):
@@ -961,22 +982,20 @@
     order = jnp.stack([core, y, 4 * h] + piece_order(fsdp, core, y)).astype(jnp.int32)
     shard = gate_weight.shape[0]
     join = shard % 16 != 0
-    x_pair = prepare(2 * count * h + count * x, h, tokens.reshape(count, width).T, positions)
-    *pair, query_weight, norm_first, norm_second = tie(
-        *x_pair, query_weight, norm_first, norm_second
+    row = lax.broadcasted_iota(jnp.int32, (8, shard), 0)
+    gain_rows = jnp.where(row == 0, norm_first.astype(F32), norm_second.astype(F32))
+    gain_rows = jnp.where(row < 2, gain_rows, 0.0)
+    *pair, packed = prepare(
+        2 * count * h + count * x,
+        h,
+        tokens.reshape(count, width).T,
+        positions,
+        query_weight,
+        key_weight,
+        value_weight,
+        gain_rows,
     )
     xs = send_home(send, pair)
-    packed = jnp.concatenate(
-        [
-            query_weight,
-            key_weight,
-            value_weight,
-            norm_first[:, None],
-            norm_second[:, None],
-            jnp.zeros((shard, 62), BF16),
-        ],
-        axis=1,
-    )
     first_parts = gather_y(packed, send, fsdp)
     first_parts = gather_pieces(first_parts, send, fsdp, core, y, join, 0)
     cot_t, _ = tie(cotangent.reshape(count, width).T, first_parts[-1])

time: 264 us -> 255 us (0.966)
  waiting for transfers between devices: 68.7 us -> 54.3 us
  Pallas kernels: 89 us -> 93.3 us
  local copies, waits for them, and re-layouts: 7.36 us -> 3.46 us
  starting transfers between devices: 81.9 us -> 85.7 us
    all_to_all x2, waiting for transfers between devices: 20.5 us -> 10.8 us  [exchange(): return lax.all_to_all(parts, axes, 0, 0, tiled=True)]
    ppermute x44, starting transfers between devices: 64.8 us -> 70.8 us  [along(): return lambda a: lax.ppermute(a, AXES, pairs)]
    all_to_all x1, waiting for transfers between devices: 5.4 us -> 0.01 us  [gather_over(): return lax.all_to_all(spread, axes, 0, 0, tiled=True).reshape(-1, 128)]
    pallas_call x1 -> x3, Pallas kernels: 1.94 us -> 6.09 us  [the longest x2 3.79 us: chip_sum(): pl.pallas_call(chip_kernel, out_shape=out, grid=(1,), in_specs=[one, one]...]
  transfers between devices with their start and end apart: 47 -> 47, of which waited for: 15 -> 13; matrix products, arithmetic and copies ran while one was open for 4% -> 4% of each run, Pallas kernels for 24% -> 26%
where the time goes in v4:
time: 255 us; the launch traced here: 250 us
  Pallas kernels  93.3 us (37%)
  starting transfers between devices  85.7 us (34%)
  waiting for transfers between devices  54.3 us (21%)
  other arithmetic  12.3 us (5%)
  local copies, waits for them, and re-layouts  3.46 us (1%)
    ppermute x44, starting transfers between devices, along(): return lambda a: lax.ppermute(a, AXES, pairs)  70.8 us
    ppermute x44, waiting for transfers between devices, along(): return lambda a: lax.ppermute(a, AXES, pairs)  43.6 us
    pallas_call x1, Pallas kernels, feed(): pl.pallas_call(functools.partial(feed_kernel, fsdp, len(parts), ff // 4 i...  18.6 us
    pallas_call x3, Pallas kernels, attend_backward(): pl.pallas_call(functools.partial(backward_kernel, stage, first, own_type)...  18.4 us
    pallas_call x3, Pallas kernels, attend_forward(): pl.pallas_call(functools.partial(forward_kernel, stage, last), out_shape=...  16.4 us
    all_to_all x2, starting transfers between devices, exchange(): return lax.all_to_all(parts, axes, 0, 0, tiled=True)  10.9 us
    all_to_all x2, waiting for transfers between devices, exchange(): return lax.all_to_all(parts, axes, 0, 0, tiled=True)  10.8 us
    pallas_call x5, Pallas kernels, simple_call(): pl.pallas_call(kernel, out_shape=out_shape, grid=(1,), in_specs=wholes(*g...  10.2 us
  transfers between devices with their start and end apart: 47, of which 13 were waited for; matrix products, arithmetic and copies ran while one was open for 4% of the time, Pallas kernels for 26%

profile of v4, /device:TPU:0, one launch (start us, length us, event | category | flops | bytes accessed | tf_op | source)
XLA Modules:
  0.0 250.0 jit_solution(5765997802229092725)
XLA Ops:
  3.2 2.3 shard_map.203
  5.5 3.0 %collective-permute-start = (bf16[144,1024]{1,0:T(8,128)(2,1)}, bf16[144,1024]{1,0:T(8,128)(2,1)S(1)}, u32[]{:S(2)}, u32[]{:S(2)}) collective-permute-start(bf16[144,1024]{1,0:T(8,128)(2,1)} %get-tuple-element.113.refs_5_.refs_14_), channel_id=1, source_target_pairs={{0,16},{1,17},{2,18},{3,19},{4,20},{5,21},{6,22},{7,23},{8,24},{9,... | collective-permute-start | bytes 884744 | tf_op jit(solution)/shard_map/ppermute | solution.py:40
  8.5 1.6 collective-permute-start.2
  10.1 6.4 %collective-permute-start.3 = (bf16[592,256]{1,0:T(8,128)(2,1)}, bf16[592,256]{1,0:T(8,128)(2,1)S(1)}, u32[]{:S(2)}, u32[]{:S(2)}) collective-permute-start(bf16[592,256]{1,0:T(8,128)(2,1)} %get-tuple-element.116), channel_id=1, source_target_pairs={{0,6},{1,14},{2,8},{3,0},{4,4},{5,12},{6,10},{7,2},{8,7},{9,15},{1... | collective-permute-start | bytes 909320 | tf_op jit(solution)/shard_map/ppermute | solution.py:40
  17.2 0.9 collective-permute-start.1
  18.1 2.3 pad_maximum_fusion.refs_7_
  22.3 0.7 copy-done
  23.0 2.1 collective-permute-done.3.refs_2_
  25.8 1.0 multiply_sine_fusion
  26.8 4.8 %shard_map.204 = (bf16[2,3,64,768]{3,2,1,0:T(8,128)(2,1)}, bf16[2,3,256,128]{3,2,1,0:T(8,128)(2,1)}, bf16[576,512]{1,0:T(8,128)(2,1)}, bf16[576,128]{1,0:T(8,128)(2,1)}, s32[2,1,256]{2,1,0:T(1,128)}, /*index=5*/s32[8]{0:T(128)}) custom-call(s32[7]{0:T(128)} %stack.47.refs_0_, bf16[592,256]{1,0:T(8,128)(2,1)} %copy-done, bf16[592,256]{1,0:T(8,128)(2,1)} %copy-done.1, ...), custom_call_target="tpu_custom_call" | custom-call | tf_op jit(solution)/shard_map/pallas_call | solution.py:411
  31.7 7.7 %collective-permute-start.7 = (bf16[2,3,256,128]{3,2,1,0:T(8,128)(2,1)}, bf16[2,3,256,128]{3,2,1,0:T(8,128)(2,1)}, u32[]{:S(2)}, u32[]{:S(2)}) collective-permute-start(bf16[2,3,256,128]{3,2,1,0:T(8,128)(2,1)} %get-tuple-element.123.refs_3_.refs_6_), channel_id=1, source_target_pairs={{0,2},{1,3},{2,4},{3,5},{4,6},{5,7},{8,10},{9,11},{10,12},{11,13},... | collective-permute-start | bytes 1179656 | tf_op jit(solution)/shard_map/ppermute | solution.py:40
  39.4 10.2 %shard_map.205 = (f32[2,3,1,768]{3,2,1,0:T(1,128)}, f32[2,3,1,768]{3,2,1,0:T(1,128)}, f32[2,3,64,768]{3,2,1,0:T(8,128)}) custom-call(s32[8]{0:T(128)} %get-tuple-element.182.refs_0_, s32[2,1,256]{2,1,0:T(1,128)} %get-tuple-element.121.refs_1_, bf16[2,3,64,768]{3,2,1,0:T(8,128)(2,1)} %get-tuple-element.122.refs_2_, ...), custom_call_target="tpu_custom_call" | custom-call | tf_op jit(solution)/shard_map/pallas_call | solution.py:251
  49.8 3.3 %collective-permute-start.9 = (bf16[2,3,256,128]{3,2,1,0:T(8,128)(2,1)}, bf16[2,3,256,128]{3,2,1,0:T(8,128)(2,1)}, u32[]{:S(2)}, u32[]{:S(2)}) collective-permute-start(bf16[2,3,256,128]{3,2,1,0:T(8,128)(2,1)} %collective-permute-done.7.refs_3_.refs_6_), channel_id=1, source_target_pairs={{0,2},{1,3},{2,4},{3,5},{4,6},{5,7},{8,10},{9,11},{10,12},{11,13},... | collective-permute-start | bytes 1179656 | tf_op jit(solution)/shard_map/ppermute | solution.py:40
  54.1 1.9 broadcast_select_fusion.4
  56.0 3.3 %collective-permute-start.6 = (bf16[576,256]{1,0:T(8,128)(2,1)}, bf16[576,256]{1,0:T(8,128)(2,1)}, u32[]{:S(2)}, u32[]{:S(2)}) collective-permute-start(bf16[576,256]{1,0:T(8,128)(2,1)} %get-tuple-element.219), channel_id=1, source_target_pairs={{0,6},{1,14},{2,8},{3,0},{4,4},{5,12},{6,10},{7,2},{8,7},{9,15},{1... | collective-permute-start | bytes 884744 | tf_op jit(solution)/shard_map/ppermute | solution.py:40
  59.4 3.1 %shard_map.206 = (f32[2,3,1,768]{3,2,1,0:T(1,128)}, f32[2,3,1,768]{3,2,1,0:T(1,128)}, f32[2,3,64,768]{3,2,1,0:T(8,128)}) custom-call(s32[8]{0:T(128)} %get-tuple-element.182.refs_0_, s32[2,1,256]{2,1,0:T(1,128)} %get-tuple-element.121.refs_1_, ...), custom_call_target="tpu_custom_call", output_to_operand_aliasing={{0}: (5, {}), {1}: (6, {}), {2}: (7, {})} | custom-call | tf_op jit(solution)/shard_map/pallas_call | solution.py:251
  62.6 5.5 %collective-permute-done.6.refs_4_ = bf16[576,256]{1,0:T(8,128)(2,1)} collective-permute-done((bf16[576,256]{1,0:T(8,128)(2,1)}, bf16[576,256]{1,0:T(8,128)(2,1)}, u32[]{:S(2)}, u32[]{:S(2)}) %collective-permute-start.6) | collective-permute-done | bytes 294944 | tf_op jit(solution)/shard_map/ppermute | solution.py:40
  68.6 3.7 %collective-permute-start.5 = (bf16[576,256]{1,0:T(8,128)(2,1)}, bf16[576,256]{1,0:T(8,128)(2,1)}, u32[]{:S(2)}, u32[]{:S(2)}) collective-permute-start(bf16[576,256]{1,0:T(8,128)(2,1)} %get-tuple-element.220), channel_id=1, source_target_pairs={{0,0},{1,8},{2,14},{3,6},{4,2},{5,10},{6,12},{7,4},{8,1},{9,9},{10... | collective-permute-start | bytes 884744 | tf_op jit(solution)/shard_map/ppermute | solution.py:40
  72.3 3.1 %shard_map.207 = (bf16[2,3,64,768]{3,2,1,0:T(8,128)(2,1)}, f32[2,3,1,768]{3,2,1,0:T(1,128)}) custom-call(s32[8]{0:T(128)} %get-tuple-element.182.refs_0_, s32[2,1,256]{2,1,0:T(1,128)} %get-tuple-element.121.refs_1_, bf16[2,3,64,768]{3,2,1,0:T(8,128)(2,1)} %get-tuple-element.122.refs_2_, bf16[2,3,256,128]{3,2,1,0:T(8,128)(2,1)} %collective-permute-done.9.refs_3_.refs_6_, ...), custom_call_target="tpu_custom_call" | custom-call | tf_op jit(solution)/shard_map/pallas_call | solution.py:251
  75.5 18.6 %shard_map.208 = (bf16[576,256]{1,0:T(8,128)(2,1)}, bf16[576,256]{1,0:T(8,128)(2,1)}, f32[576,512]{1,0:T(8,128)}, bf16[2,3,64,768]{3,2,1,0:T(8,128)(2,1)}, f32[2...) custom-call(s32[7]{0:T(128)} %stack.47.refs_0_, ...), custom_call_target="tpu_custom_call" | custom-call | flops 21849999360 | tf_op jit(solution)/shard_map/pallas_call | solution.py:595
  94.1 1.6 collective-permute-start.18
  95.6 3.4 %shard_map.210 = (f32[2,3,64,768]{3,2,1,0:T(8,128)}, bf16[2,3,256,128]{3,2,1,0:T(8,128)(2,1)}, bf16[3,256,128]{2,1,0:T(8,128)(2,1)}, bf16[3,256,128]{2,1,0:T(8,128)(2,1)}) custom-call(s32[8]{0:T(128)} %get-tuple-element.182.refs_0_, s32[2,1,256]{2,1,0:T(1,128)} %get-tuple-element.121.refs_1_, bf16[2,3,64,768]{3,2,1,0:T(8,128)(2,1)} %get-tuple-element.122.refs_2_, ...), custom_call_target="tpu_custom_call" | custom-call | flops 4600000000 | tf_op jit(solution)/shard_map/pallas_call | solution.py:277
  99.5 1.9 collective-permute-done.19.twin_a
  101.7 2.0 shard_map.211
  103.7 3.7 %collective-permute-start.24 = (bf16[576,256]{1,0:T(8,128)(2,1)}, bf16[576,256]{1,0:T(8,128)(2,1)}, u32[]{:S(2)}, u32[]{:S(2)}) collective-permute-start(bf16[576,256]{1,0:T(8,128)(2,1)} %get-tuple-element.162), channel_id=1, source_target_pairs={{0,0},{8,1},{14,2},{6,3},{2,4},{10,5},{12,6},{4,7},{1,8},{9,9},{15... | collective-permute-start | bytes 884744 | tf_op jit(solution)/shard_map/ppermute | solution.py:40
  107.5 11.1 %collective-permute-start.25 = (bf16[576,256]{1,0:T(8,128)(2,1)}, bf16[576,256]{1,0:T(8,128)(2,1)}, u32[]{:S(2)}, u32[]{:S(2)}) collective-permute-start(bf16[576,256]{1,0:T(8,128)(2,1)} %get-tuple-element.163), channel_id=1, source_target_pairs={{6,0},{14,1},{8,2},{0,3},{4,4},{12,5},{10,6},{2,7},{7,8},{15,9},{9... | collective-permute-start | bytes 884744 | tf_op jit(solution)/shard_map/ppermute | solution.py:40
  118.6 3.1 %shard_map.209 = (bf16[2,1504,128]{2,1,0:T(8,128)(2,1)}, bf16[2,1504,128]{2,1,0:T(8,128)(2,1)}) custom-call(s32[1]{0:T(128)} %bitcast.13.x, bf16[2,6016,128]{2,1,0:T(8,128)(2,1)} %get-tuple-element.142.refs_0_.refs_1_.refs_2_.refs_3_, bf16[2,6016,128]{2,1,0:T(8,128)(2,1)} %get-tuple-element.142.refs_0_.refs_1_.refs_2_.refs_3_, ...), custom_call_target="tpu_custom_call" | custom-call | tf_op jit(solution)/shard_map/pallas_call | solution.py:882
  121.7 1.3 collective-permute-start.23
  123.6 3.6 %shard_map.212 = (f32[2,3,64,768]{3,2,1,0:T(8,128)}, bf16[2,3,256,128]{3,2,1,0:T(8,128)(2,1)}, bf16[3,256,128]{2,1,0:T(8,128)(2,1)}, bf16[3,256,128]{2,1,0:T(8,128)(2,1)}) custom-call(s32[8]{0:T(128)} %get-tuple-element.182.refs_0_, s32[2,1,256]{2,1,0:T(1,128)} %get-tuple-element.121.refs_1_, ...), custom_call_target="tpu_custom_call", output_to_operand_aliasing={{0}: (8, {})} | custom-call | flops 16099999744 | tf_op jit(solution)/shard_map/pallas_call | solution.py:277
  127.6 5.4 %collective-permute-done.25 = bf16[576,256]{1,0:T(8,128)(2,1)} collective-permute-done((bf16[576,256]{1,0:T(8,128)(2,1)}, bf16[576,256]{1,0:T(8,128)(2,1)}, u32[]{:S(2)}, u32[]{:S(2)}) %collective-permute-start.25) | collective-permute-done | bytes 294944 | tf_op jit(solution)/shard_map/ppermute | solution.py:40
  133.0 1.8 collective-permute-done.22.twin_b
  134.8 5.6 %collective-permute-done.23.refs_0_ = bf16[2,3,256,128]{3,2,1,0:T(8,128)(2,1)} collective-permute-done((bf16[2,3,256,128]{3,2,1,0:T(8,128)(2,1)}, bf16[2,3,256,128]{3,2,1,0:T(8,128)(2,1)}, u32[]{:S(2)}, u32[]{:S(2)}) %collective-permute-start.23) | collective-permute-done | bytes 393248 | tf_op jit(solution)/shard_map/ppermute | solution.py:40
  140.4 2.2 shard_map.215
  142.6 2.8 %collective-permute-done.27.refs_10_.refs_11_ = bf16[2,1504,128]{2,1,0:T(8,128)(2,1)} collective-permute-done((bf16[2,1504,128]{2,1,0:T(8,128)(2,1)}, bf16[2,1504,128]{2,1,0:T(8,128)(2,1)}, u32[]{:S(2)}, u32[]{:S(2)}) %collective-permute-start.27) | collective-permute-done | bytes 770080 | tf_op jit(solution)/shard_map/ppermute | solution.py:40
  145.4 3.6 %shard_map.213 = (bf16[1504,128]{1,0:T(8,128)(2,1)}, bf16[1504,128]{1,0:T(8,128)(2,1)}, bf16[1504,128]{1,0:T(8,128)(2,1)}, bf16[1504,128]{1,0:T(8,128)(2,1)}) custom-call(s32[1]{0:T(128)} %bitcast.13.x, bf16[2,6016,128]{2,1,0:T(8,128)(2,1)} %get-tuple-element.142.refs_0_.refs_1_.refs_2_.refs_3_, ...), custom_call_target="tpu_custom_call" | custom-call | tf_op jit(solution)/shard_map/pallas_call | solution.py:918
  149.0 0.9 collective-permute-start.28
  149.9 1.3 collective-permute-start.29
  151.2 1.3 collective-permute-start.32
  152.5 11.5 %shard_map.216 = (f32[2,3,64,768]{3,2,1,0:T(8,128)}, f32[2,3,256,128]{3,2,1,0:T(8,128)}, bf16[3,256,128]{2,1,0:T(8,128)(2,1)}, bf16[3,256,128]{2,1,0:T(8,128)(2,1)}) custom-call(s32[8]{0:T(128)} %get-tuple-element.182.refs_0_, s32[2,1,256]{2,1,0:T(1,128)} %get-tuple-element.121.refs_1_, ...), custom_call_target="tpu_custom_call", output_to_operand_aliasing={{0}: (8, {})} | custom-call | flops 13799999488 | tf_op jit(solution)/shard_map/pallas_call | solution.py:277
  164.5 2.4 shard_map.214
  166.9 6.9 %all-to-all-start = ((bf16[4,752,128]{2,1,0:T(8,128)(2,1)}), bf16[4,752,128]{2,1,0:T(8,128)(2,1)}, u32[]{:S(2)}, u32[]{:S(2)}) async-start(bf16[4,752,128]{2,1,0:T(8,128)(2,1)} %bitcast.33), calls=%async_computation | async-start | bytes 1540096 | tf_op jit(solution)/shard_map/all_to_all | solution.py:839
  173.8 6.9 %shard_map.217 = (bf16[576,256]{1,0:T(8,128)(2,1)}, bf16[576,256]{1,0:T(8,128)(2,1)}, bf16[2,1152,128]{2,1,0:T(8,128)(2,1)}, bf16[2,1152,128]{2,1,0:T(8,128)(2,1)}) custom-call(s32[7]{0:T(128)} %stack.47.refs_0_, bf16[592,256]{1,0:T(8,128)(2,1)} %copy-done, bf16[592,256]{1,0:T(8,128)(2,1)} %copy-done.1, f32[32,512]{1,0:T(8,128)} %get-tuple-element.222.refs_3_, ...), custom_call_target="tpu_custom_call" | custom-call | flops 8049999872 | tf_op jit(solution)/shard_map/pallas_call | solution.py:688
  180.7 2.3 collective-permute-done.33.got
  183.1 10.8 %all-to-all-done.got = bf16[4,752,128]{2,1,0:T(8,128)(2,1)} async-done(((bf16[4,752,128]{2,1,0:T(8,128)(2,1)}), bf16[4,752,128]{2,1,0:T(8,128)(2,1)}, u32[]{:S(2)}, u32[]{:S(2)}) %all-to-all-start) | async-done | bytes 770080 | tf_op jit(solution)/shard_map/all_to_all | solution.py:839
  193.8 1.8 shard_map.219
  196.3 1.9 shard_map.218.refs_0_
  198.2 1.5 collective-permute-start.36
  200.2 3.7 %collective-permute-done.39.refs_0_ = bf16[1152,128]{1,0:T(8,128)(2,1)} collective-permute-done((bf16[1152,128]{1,0:T(8,128)(2,1)}, bf16[1152,128]{1,0:T(8,128)(2,1)}, u32[]{:S(2)}, u32[]{:S(2)}) %collective-permute-start.39) | collective-permute-done | bytes 294944 | tf_op jit(solution)/shard_map/ppermute | solution.py:40
  204.0 2.0 shard_map.220
  205.9 4.1 %all-to-all-start.1 = ((bf16[8,144,128]{2,1,0:T(8,128)(2,1)}), bf16[8,144,128]{2,1,0:T(8,128)(2,1)}, u32[]{:S(2)}, u32[]{:S(2)}) async-start(bf16[8,144,128]{2,1,0:T(8,128)(2,1)} %bitcast.34), calls=%async_computation.1 | async-start | bytes 589824 | tf_op jit(solution)/shard_map/all_to_all | solution.py:839
  210.6 1.9 collective-permute-start.40
  212.6 6.2 %collective-permute-done.35.refs_2_ = bf16[752,128]{1,0:T(8,128)(2,1)} collective-permute-done((bf16[752,128]{1,0:T(8,128)(2,1)}, bf16[752,128]{1,0:T(8,128)(2,1)}, u32[]{:S(2)}, u32[]{:S(2)}) %collective-permute-start.35) | collective-permute-done | bytes 192544 | tf_op jit(solution)/shard_map/ppermute | solution.py:40
  218.8 2.0 collective-permute-start.41
  220.9 1.1 broadcast_select_fusion.3
  222.0 0.9 maximum_bitcast_fusion
  222.8 3.7 %collective-permute-start.37 = (bf16[576,256]{1,0:T(8,128)(2,1)}, bf16[576,256]{1,0:T(8,128)(2,1)}, u32[]{:S(2)}, u32[]{:S(2)}) collective-permute-start(bf16[576,256]{1,0:T(8,128)(2,1)} %get-tuple-element.198), channel_id=1, source_target_pairs={{0,0},{8,1},{14,2},{6,3},{2,4},{10,5},{12,6},{4,7},{1,8},{9,9},{15... | collective-permute-start | bytes 884744 | tf_op jit(solution)/shard_map/ppermute | solution.py:40
  226.6 1.7 shard_map.221
  228.3 4.1 %all-to-all-start.2 = ((bf16[8,144,128]{2,1,0:T(8,128)(2,1)}), bf16[8,144,128]{2,1,0:T(8,128)(2,1)}, u32[]{:S(2)}, u32[]{:S(2)}) async-start(bf16[8,144,128]{2,1,0:T(8,128)(2,1)} %shard_map.221), calls=%async_computation.2 | async-start | bytes 589824 | tf_op jit(solution)/shard_map/all_to_all | solution.py:847
  232.4 4.7 %collective-permute-start.38 = (bf16[576,256]{1,0:T(8,128)(2,1)}, bf16[576,256]{1,0:T(8,128)(2,1)}, u32[]{:S(2)}, u32[]{:S(2)}) collective-permute-start(bf16[576,256]{1,0:T(8,128)(2,1)} %get-tuple-element.199), channel_id=1, source_target_pairs={{6,0},{14,1},{8,2},{0,3},{4,4},{12,5},{10,6},{2,7},{7,8},{15,9},{9... | collective-permute-start | bytes 884744 | tf_op jit(solution)/shard_map/ppermute | solution.py:40
  237.1 3.3 %shard_map.223 = (f32[144,1536]{1,0:T(8,128)}, f32[144,1536]{1,0:T(8,128)}, f32[144,576]{1,0:T(8,128)}, f32[576,384]{1,0:T(8,128)}) custom-call(s32[2]{0:T(128)} %pad_add_fusion.1.sc, bf16[752,128]{1,0:T(8,128)(2,1)} %shard_map.218.refs_0_, bf16[752,128]{1,0:T(8,128)(2,1)} %collective-permute-done.34.refs_1_, ...), custom_call_target="tpu_custom_call" | custom-call | flops 3449999872 | tf_op jit(solution)/shard_map/pallas_call | solution.py:770
  240.4 5.8 %collective-permute-done.38 = bf16[576,256]{1,0:T(8,128)(2,1)} collective-permute-done((bf16[576,256]{1,0:T(8,128)(2,1)}, bf16[576,256]{1,0:T(8,128)(2,1)}, u32[]{:S(2)}, u32[]{:S(2)}) %collective-permute-start.38) | collective-permute-done | bytes 294944 | tf_op jit(solution)/shard_map/ppermute | solution.py:40
  246.2 1.1 broadcast_select_fusion.1
  247.3 0.9 maximum_bitcast_fusion.1
  248.2 1.9 shard_map.222
  (78 shorter events, 12.2 us)
Async XLA Ops:
  5.5 11.0 %collective-permute-start = (bf16[144,1024]{1,0:T(8,128)(2,1)}, bf16[144,1024]{1,0:T(8,128)(2,1)S(1)}, u32[]{:S(2)}, u32[]{:S(2)}) collective-permute-start(bf16[144,1024]{1,0:T(8,128)(2,1)} %get-tuple-element.113.refs_5_.refs_14_), channel_id=1, source_target_pairs={{0,16},{1,17},{2,18},{3,19},{4,20},{5,21},{6,22},{7,23},{8,24},{9,... | collective-permute-start | bytes 884744 | tf_op jit(solution)/shard_map/ppermute | solution.py:40
  8.5 18.3 %collective-permute-start.4 = (bf16[144,1024]{1,0:T(8,128)(2,1)}, bf16[144,1024]{1,0:T(8,128)(2,1)}, u32[]{:S(2)}, u32[]{:S(2)}) collective-permute-start(bf16[144,1024]{1,0:T(8,128)(2,1)} %get-tuple-element.113.refs_5_.refs_14_), channel_id=1, source_target_pairs={{0,8},{1,9},{2,10},{3,11},{4,12},{5,13},{6,14},{7,15},{8,0},{9,1},... | collective-permute-start | bytes 884744 | tf_op jit(solution)/shard_map/ppermute | solution.py:40
  8.5 13.8 %collective-permute-start.2 = (bf16[592,256]{1,0:T(8,128)(2,1)}, bf16[592,256]{1,0:T(8,128)(2,1)S(1)}, u32[]{:S(2)}, u32[]{:S(2)}) collective-permute-start(bf16[592,256]{1,0:T(8,128)(2,1)} %get-tuple-element.115), channel_id=1, source_target_pairs={{0,0},{1,8},{2,14},{3,6},{4,2},{5,10},{6,12},{7,4},{8,1},{9,9},{10... | collective-permute-start | bytes 909320 | tf_op jit(solution)/shard_map/ppermute | solution.py:40
  10.1 15.0 %collective-permute-start.3 = (bf16[592,256]{1,0:T(8,128)(2,1)}, bf16[592,256]{1,0:T(8,128)(2,1)S(1)}, u32[]{:S(2)}, u32[]{:S(2)}) collective-permute-start(bf16[592,256]{1,0:T(8,128)(2,1)} %get-tuple-element.116), channel_id=1, source_target_pairs={{0,6},{1,14},{2,8},{3,0},{4,4},{5,12},{6,10},{7,2},{8,7},{9,15},{1... | collective-permute-start | bytes 909320 | tf_op jit(solution)/shard_map/ppermute | solution.py:40
  16.5 0.7 copy-start.2
  17.2 3.2 %collective-permute-start.1 = (bf16[144,1024]{1,0:T(8,128)(2,1)S(1)}, bf16[144,1024]{1,0:T(8,128)(2,1)S(1)}, u32[]{:S(2)}, u32[]{:S(2)}) collective-permute-start(bf16[144,1024]{1,0:T(8,128)(2,1)S(1)} %collective-permute-done.refs_6_.refs_15_), channel_id=1, source_target_pairs={{0,8},{1,9},{2,10},{3,11},{4,12},{5,13},{6,14},{7,15},{8,0},{9,1},... | collective-permute-start | bytes 884744 | tf_op jit(solution)/shard_map/ppermute | solution.py:40
  20.4 0.7 copy-start.3
  21.1 32.2 %collective-permute-start.12 = (bf16[144,3648]{1,0:T(8,128)(2,1)}, bf16[144,3648]{1,0:T(8,128)(2,1)}, u32[]{:S(2)}, u32[]{:S(2)}) collective-permute-start(bf16[144,3648]{1,0:T(8,128)(2,1)} %pad_maximum_fusion.refs_7_), channel_id=1, source_target_pairs={{0,16},{1,17},{2,18},{3,19},{4,20},{5,21},{6,22},{7,23},{8,24},{9,... | collective-permute-start | bytes 3151880 | tf_op jit(solution)/shard_map/ppermute | solution.py:40
  22.3 0.7 copy-start
  25.1 0.7 copy-start.1
  31.7 7.7 %collective-permute-start.8 = (bf16[2,3,256,128]{3,2,1,0:T(8,128)(2,1)}, bf16[2,3,256,128]{3,2,1,0:T(8,128)(2,1)}, u32[]{:S(2)}, u32[]{:S(2)}) collective-permute-start(bf16[2,3,256,128]{3,2,1,0:T(8,128)(2,1)} %get-tuple-element.123.refs_3_.refs_6_), channel_id=1, source_target_pairs={{0,8},{1,9},{2,10},{3,11},{4,12},{5,13},{6,14},{7,15},{8,0},{9,1},... | collective-permute-start | bytes 1179656 | tf_op jit(solution)/shard_map/ppermute | solution.py:40
  31.7 17.9 %collective-permute-start.7 = (bf16[2,3,256,128]{3,2,1,0:T(8,128)(2,1)}, bf16[2,3,256,128]{3,2,1,0:T(8,128)(2,1)}, u32[]{:S(2)}, u32[]{:S(2)}) collective-permute-start(bf16[2,3,256,128]{3,2,1,0:T(8,128)(2,1)} %get-tuple-element.123.refs_3_.refs_6_), channel_id=1, source_target_pairs={{0,2},{1,3},{2,4},{3,5},{4,6},{5,7},{8,10},{9,11},{10,12},{11,13},... | collective-permute-start | bytes 1179656 | tf_op jit(solution)/shard_map/ppermute | solution.py:40
  49.6 6.4 %collective-permute-start.10 = (bf16[2,3,256,128]{3,2,1,0:T(8,128)(2,1)}, bf16[2,3,256,128]{3,2,1,0:T(8,128)(2,1)}, u32[]{:S(2)}, u32[]{:S(2)}) collective-permute-start(bf16[2,3,256,128]{3,2,1,0:T(8,128)(2,1)} %collective-permute-done.7.refs_3_.refs_6_), channel_id=1, source_target_pairs={{0,8},{1,9},{2,10},{3,11},{4,12},{5,13},{6,14},{7,15},{8,0},{9,1},... | collective-permute-start | bytes 1179656 | tf_op jit(solution)/shard_map/ppermute | solution.py:40
  49.8 12.7 %collective-permute-start.9 = (bf16[2,3,256,128]{3,2,1,0:T(8,128)(2,1)}, bf16[2,3,256,128]{3,2,1,0:T(8,128)(2,1)}, u32[]{:S(2)}, u32[]{:S(2)}) collective-permute-start(bf16[2,3,256,128]{3,2,1,0:T(8,128)(2,1)} %collective-permute-done.7.refs_3_.refs_6_), channel_id=1, source_target_pairs={{0,2},{1,3},{2,4},{3,5},{4,6},{5,7},{8,10},{9,11},{10,12},{11,13},... | collective-permute-start | bytes 1179656 | tf_op jit(solution)/shard_map/ppermute | solution.py:40
  53.1 22.3 %collective-permute-start.13 = (bf16[144,3648]{1,0:T(8,128)(2,1)}, bf16[144,3648]{1,0:T(8,128)(2,1)}, u32[]{:S(2)}, u32[]{:S(2)}) collective-permute-start(bf16[144,3648]{1,0:T(8,128)(2,1)} %pad_maximum_fusion.refs_7_), channel_id=1, source_target_pairs={{0,8},{1,9},{2,10},{3,11},{4,12},{5,13},{6,14},{7,15},{8,0},{9,1},... | collective-permute-start | bytes 3151880 | tf_op jit(solution)/shard_map/ppermute | solution.py:40
  53.3 22.1 %collective-permute-start.14 = (bf16[144,3648]{1,0:T(8,128)(2,1)}, bf16[144,3648]{1,0:T(8,128)(2,1)}, u32[]{:S(2)}, u32[]{:S(2)}) collective-permute-start(bf16[144,3648]{1,0:T(8,128)(2,1)} %collective-permute-done.12.refs_8_), channel_id=1, source_target_pairs={{0,8},{1,9},{2,10},{3,11},{4,12},{5,13},{6,14},{7,15},{8,0},{9,1},... | collective-permute-start | bytes 3151880 | tf_op jit(solution)/shard_map/ppermute | solution.py:40
  53.6 14.5 %collective-permute-start.15 = (bf16[576,384]{1,0:T(8,128)(2,1)}, bf16[576,384]{1,0:T(8,128)(2,1)}, u32[]{:S(2)}, u32[]{:S(2)}) collective-permute-start(bf16[576,384]{1,0:T(8,128)(2,1)} %bitcast.38), channel_id=1, source_target_pairs={{0,16},{1,17},{2,18},{3,19},{4,20},{5,21},{6,22},{7,23},{8,24},{9,... | collective-permute-start | bytes 1327112 | tf_op jit(solution)/shard_map/ppermute | solution.py:40
  56.0 12.0 %collective-permute-start.6 = (bf16[576,256]{1,0:T(8,128)(2,1)}, bf16[576,256]{1,0:T(8,128)(2,1)}, u32[]{:S(2)}, u32[]{:S(2)}) collective-permute-start(bf16[576,256]{1,0:T(8,128)(2,1)} %get-tuple-element.219), channel_id=1, source_target_pairs={{0,6},{1,14},{2,8},{3,0},{4,4},{5,12},{6,10},{7,2},{8,7},{9,15},{1... | collective-permute-start | bytes 884744 | tf_op jit(solution)/shard_map/ppermute | solution.py:40
  62.5 6.1 %collective-permute-start.11 = (bf16[2,3,256,128]{3,2,1,0:T(8,128)(2,1)}, bf16[2,3,256,128]{3,2,1,0:T(8,128)(2,1)}, u32[]{:S(2)}, u32[]{:S(2)}) collective-permute-start(bf16[2,3,256,128]{3,2,1,0:T(8,128)(2,1)} %collective-permute-done.9.refs_3_.refs_6_), channel_id=1, source_target_pairs={{0,8},{1,9},{2,10},{3,11},{4,12},{5,13},{6,14},{7,15},{8,0},{9,1},... | collective-permute-start | bytes 1179656 | tf_op jit(solution)/shard_map/ppermute | solution.py:40
  68.1 7.4 %collective-permute-start.16 = (bf16[576,384]{1,0:T(8,128)(2,1)}, bf16[576,384]{1,0:T(8,128)(2,1)}, u32[]{:S(2)}, u32[]{:S(2)}) collective-permute-start(bf16[576,384]{1,0:T(8,128)(2,1)} %bitcast.39), channel_id=1, source_target_pairs={{0,8},{1,9},{2,10},{3,11},{4,12},{5,13},{6,14},{7,15},{8,0},{9,1},... | collective-permute-start | bytes 1327112 | tf_op jit(solution)/shard_map/ppermute | solution.py:40
  68.1 7.4 %collective-permute-start.17 = (bf16[576,384]{1,0:T(8,128)(2,1)}, bf16[576,384]{1,0:T(8,128)(2,1)}, u32[]{:S(2)}, u32[]{:S(2)}) collective-permute-start(bf16[576,384]{1,0:T(8,128)(2,1)} %collective-permute-done.15.refs_12_), channel_id=1, source_target_pairs={{0,8},{1,9},{2,10},{3,11},{4,12},{5,13},{6,14},{7,15},{8,0},{9,1},... | collective-permute-start | bytes 1327112 | tf_op jit(solution)/shard_map/ppermute | solution.py:40
  68.6 6.8 %collective-permute-start.5 = (bf16[576,256]{1,0:T(8,128)(2,1)}, bf16[576,256]{1,0:T(8,128)(2,1)}, u32[]{:S(2)}, u32[]{:S(2)}) collective-permute-start(bf16[576,256]{1,0:T(8,128)(2,1)} %get-tuple-element.220), channel_id=1, source_target_pairs={{0,0},{1,8},{2,14},{3,6},{4,2},{5,10},{6,12},{7,4},{8,1},{9,9},{10... | collective-permute-start | bytes 884744 | tf_op jit(solution)/shard_map/ppermute | solution.py:40
  94.1 24.5 %collective-permute-start.18 = (bf16[2,6016,128]{2,1,0:T(8,128)(2,1)}, bf16[2,6016,128]{2,1,0:T(8,128)(2,1)}, u32[]{:S(2)}, u32[]{:S(2)}) collective-permute-start(bf16[2,6016,128]{2,1,0:T(8,128)(2,1)} %get-tuple-element.143), channel_id=1, source_target_pairs={{0,8},{1,9},{2,10},{3,11},{4,12},{5,13},{6,14},{7,15},{8,0},{9,1},... | collective-permute-start | bytes 9240584 | tf_op jit(solution)/shard_map/ppermute | solution.py:40
  99.0 2.4 collective-permute-start.19
  99.0 2.7 %collective-permute-start.20 = (bf16[3,256,128]{2,1,0:T(8,128)(2,1)}, bf16[3,256,128]{2,1,0:T(8,128)(2,1)}, u32[]{:S(2)}, u32[]{:S(2)}) collective-permute-start(bf16[3,256,128]{2,1,0:T(8,128)(2,1)} %get-tuple-element.152), channel_id=1, source_target_pairs={{0,8},{1,9},{2,10},{3,11},{4,12},{5,13},{6,14},{7,15},{8,0},{9,1},... | collective-permute-start | bytes 589832 | tf_op jit(solution)/shard_map/ppermute | solution.py:40
  103.7 23.5 %collective-permute-start.24 = (bf16[576,256]{1,0:T(8,128)(2,1)}, bf16[576,256]{1,0:T(8,128)(2,1)}, u32[]{:S(2)}, u32[]{:S(2)}) collective-permute-start(bf16[576,256]{1,0:T(8,128)(2,1)} %get-tuple-element.162), channel_id=1, source_target_pairs={{0,0},{8,1},{14,2},{6,3},{2,4},{10,5},{12,6},{4,7},{1,8},{9,9},{15... | collective-permute-start | bytes 884744 | tf_op jit(solution)/shard_map/ppermute | solution.py:40
  107.5 25.5 %collective-permute-start.25 = (bf16[576,256]{1,0:T(8,128)(2,1)}, bf16[576,256]{1,0:T(8,128)(2,1)}, u32[]{:S(2)}, u32[]{:S(2)}) collective-permute-start(bf16[576,256]{1,0:T(8,128)(2,1)} %get-tuple-element.163), channel_id=1, source_target_pairs={{6,0},{14,1},{8,2},{0,3},{4,4},{12,5},{10,6},{2,7},{7,8},{15,9},{9... | collective-permute-start | bytes 884744 | tf_op jit(solution)/shard_map/ppermute | solution.py:40
  121.7 18.7 %collective-permute-start.23 = (bf16[2,3,256,128]{3,2,1,0:T(8,128)(2,1)}, bf16[2,3,256,128]{3,2,1,0:T(8,128)(2,1)}, u32[]{:S(2)}, u32[]{:S(2)}) collective-permute-start(bf16[2,3,256,128]{3,2,1,0:T(8,128)(2,1)} %shard_map.211), channel_id=1, source_target_pairs={{2,0},{3,1},{4,2},{5,3},{6,4},{7,5},{10,8},{11,9},{12,10},{13,11},... | collective-permute-start | bytes 1179656 | tf_op jit(solution)/shard_map/ppermute | solution.py:40
  123.0 19.6 %collective-permute-start.26 = (bf16[2,1504,128]{2,1,0:T(8,128)(2,1)}, bf16[2,1504,128]{2,1,0:T(8,128)(2,1)}, u32[]{:S(2)}, u32[]{:S(2)}) collective-permute-start(bf16[2,1504,128]{2,1,0:T(8,128)(2,1)} %get-tuple-element.166), channel_id=1, source_target_pairs={{0,16},{1,17},{2,18},{3,19},{4,20},{5,21},{6,22},{7,23},{8,24},{9,... | collective-permute-start | bytes 2310152 | tf_op jit(solution)/shard_map/ppermute | solution.py:40
  123.6 21.8 %collective-permute-start.27 = (bf16[2,1504,128]{2,1,0:T(8,128)(2,1)}, bf16[2,1504,128]{2,1,0:T(8,128)(2,1)}, u32[]{:S(2)}, u32[]{:S(2)}) collective-permute-start(bf16[2,1504,128]{2,1,0:T(8,128)(2,1)} %get-tuple-element.167), channel_id=1, source_target_pairs={{0,1},{1,0},{2,3},{3,2},{4,5},{5,4},{6,7},{7,6},{8,9},{9,8},{10,11... | collective-permute-start | bytes 2310152 | tf_op jit(solution)/shard_map/ppermute | solution.py:40
  127.2 5.8 %collective-permute-start.21 = (bf16[3,256,128]{2,1,0:T(8,128)(2,1)}, bf16[3,256,128]{2,1,0:T(8,128)(2,1)}, u32[]{:S(2)}, u32[]{:S(2)}) collective-permute-start(bf16[3,256,128]{2,1,0:T(8,128)(2,1)} %get-tuple-element.158), channel_id=1, source_target_pairs={{0,8},{1,9},{2,10},{3,11},{4,12},{5,13},{6,14},{7,15},{8,0},{9,1},... | collective-permute-start | bytes 589832 | tf_op jit(solution)/shard_map/ppermute | solution.py:40
  133.0 1.8 collective-permute-start.22
  149.0 15.5 %collective-permute-start.28 = (bf16[1504,128]{1,0:T(8,128)(2,1)}, bf16[1504,128]{1,0:T(8,128)(2,1)}, u32[]{:S(2)}, u32[]{:S(2)}) collective-permute-start(bf16[1504,128]{1,0:T(8,128)(2,1)} %get-tuple-element.174), channel_id=1, source_target_pairs={{0,1},{1,0},{2,3},{3,2},{4,5},{5,4},{6,7},{7,6},{8,9},{9,8},{10,11... | collective-permute-start | bytes 1155080 | tf_op jit(solution)/shard_map/ppermute | solution.py:40
  149.9 14.6 %collective-permute-start.29 = (bf16[1504,128]{1,0:T(8,128)(2,1)}, bf16[1504,128]{1,0:T(8,128)(2,1)}, u32[]{:S(2)}, u32[]{:S(2)}) collective-permute-start(bf16[1504,128]{1,0:T(8,128)(2,1)} %get-tuple-element.176), channel_id=1, source_target_pairs={{0,16},{1,17},{2,18},{3,19},{4,20},{5,21},{6,22},{7,23},{8,24},{9,... | collective-permute-start | bytes 1155080 | tf_op jit(solution)/shard_map/ppermute | solution.py:40
  151.2 22.5 %collective-permute-start.32 = (bf16[2,3,256,128]{3,2,1,0:T(8,128)(2,1)}, bf16[2,3,256,128]{3,2,1,0:T(8,128)(2,1)}, u32[]{:S(2)}, u32[]{:S(2)}) collective-permute-start(bf16[2,3,256,128]{3,2,1,0:T(8,128)(2,1)} %shard_map.215), channel_id=1, source_target_pairs={{2,0},{3,1},{4,2},{5,3},{6,4},{7,5},{10,8},{11,9},{12,10},{13,11},... | collective-permute-start | bytes 1179656 | tf_op jit(solution)/shard_map/ppermute | solution.py:40
  164.0 9.8 %collective-permute-start.30 = (bf16[3,256,128]{2,1,0:T(8,128)(2,1)}, bf16[3,256,128]{2,1,0:T(8,128)(2,1)}, u32[]{:S(2)}, u32[]{:S(2)}) collective-permute-start(bf16[3,256,128]{2,1,0:T(8,128)(2,1)} %get-tuple-element.191), channel_id=1, source_target_pairs={{0,8},{1,9},{2,10},{3,11},{4,12},{5,13},{6,14},{7,15},{8,0},{9,1},... | collective-permute-start | bytes 589832 | tf_op jit(solution)/shard_map/ppermute | solution.py:40
  164.0 9.8 %collective-permute-start.31 = (bf16[3,256,128]{2,1,0:T(8,128)(2,1)}, bf16[3,256,128]{2,1,0:T(8,128)(2,1)}, u32[]{:S(2)}, u32[]{:S(2)}) collective-permute-start(bf16[3,256,128]{2,1,0:T(8,128)(2,1)} %get-tuple-element.192), channel_id=1, source_target_pairs={{0,8},{1,9},{2,10},{3,11},{4,12},{5,13},{6,14},{7,15},{8,0},{9,1},... | collective-permute-start | bytes 589832 | tf_op jit(solution)/shard_map/ppermute | solution.py:40
  166.9 26.9 %all-to-all-start = ((bf16[4,752,128]{2,1,0:T(8,128)(2,1)}), bf16[4,752,128]{2,1,0:T(8,128)(2,1)}, u32[]{:S(2)}, u32[]{:S(2)}) async-start(bf16[4,752,128]{2,1,0:T(8,128)(2,1)} %bitcast.33), calls=%async_computation | async-start | bytes 1540096 | tf_op jit(solution)/shard_map/all_to_all | solution.py:839
  180.7 2.4 collective-permute-start.33
  195.7 8.3 %collective-permute-start.39 = (bf16[1152,128]{1,0:T(8,128)(2,1)}, bf16[1152,128]{1,0:T(8,128)(2,1)}, u32[]{:S(2)}, u32[]{:S(2)}) collective-permute-start(bf16[1152,128]{1,0:T(8,128)(2,1)} %shard_map.219), channel_id=1, source_target_pairs={{0,16},{1,17},{2,18},{3,19},{4,20},{5,21},{6,22},{7,23},{8,24},{9,... | collective-permute-start | bytes 884744 | tf_op jit(solution)/shard_map/ppermute | solution.py:40
  198.2 14.3 %collective-permute-start.36 = (bf16[752,128]{1,0:T(8,128)(2,1)}, bf16[752,128]{1,0:T(8,128)(2,1)}, u32[]{:S(2)}, u32[]{:S(2)}) collective-permute-start(bf16[752,128]{1,0:T(8,128)(2,1)} %shard_map.218.refs_0_), channel_id=1, source_target_pairs={{0,6},{1,7},{2,0},{3,1},{4,2},{5,3},{6,4},{7,5},{8,14},{9,15},{10,... | collective-permute-start | bytes 577544 | tf_op jit(solution)/shard_map/ppermute | solution.py:40
  199.7 19.2 %collective-permute-start.35 = (bf16[752,128]{1,0:T(8,128)(2,1)}, bf16[752,128]{1,0:T(8,128)(2,1)}, u32[]{:S(2)}, u32[]{:S(2)}) collective-permute-start(bf16[752,128]{1,0:T(8,128)(2,1)} %shard_map.218.refs_0_), channel_id=1, source_target_pairs={{0,4},{1,5},{2,6},{3,7},{4,0},{5,1},{6,2},{7,3},{8,12},{9,13},{10,... | collective-permute-start | bytes 577544 | tf_op jit(solution)/shard_map/ppermute | solution.py:40
  199.7 19.2 %collective-permute-start.34 = (bf16[752,128]{1,0:T(8,128)(2,1)}, bf16[752,128]{1,0:T(8,128)(2,1)}, u32[]{:S(2)}, u32[]{:S(2)}) collective-permute-start(bf16[752,128]{1,0:T(8,128)(2,1)} %shard_map.218.refs_0_), channel_id=1, source_target_pairs={{0,2},{1,3},{2,4},{3,5},{4,6},{5,7},{6,0},{7,1},{8,10},{9,11},{10,... | collective-permute-start | bytes 577544 | tf_op jit(solution)/shard_map/ppermute | solution.py:40
  205.9 20.6 %all-to-all-start.1 = ((bf16[8,144,128]{2,1,0:T(8,128)(2,1)}), bf16[8,144,128]{2,1,0:T(8,128)(2,1)}, u32[]{:S(2)}, u32[]{:S(2)}) async-start(bf16[8,144,128]{2,1,0:T(8,128)(2,1)} %bitcast.34), calls=%async_computation.1 | async-start | bytes 589824 | tf_op jit(solution)/shard_map/all_to_all | solution.py:839
  210.6 21.8 %collective-permute-start.40 = (bf16[752,128]{1,0:T(8,128)(2,1)}, bf16[752,128]{1,0:T(8,128)(2,1)}, u32[]{:S(2)}, u32[]{:S(2)}) collective-permute-start(bf16[752,128]{1,0:T(8,128)(2,1)} %shard_map.218.refs_0_), channel_id=1, source_target_pairs={{0,1},{1,0},{2,3},{3,2},{4,5},{5,4},{6,7},{7,6},{8,9},{9,8},{10,11... | collective-permute-start | bytes 577544 | tf_op jit(solution)/shard_map/ppermute | solution.py:40
  212.5 24.6 %collective-permute-start.43 = (bf16[752,128]{1,0:T(8,128)(2,1)}, bf16[752,128]{1,0:T(8,128)(2,1)}, u32[]{:S(2)}, u32[]{:S(2)}) collective-permute-start(bf16[752,128]{1,0:T(8,128)(2,1)} %collective-permute-done.36.refs_3_), channel_id=1, source_target_pairs={{0,1},{1,0},{2,3},{3,2},{4,5},{5,4},{6,7},{7,6},{8,9},{9,8},{10,11... | collective-permute-start | bytes 577544 | tf_op jit(solution)/shard_map/ppermute | solution.py:40
  218.8 18.3 %collective-permute-start.42 = (bf16[752,128]{1,0:T(8,128)(2,1)}, bf16[752,128]{1,0:T(8,128)(2,1)}, u32[]{:S(2)}, u32[]{:S(2)}) collective-permute-start(bf16[752,128]{1,0:T(8,128)(2,1)} %collective-permute-done.35.refs_2_), channel_id=1, source_target_pairs={{0,1},{1,0},{2,3},{3,2},{4,5},{5,4},{6,7},{7,6},{8,9},{9,8},{10,11... | collective-permute-start | bytes 577544 | tf_op jit(solution)/shard_map/ppermute | solution.py:40
  218.8 18.3 %collective-permute-start.41 = (bf16[752,128]{1,0:T(8,128)(2,1)}, bf16[752,128]{1,0:T(8,128)(2,1)}, u32[]{:S(2)}, u32[]{:S(2)}) collective-permute-start(bf16[752,128]{1,0:T(8,128)(2,1)} %collective-permute-done.34.refs_1_), channel_id=1, source_target_pairs={{0,1},{1,0},{2,3},{3,2},{4,5},{5,4},{6,7},{7,6},{8,9},{9,8},{10,11... | collective-permute-start | bytes 577544 | tf_op jit(solution)/shard_map/ppermute | solution.py:40
  222.8 17.6 %collective-permute-start.37 = (bf16[576,256]{1,0:T(8,128)(2,1)}, bf16[576,256]{1,0:T(8,128)(2,1)}, u32[]{:S(2)}, u32[]{:S(2)}) collective-permute-start(bf16[576,256]{1,0:T(8,128)(2,1)} %get-tuple-element.198), channel_id=1, source_target_pairs={{0,0},{8,1},{14,2},{6,3},{2,4},{10,5},{12,6},{4,7},{1,8},{9,9},{15... | collective-permute-start | bytes 884744 | tf_op jit(solution)/shard_map/ppermute | solution.py:40
  228.3 19.9 %all-to-all-start.2 = ((bf16[8,144,128]{2,1,0:T(8,128)(2,1)}), bf16[8,144,128]{2,1,0:T(8,128)(2,1)}, u32[]{:S(2)}, u32[]{:S(2)}) async-start(bf16[8,144,128]{2,1,0:T(8,128)(2,1)} %shard_map.221), calls=%async_computation.2 | async-start | bytes 589824 | tf_op jit(solution)/shard_map/all_to_all | solution.py:847
  232.4 13.8 %collective-permute-start.38 = (bf16[576,256]{1,0:T(8,128)(2,1)}, bf16[576,256]{1,0:T(8,128)(2,1)}, u32[]{:S(2)}, u32[]{:S(2)}) collective-permute-start(bf16[576,256]{1,0:T(8,128)(2,1)} %get-tuple-element.199), channel_id=1, source_target_pairs={{6,0},{14,1},{8,2},{0,3},{4,4},{12,5},{10,6},{2,7},{7,8},{15,9},{9... | collective-permute-start | bytes 884744 | tf_op jit(solution)/shard_map/ppermute | solution.py:40
